TPU v7x, 32 devices: a whole 2x2x4 slice. The times are simulated.
32 devices in a mesh: ctx: 4 (over y, x), fsdp: 8 (over z, core).
Axes of the slice: x: 2, y: 2, z: 4, core: 2. Of those that a mesh axis runs over, the one named last changes fastest.
Arguments:
- tokens: bfloat16 [4096, 2048], P(('ctx', 'fsdp')), may hold values from -6 to 6
- per_layer: bfloat16 [4096, 256], P(('ctx', 'fsdp')), may hold values from -6 to 6
- cotangent: bfloat16 [4096, 2048], P(('ctx', 'fsdp')), may hold values from -6 to 6
- doc_lengths: int32 [7], replicated, may hold values from 1 to 4090, as said below
- positions: int32 [4096], P(('ctx', 'fsdp')), may hold values from 0 to 4095, as said below
- w_query: float32 [2048, 2048], P('fsdp'), may hold values from -0.125 to 0.125
- w_key: float32 [2048, 512], P('fsdp'), may hold values from -0.125 to 0.125
- w_value: float32 [2048, 512], P('fsdp'), may hold values from -0.125 to 0.125
- w_out: float32 [2048, 2048], P('fsdp'), may hold values from -0.125 to 0.125
- laurel_left: float32 [2048, 64], P('fsdp'), may hold values from -0.125 to 0.125
- laurel_right: float32 [64, 2048], P('fsdp'), may hold values from -0.75 to 0.75
- w_gate: float32 [2048, 8192], P('fsdp'), may hold values from -0.125 to 0.125
- w_up: float32 [2048, 8192], P('fsdp'), may hold values from -0.125 to 0.125
- w_down: float32 [8192, 2048], P('fsdp'), may hold values from -0.0625 to 0.0625
- ple_gate: float32 [2048, 256], P('fsdp'), may hold values from -0.125 to 0.125
- ple_proj: float32 [256, 2048], P('fsdp'), may hold values from -0.375 to 0.375
- attn_in_gain: float32 [2048], P('fsdp'), may hold values from 0.25 to 1.75
- query_gain: float32 [256], P('fsdp'), may hold values from 0.25 to 1.75
- key_gain: float32 [256], P('fsdp'), may hold values from 0.25 to 1.75
- attn_out_gain: float32 [2048], P('fsdp'), may hold values from 0.25 to 1.75
- laurel_gain: float32 [2048], P('fsdp'), may hold values from 0.25 to 1.75
- ffn_in_gain: float32 [2048], P('fsdp'), may hold values from 0.25 to 1.75
- ffn_out_gain: float32 [2048], P('fsdp'), may hold values from 0.25 to 1.75
- ple_gain: float32 [2048], P('fsdp'), may hold values from 0.25 to 1.75
Outputs:
- layer_out: bfloat16 [4096, 2048], P(('ctx', 'fsdp'))
- grad_tokens: float32 [4096, 2048], P(('ctx', 'fsdp'))
- grad_per_layer: float32 [4096, 256], P(('ctx', 'fsdp'))
- grad_w_query: float32 [2048, 2048], P('fsdp')
- grad_w_key: float32 [2048, 512], P('fsdp')
- grad_w_value: float32 [2048, 512], P('fsdp')
- grad_w_out: float32 [2048, 2048], P('fsdp')
- grad_laurel_left: float32 [2048, 64], P('fsdp')
- grad_laurel_right: float32 [64, 2048], P('fsdp')
- grad_w_gate: float32 [2048, 8192], P('fsdp')
- grad_w_up: float32 [2048, 8192], P('fsdp')
- grad_w_down: float32 [8192, 2048], P('fsdp')
- grad_ple_gate: float32 [2048, 256], P('fsdp')
- grad_ple_proj: float32 [256, 2048], P('fsdp')
- grad_attn_in_gain: float32 [2048], P('fsdp')
- grad_query_gain: float32 [256], P('fsdp')
- grad_key_gain: float32 [256], P('fsdp')
- grad_attn_out_gain: float32 [2048], P('fsdp')
- grad_laurel_gain: float32 [2048], P('fsdp')
- grad_ffn_in_gain: float32 [2048], P('fsdp')
- grad_ffn_out_gain: float32 [2048], P('fsdp')
- grad_ple_gain: float32 [2048], P('fsdp')
Inputs may be any that keep to these rules, and one draw needn't show every extreme that they name: `doc_lengths`: the 7 lengths are in token order and sum to 4096; the first (6) // 2 and the last (6) // 2 are each at most 21. Each document's positions start at 0 at its first token and rise by 1 or 2 from one token to the next.
All inputs are finite; a program needn't handle non-finite values.
Results may differ from a plain program's by a relative error of at most 0.025.
Values may be sent and summed in bfloat16 or wider, within the bound.
A program may use at most 256 MiB of HBM per device.

v0:
```python
import functools
import math

import jax
import jax.numpy as jnp
from jax import lax
from jax.sharding import PartitionSpec as P

HQ = 8
KV = 2
HD = 256
WINDOW = 1024


EPSILON = 1e-06
NEGATIVE = -1e30
ROPE_BASE = 10000.0
HALF_ROOT = 1.0 / math.sqrt(2.0)


def passed_along(block, axis, distance):
    devices = range(lax.axis_size(axis))
    route = [(i - distance, i) for i in devices if i - distance in devices]
    return lax.ppermute(block, axis, route)


def matmul(left_mat, right_mat):
    return jnp.dot(left_mat, right_mat, preferred_element_type=jnp.float32)


def matmul_tn(left_mat, right_mat):
    return lax.dot_general(
        left_mat, right_mat, (((0,), (0,)), ((), ())), preferred_element_type=jnp.float32
    )


def matmul_nt(left_mat, right_mat):
    return lax.dot_general(
        left_mat, right_mat, (((1,), (1,)), ((), ())), preferred_element_type=jnp.float32
    )


def rms_norm(values, gain_vec):
    return (
        values * lax.rsqrt(jnp.mean(values * values, axis=-1, keepdims=True) + EPSILON) * gain_vec
    )


def rope_tables(positions, width):
    half_width = width // 2
    frequency = jnp.exp(
        jnp.arange(half_width, dtype=jnp.float32) * (-2.0 * math.log(ROPE_BASE) / width)
    )
    angles = positions.astype(jnp.float32)[:, None] * frequency[None, :]
    return (jnp.cos(angles)[:, None, :], jnp.sin(angles)[:, None, :])


def rotate(values, cosine, sine_part):
    half_width = values.shape[-1] // 2
    first_half = values[..., :half_width]
    second_half = values[..., half_width:]
    return jnp.concatenate(
        [
            first_half * cosine - second_half * sine_part,
            second_half * cosine + first_half * sine_part,
        ],
        axis=-1,
    )


def document_ids(doc_lengths, places):
    doc_ends = jnp.cumsum(doc_lengths)
    return jnp.sum((places[:, None] >= doc_ends[None, :-1]).astype(jnp.int32), axis=1)


def query_key(cosine, sine_part, query_lin, key_lin, gain_query, gain_key):
    tok_count = query_lin.shape[0]
    query_rot = rotate(
        rms_norm(query_lin.reshape(tok_count, HQ, HD), gain_query), cosine, sine_part
    )
    key_rot = rotate(rms_norm(key_lin.reshape(tok_count, KV, HD), gain_key), cosine, sine_part)
    return (query_rot, key_rot)


def mix_piece(inputs, normed, projected, widened, gain_post, gain_laurel):
    return (
        inputs + rms_norm(projected, gain_post) + normed + rms_norm(widened, gain_laurel)
    ) * HALF_ROOT


def geglu(gate_lin, up_lin):
    return jax.nn.gelu(gate_lin, approximate=True) * up_lin


def ffn_out_piece(mixed, down_lin, gain_ffout):
    return mixed + rms_norm(down_lin, gain_ffout)


def ple_act(ple_lin, ple_input):
    return jax.nn.gelu(ple_lin, approximate=True) * ple_input


def final_piece(layer_mid, ple_wide, gain_ple):
    return layer_mid + rms_norm(ple_wide, gain_ple)


def visibility(doc_lengths, query_start, key_start, tok_count, span_len):
    query_places = query_start + jnp.arange(tok_count, dtype=jnp.int32)
    key_places = key_start + jnp.arange(span_len, dtype=jnp.int32)
    distance = query_places[:, None] - key_places[None, :]
    query_docs = document_ids(doc_lengths, query_places)
    key_docs = document_ids(doc_lengths, key_places)
    return (
        (distance >= 0)
        & (distance < WINDOW)
        & (key_places[None, :] >= 0)
        & (query_docs[:, None] == key_docs[None, :])
    )


def attend_forward(query_low, span_kv, visible):
    tok_count = query_low.shape[0]
    scale_factor = 1.0 / math.sqrt(HD)
    scores = (
        jnp.einsum("tkgh,skh->kgts", query_low, span_kv[0], preferred_element_type=jnp.float32)
        * scale_factor
    )
    scores = jnp.where(visible, scores, NEGATIVE)
    row_top = jnp.max(scores, axis=-1, keepdims=True)
    shifted = jnp.exp(scores - row_top)
    row_total = jnp.sum(shifted, axis=-1, keepdims=True)
    attn_probs = shifted / row_total
    attended = jnp.einsum(
        "kgts,skh->tkgh",
        attn_probs.astype(jnp.bfloat16),
        span_kv[1],
        preferred_element_type=jnp.float32,
    )
    return (attended.reshape(tok_count, -1), row_top + jnp.log(row_total))


def attend_backward(query_low, span_kv, visible, log_total, grad_out_low):
    scale_factor = 1.0 / math.sqrt(HD)
    scores = (
        jnp.einsum("tkgh,skh->kgts", query_low, span_kv[0], preferred_element_type=jnp.float32)
        * scale_factor
    )
    attn_probs = jnp.where(visible, jnp.exp(jnp.where(visible, scores, NEGATIVE) - log_total), 0.0)
    grad_probs = jnp.einsum(
        "tkgh,skh->kgts", grad_out_low, span_kv[1], preferred_element_type=jnp.float32
    )
    inner_sum = jnp.sum(attn_probs * grad_probs, axis=-1, keepdims=True)
    grad_scores = (attn_probs * (grad_probs - inner_sum)).astype(jnp.bfloat16)
    grad_query = (
        jnp.einsum("kgts,skh->tkgh", grad_scores, span_kv[0], preferred_element_type=jnp.float32)
        * scale_factor
    )
    grad_keys = (
        jnp.einsum("kgts,tkgh->skh", grad_scores, query_low, preferred_element_type=jnp.float32)
        * scale_factor
    )
    grad_values = jnp.einsum(
        "kgts,tkgh->skh",
        attn_probs.astype(jnp.bfloat16),
        grad_out_low,
        preferred_element_type=jnp.float32,
    )
    return (grad_query, jnp.stack([grad_keys, grad_values]))


def settle(act_low, grad_low):
    act_cols = lax.all_to_all(act_low, "fsdp", split_axis=1, concat_axis=0, tiled=True)
    shard_rows = matmul_tn(act_cols, lax.all_gather(grad_low, "fsdp", axis=0, tiled=True))
    return lax.psum(shard_rows.astype(jnp.bfloat16), "ctx").astype(jnp.float32)


def local(
    tokens,
    per_layer,
    cotangent,
    doc_lengths,
    positions,
    w_query,
    w_key,
    w_value,
    w_out,
    laurel_left,
    laurel_right,
    w_gate,
    w_up,
    w_down,
    ple_gate,
    ple_proj,
    attn_in_gain,
    query_gain,
    key_gain,
    attn_out_gain,
    laurel_gain,
    ffn_in_gain,
    ffn_out_gain,
    ple_gain,
):
    bfloat = jnp.bfloat16
    tok_count = tokens.shape[0]
    span_len = WINDOW + tok_count
    groups = HQ // KV
    dev_index = lax.axis_index("ctx") * lax.axis_size("fsdp") + lax.axis_index("fsdp")
    query_start = dev_index * tok_count
    key_start = query_start - WINDOW
    visible = visibility(doc_lengths, query_start, key_start, tok_count, span_len)
    cosine, sine_part = rope_tables(positions, HD)
    gain_in, gain_query, gain_key, gain_post, gain_laurel, gain_ffin, gain_ffout, gain_ple = (
        lax.all_gather(attn_in_gain, "fsdp", axis=0, tiled=True),
        lax.all_gather(query_gain, "fsdp", axis=0, tiled=True),
        lax.all_gather(key_gain, "fsdp", axis=0, tiled=True),
        lax.all_gather(attn_out_gain, "fsdp", axis=0, tiled=True),
        lax.all_gather(laurel_gain, "fsdp", axis=0, tiled=True),
        lax.all_gather(ffn_in_gain, "fsdp", axis=0, tiled=True),
        lax.all_gather(ffn_out_gain, "fsdp", axis=0, tiled=True),
        lax.all_gather(ple_gain, "fsdp", axis=0, tiled=True),
    )
    full_query, full_key, full_value, full_out, full_left, full_right = (
        lax.all_gather(w_query.astype(bfloat), "fsdp", axis=0, tiled=True),
        lax.all_gather(w_key.astype(bfloat), "fsdp", axis=0, tiled=True),
        lax.all_gather(w_value.astype(bfloat), "fsdp", axis=0, tiled=True),
        lax.all_gather(w_out.astype(bfloat), "fsdp", axis=0, tiled=True),
        lax.all_gather(laurel_left.astype(bfloat), "fsdp", axis=0, tiled=True),
        lax.all_gather(laurel_right.astype(bfloat), "fsdp", axis=0, tiled=True),
    )
    inputs = tokens.astype(jnp.float32)
    ple_input = per_layer.astype(jnp.float32)
    normed, norm_back = jax.vjp(rms_norm, inputs, gain_in)
    normed_low = normed.astype(bfloat)
    query_lin = matmul(normed_low, full_query)
    key_lin = matmul(normed_low, full_key)
    value_lin = matmul(normed_low, full_value)
    (query_rot, key_rot), rope_back = jax.vjp(
        functools.partial(query_key, cosine, sine_part), query_lin, key_lin, gain_query, gain_key
    )
    query_low = query_rot.astype(bfloat).reshape(tok_count, KV, groups, HD)
    keys_values = jnp.stack(
        [key_rot.astype(bfloat), value_lin.astype(bfloat).reshape(tok_count, KV, HD)]
    )
    block_kv = lax.all_gather(keys_values, "fsdp", axis=1, tiled=True)
    block_len = block_kv.shape[1]
    before_kv = passed_along(block_kv, "ctx", 1)
    span_offset = block_len + lax.axis_index("fsdp") * tok_count - WINDOW
    span_kv = lax.dynamic_slice_in_dim(
        jnp.concatenate([before_kv, block_kv], axis=1), span_offset, span_len, 1
    )
    attended, log_total = attend_forward(query_low, span_kv, visible)
    attended_low = attended.astype(bfloat)
    projected = matmul(attended_low, full_out)
    narrow_low = matmul(normed_low, full_left).astype(bfloat)
    widened = matmul(narrow_low, full_right)
    mixed, mix_back = jax.vjp(mix_piece, inputs, normed, projected, widened, gain_post, gain_laurel)
    full_gate, full_up, full_down, full_pgate, full_pproj = (
        lax.all_gather(w_gate.astype(bfloat), "fsdp", axis=0, tiled=True),
        lax.all_gather(w_up.astype(bfloat), "fsdp", axis=0, tiled=True),
        lax.all_gather(w_down.astype(bfloat), "fsdp", axis=0, tiled=True),
        lax.all_gather(ple_gate.astype(bfloat), "fsdp", axis=0, tiled=True),
        lax.all_gather(ple_proj.astype(bfloat), "fsdp", axis=0, tiled=True),
    )
    ffn_normed, ffn_norm_back = jax.vjp(rms_norm, mixed, gain_ffin)
    ffn_low = ffn_normed.astype(bfloat)
    gate_lin = matmul(ffn_low, full_gate)
    up_lin = matmul(ffn_low, full_up)
    hidden, geglu_back = jax.vjp(geglu, gate_lin, up_lin)
    hidden_low = hidden.astype(bfloat)
    down_lin = matmul(hidden_low, full_down)
    layer_mid, ffn_out_back = jax.vjp(ffn_out_piece, mixed, down_lin, gain_ffout)
    layer_low = layer_mid.astype(bfloat)
    ple_lin = matmul(layer_low, full_pgate)
    ple_mid, ple_back = jax.vjp(ple_act, ple_lin, ple_input)
    ple_low = ple_mid.astype(bfloat)
    ple_wide = matmul(ple_low, full_pproj)
    out_full, final_back = jax.vjp(final_piece, layer_mid, ple_wide, gain_ple)
    full_gate, full_up, full_down, full_pgate, full_pproj = (
        lax.all_gather(w_gate.astype(bfloat), "fsdp", axis=0, tiled=True),
        lax.all_gather(w_up.astype(bfloat), "fsdp", axis=0, tiled=True),
        lax.all_gather(w_down.astype(bfloat), "fsdp", axis=0, tiled=True),
        lax.all_gather(ple_gate.astype(bfloat), "fsdp", axis=0, tiled=True),
        lax.all_gather(ple_proj.astype(bfloat), "fsdp", axis=0, tiled=True),
    )
    grad_layer, grad_pwide, grad_gple = final_back(cotangent.astype(jnp.float32))
    grad_pwide_low = grad_pwide.astype(bfloat)
    grad_pproj = settle(ple_low, grad_pwide_low)
    grad_plemid = matmul_nt(grad_pwide_low, full_pproj)
    grad_plelin, grad_pleinput = ple_back(grad_plemid)
    grad_plelin_low = grad_plelin.astype(bfloat)
    grad_pgate = settle(layer_low, grad_plelin_low)
    grad_layer = grad_layer + matmul_nt(grad_plelin_low, full_pgate)
    grad_mixed, grad_down, grad_gffout = ffn_out_back(grad_layer)
    grad_down_low = grad_down.astype(bfloat)
    grad_wdown = settle(hidden_low, grad_down_low)
    grad_hidden = matmul_nt(grad_down_low, full_down)
    grad_gate, grad_up = geglu_back(grad_hidden)
    grad_gate_low = grad_gate.astype(bfloat)
    grad_up_low = grad_up.astype(bfloat)
    grad_wgate = settle(ffn_low, grad_gate_low)
    grad_wup = settle(ffn_low, grad_up_low)
    grad_ffn = matmul_nt(grad_gate_low, full_gate) + matmul_nt(grad_up_low, full_up)
    grad_mixed_more, grad_gffin = ffn_norm_back(grad_ffn)
    grad_mixed = grad_mixed + grad_mixed_more
    full_query, full_key, full_value, full_out, full_left, full_right = (
        lax.all_gather(w_query.astype(bfloat), "fsdp", axis=0, tiled=True),
        lax.all_gather(w_key.astype(bfloat), "fsdp", axis=0, tiled=True),
        lax.all_gather(w_value.astype(bfloat), "fsdp", axis=0, tiled=True),
        lax.all_gather(w_out.astype(bfloat), "fsdp", axis=0, tiled=True),
        lax.all_gather(laurel_left.astype(bfloat), "fsdp", axis=0, tiled=True),
        lax.all_gather(laurel_right.astype(bfloat), "fsdp", axis=0, tiled=True),
    )
    grad_in_first, grad_normed, grad_proj, grad_lwide, grad_gpost, grad_glaurel = mix_back(
        grad_mixed
    )
    grad_proj_low = grad_proj.astype(bfloat)
    grad_wout = settle(attended_low, grad_proj_low)
    grad_att_low = matmul_nt(grad_proj_low, full_out).astype(bfloat)
    grad_lwide_low = grad_lwide.astype(bfloat)
    grad_wright = settle(narrow_low, grad_lwide_low)
    grad_narrow_low = matmul_nt(grad_lwide_low, full_right).astype(bfloat)
    grad_wleft = settle(normed_low, grad_narrow_low)
    grad_normed = grad_normed + matmul_nt(grad_narrow_low, full_left)
    grad_query_att, grad_span = attend_backward(
        query_low, span_kv, visible, log_total, grad_att_low.reshape(tok_count, KV, groups, HD)
    )
    whole_grad = jnp.zeros((2, 2 * block_len, KV, HD), jnp.float32)
    whole_grad = lax.dynamic_update_slice_in_dim(whole_grad, grad_span, span_offset, 1)
    returned = passed_along(whole_grad[:, :block_len].astype(jnp.bfloat16), "ctx", -1).astype(
        jnp.float32
    )
    own_grad = lax.psum_scatter(
        (whole_grad[:, block_len:] + returned).astype(jnp.bfloat16),
        "fsdp",
        scatter_dimension=1,
        tiled=True,
    ).astype(jnp.float32)
    grad_qlin, grad_klin, grad_gquery, grad_gkey = rope_back(
        (grad_query_att.reshape(tok_count, HQ, HD), own_grad[0])
    )
    grad_qlin_low = grad_qlin.astype(bfloat)
    grad_klin_low = grad_klin.astype(bfloat)
    grad_vlin_low = own_grad[1].reshape(tok_count, KV * HD).astype(bfloat)
    grad_wquery = settle(normed_low, grad_qlin_low)
    grad_wkey = settle(normed_low, grad_klin_low)
    grad_wvalue = settle(normed_low, grad_vlin_low)
    grad_normed = (
        grad_normed
        + matmul_nt(grad_qlin_low, full_query)
        + matmul_nt(grad_klin_low, full_key)
        + matmul_nt(grad_vlin_low, full_value)
    )
    grad_in_second, grad_gin = norm_back(grad_normed)
    grad_tokens = grad_in_first + grad_in_second
    sum_gin, sum_gquery, sum_gkey, sum_gpost, sum_glaurel, sum_gffin, sum_gffout, sum_gple = (
        lax.psum(
            (
                grad_gin,
                grad_gquery,
                grad_gkey,
                grad_gpost,
                grad_glaurel,
                grad_gffin,
                grad_gffout,
                grad_gple,
            ),
            ("ctx", "fsdp"),
        )
    )
    wide_rows = attn_in_gain.shape[0]
    head_rows = query_gain.shape[0]
    wide_start = lax.axis_index("fsdp") * wide_rows
    head_start = lax.axis_index("fsdp") * head_rows

    def wide_part(full_vec):
        return lax.dynamic_slice_in_dim(full_vec, wide_start, wide_rows, 0)

    def head_part(full_vec):
        return lax.dynamic_slice_in_dim(full_vec, head_start, head_rows, 0)

    return (
        out_full.astype(bfloat),
        grad_tokens,
        grad_pleinput,
        grad_wquery,
        grad_wkey,
        grad_wvalue,
        grad_wout,
        grad_wleft,
        grad_wright,
        grad_wgate,
        grad_wup,
        grad_wdown,
        grad_pgate,
        grad_pproj,
        wide_part(sum_gin),
        head_part(sum_gquery),
        head_part(sum_gkey),
        wide_part(sum_gpost),
        wide_part(sum_glaurel),
        wide_part(sum_gffin),
        wide_part(sum_gffout),
        wide_part(sum_gple),
    )


def solution(mesh):
    in_specs = (
        P(("ctx", "fsdp"), None),
        P(("ctx", "fsdp"), None),
        P(("ctx", "fsdp"), None),
        P(),
        P(("ctx", "fsdp")),
        P("fsdp", None),
        P("fsdp", None),
        P("fsdp", None),
        P("fsdp", None),
        P("fsdp", None),
        P("fsdp", None),
        P("fsdp", None),
        P("fsdp", None),
        P("fsdp", None),
        P("fsdp", None),
        P("fsdp", None),
        P("fsdp"),
        P("fsdp"),
        P("fsdp"),
        P("fsdp"),
        P("fsdp"),
        P("fsdp"),
        P("fsdp"),
        P("fsdp"),
    )
    out_specs = (
        P(("ctx", "fsdp"), None),
        P(("ctx", "fsdp"), None),
        P(("ctx", "fsdp"), None),
        P("fsdp", None),
        P("fsdp", None),
        P("fsdp", None),
        P("fsdp", None),
        P("fsdp", None),
        P("fsdp", None),
        P("fsdp", None),
        P("fsdp", None),
        P("fsdp", None),
        P("fsdp", None),
        P("fsdp", None),
        P("fsdp"),
        P("fsdp"),
        P("fsdp"),
        P("fsdp"),
        P("fsdp"),
        P("fsdp"),
        P("fsdp"),
        P("fsdp"),
    )
    return jax.shard_map(local, mesh=mesh, in_specs=in_specs, out_specs=out_specs, check_vma=False)
```

profile of v0, /device:TPU:0, one launch (start us, length us, event | category | flops | bytes accessed | tf_op | source)
XLA Modules:
  0.0 2411.7 jit_solution(16484588854279291133)
XLA Ops:
  15.2 18.4 all-reduce.7
  47.5 25.6 %all-gather.26.cloned.1.call-done = bf16[2048,512]{1,0:T(8,128)(2,1)} async-done(((bf16[256,512]{1,0:T(8,128)(2,1)}), bf16[2048,512]{1,0:T(8,128)(2,1)}) %all-gather.26.cloned.1.call-update) | async-done | bytes 2097168 | tf_op jit(solution)/shard_map/all_gather | solution.py:224
  126.5 11.6 all-gather.3
  159.7 16.8 all_gather.113
  176.5 15.9 all_gather.114
  214.8 61.6 %all-gather.34.cloned.1.call-done = bf16[2048,2048]{1,0:T(8,128)(2,1)} async-done(((bf16[256,2048]{1,0:T(8,128)(2,1)}), bf16[2048,2048]{1,0:T(8,128)(2,1)}) %all-gather.34.cloned.1.call-update) | async-done | bytes 8388624 | tf_op jit(solution)/shard_map/all_gather | solution.py:226
  284.3 281.3 %all-gather.36.cloned.1.call-done = bf16[2048,8192]{1,0:T(8,128)(2,1)} async-done(((bf16[256,8192]{1,0:T(8,128)(2,1)}), bf16[2048,8192]{1,0:T(8,128)(2,1)}) %all-gather.36.cloned.1.call-update) | async-done | bytes 33554448 | tf_op jit(solution)/shard_map/all_gather | solution.py:258
  565.6 19.7 fusion.83
  585.3 269.3 %all-gather.38.cloned.1.call-done = bf16[2048,8192]{1,0:T(8,128)(2,1)} async-done(((bf16[256,8192]{1,0:T(8,128)(2,1)}), bf16[2048,8192]{1,0:T(8,128)(2,1)}) %all-gather.38.cloned.1.call-update) | async-done | bytes 33554448 | tf_op jit(solution)/shard_map/all_gather | solution.py:259
  854.6 20.6 multiply_convert_fusion.1
  875.2 267.9 %all-gather.40.cloned.1.call-done = bf16[8192,2048]{1,0:T(8,128)(2,1)} async-done(((bf16[1024,2048]{1,0:T(8,128)(2,1)}), bf16[8192,2048]{1,0:T(8,128)(2,1)}) %all-gather.40.cloned.1.call-update) | async-done | bytes 33554448 | tf_op jit(solution)/shard_map/all_gather | solution.py:260
  1143.1 13.8 multiply_reduce_fusion.11
  1167.9 21.5 all-gather.44.cloned.1.call-done
  1203.5 20.8 multiply_convert_fusion
  1224.3 17.3 fusion.84
  1241.6 18.7 multiply_reduce_fusion.1
  1285.5 48.4 %collective-permute-done.1 = bf16[2,1024,2,256]{3,1,2,0:T(8,128)(2,1)S(1)} collective-permute-done((bf16[2,1024,2,256]{3,1,2,0:T(8,128)(2,1)S(1)}, bf16[2,1024,2,256]{3,1,2,0:T(8,128)(2,1)S(1)}, u32[]{:S(2)}, u32[]{:S(2)}) %collective-permute-start.1) | collective-permute-done | bytes 2097184 | tf_op jit(solution)/shard_map/ppermute | solution.py:24
  1350.4 20.9 reduce-scatter.2.cloned.1.call-done
  1389.4 29.0 %all-to-all-done = bf16[128,8,256]{2,0,1:T(8,128)(2,1)S(1)} async-done(((bf16[128,8,256]{2,0,1:T(8,128)(2,1)}), bf16[128,8,256]{2,0,1:T(8,128)(2,1)S(1)}, u32[]{:S(2)}, u32[]{:S(2)}) %all-to-all-start) | async-done | bytes 524320 | tf_op jit(solution)/shard_map/all_to_all | solution.py:172
  1434.0 20.3 all-to-all-done.5
  1461.0 71.8 %all_gather.128 = bf16[1024,64]{0,1:T(8,128)(2,1)S(1)} all-gather(bf16[128,64]{0,1:T(8,128)(2,1)S(1)} %convolution_convert_fusion.13), channel_id=1, replica_groups=mesh['ctx'=4,'fsdp'=8] {'fsdp'}, dimensions={0}, use_global_device_ids=true | all-gather | bytes 147456 | tf_op jit(solution)/shard_map/all_gather | solution.py:173
  1532.8 16.9 all_gather.133
  1576.6 50.8 %all-gather.60.cloned.1.call-done = bf16[1024,2048]{1,0:T(8,128)(2,1)} async-done(((bf16[128,2048]{1,0:T(8,128)(2,1)}), bf16[1024,2048]{1,0:T(8,128)(2,1)}) %all-gather.60.cloned.1.call-update) | async-done | bytes 4194320 | tf_op jit(solution)/shard_map/all_gather | solution.py:173
  1640.6 45.4 %all-gather.52.cloned.1.call-done = bf16[1024,2048]{1,0:T(8,128)(2,1)} async-done(((bf16[128,2048]{1,0:T(8,128)(2,1)}), bf16[1024,2048]{1,0:T(8,128)(2,1)}) %all-gather.52.cloned.1.call-update) | async-done | bytes 4194320 | tf_op jit(solution)/shard_map/all_gather | solution.py:173
  1690.4 19.7 all-gather.48.cloned.1.call-done
  1712.5 21.6 all-gather.50.cloned.1.call-done
  1736.6 148.9 %all-gather.56.cloned.1.call-done = bf16[1024,8192]{1,0:T(8,128)(2,1)} async-done(((bf16[128,8192]{1,0:T(8,128)(2,1)}), bf16[1024,8192]{1,0:T(8,128)(2,1)}) %all-gather.56.cloned.1.call-update) | async-done | bytes 16777232 | tf_op jit(solution)/shard_map/all_gather | solution.py:173
  1885.5 12.1 convolution_convert_fusion.1
  1897.6 139.3 %all-gather.58.cloned.1.call-done = bf16[1024,8192]{1,0:T(8,128)(2,1)} async-done(((bf16[128,8192]{1,0:T(8,128)(2,1)}), bf16[1024,8192]{1,0:T(8,128)(2,1)}) %all-gather.58.cloned.1.call-update) | async-done | bytes 16777232 | tf_op jit(solution)/shard_map/all_gather | solution.py:173
  2036.9 12.1 convolution_convert_fusion
  2059.3 39.6 %all-reduce.6 = (f32[2048]{0:T(1024)S(1)}, f32[256]{0:T(256)S(1)}, f32[256]{0:T(256)S(1)}, f32[2048]{0:T(1024)S(1)}, f32[2048]{0:T(1024)S(1)}, /*index=5*/f32[20...) all-reduce(f32[2048]{0:T(1024)S(1)} %get-tuple-element.32, ...), channel_id=1, replica_groups=mesh['ctx'=4,'fsdp'=8] {'ctx','fsdp'}, use_global_device_ids=true, to_apply=%region_35.36 | all-reduce | flops 12800 | bytes 102400 | tf_op jit(solution)/shard_map/psum | solution.py:356
  2108.0 272.6 %all-reduce.15.cloned.1.call-done = (bf16[256,2048]{1,0:T(8,128)(2,1)}, bf16[256,512]{1,0:T(8,128)(2,1)}, bf16[256,512]{1,0:T(8,128)(2,1)}, bf16[256,2048]{1,0:T...) async-done(((bf16[256,2048]{1,0:T(8,128)(2,1)}, ...) | async-done | bytes 15466512 | tf_op jit(solution)/shard_map/psum | solution.py:174
  (470 shorter events, 324.6 us)
Async XLA Ops:
  7.2 38.2 %all-gather.28.cloned.1.call-start = ((), (), s32[]{:S(2)}) async-start(), calls=%async_computation.9 | async-start | bytes 2359296 | tf_op jit(solution)/shard_map/all_gather | solution.py:225
  9.0 64.1 %all-gather.26.cloned.1.call-start = ((), (), s32[]{:S(2)}) async-start(), calls=%async_computation.8 | async-start | bytes 2359296 | tf_op jit(solution)/shard_map/all_gather | solution.py:224
  10.9 112.0 %all-gather.30.cloned.1.call-start = ((), (), s32[]{:S(2)}) async-start(), calls=%async_computation.10 | async-start | bytes 2359296 | tf_op jit(solution)/shard_map/all_gather | solution.py:244
  33.7 174.5 %copy-start.84 = (f32[256]{0:T(256)}, f32[256]{0:T(256)S(1)}, u32[]{:S(2)}) copy-start(f32[256]{0:T(256)S(1)} %get-tuple-element.49) | copy-start | bytes 3076
  77.0 124.8 %all-gather.32.cloned.1.call-start = ((), (), s32[]{:S(2)}) async-start(), calls=%async_computation.11 | async-start | bytes 9437184 | tf_op jit(solution)/shard_map/all_gather | solution.py:223
  79.8 196.6 %all-gather.34.cloned.1.call-start = ((), (), s32[]{:S(2)}) async-start(), calls=%async_computation.12 | async-start | bytes 9437184 | tf_op jit(solution)/shard_map/all_gather | solution.py:226
  82.6 483.0 %all-gather.36.cloned.1.call-start = ((), (), s32[]{:S(2)}) async-start(), calls=%async_computation.13 | async-start | bytes 37748736 | tf_op jit(solution)/shard_map/all_gather | solution.py:258
  89.0 765.7 %all-gather.38.cloned.1.call-start = ((), (), s32[]{:S(2)}) async-start(), calls=%async_computation.14 | async-start | bytes 37748736 | tf_op jit(solution)/shard_map/all_gather | solution.py:259
  95.1 1048.0 %all-gather.40.cloned.1.call-start = ((), (), s32[]{:S(2)}) async-start(), calls=%async_computation.15 | async-start | bytes 37748736 | tf_op jit(solution)/shard_map/all_gather | solution.py:260
  101.3 1064.2 %all-gather.42.cloned.1.call-start = ((), (), s32[]{:S(2)}) async-start(), calls=%async_computation.16 | async-start | bytes 1179648 | tf_op jit(solution)/shard_map/all_gather | solution.py:261
  102.9 1086.5 %all-gather.44.cloned.1.call-start = ((), (), s32[]{:S(2)}) async-start(), calls=%async_computation.17 | async-start | bytes 1179648 | tf_op jit(solution)/shard_map/all_gather | solution.py:262
  103.6 1267.7 %reduce-scatter.2.cloned.1.call-start = ((), (), s32[]{:S(2)}) async-start(), calls=%async_computation.18 | async-start | bytes 2359296 | tf_op jit(solution)/shard_map/reduce_scatter | solution.py:332
  122.9 75.4 %collective-permute-start = (bf16[2,1024,2,256]{3,1,2,0:T(8,128)(2,1)}, bf16[2,1024,2,256]{3,1,2,0:T(8,128)(2,1)S(1)}, u32[]{:S(2)}, u32[]{:S(2)}) collective-permute-start(bf16[2,1024,2,256]{3,1,2,0:T(8,128)(2,1)} %all-gather.30.cloned.1.call-done), channel_id=1, source_target_pairs={{0,8},{8,16},{16,24},{1,9},{9,17},{17,25},{2,10},{10,18},{18,26},{... | collective-permute-start | bytes 6291464 | tf_op jit(solution)/shard_map/ppermute | solution.py:24
  1284.2 49.7 %collective-permute-start.1 = (bf16[2,1024,2,256]{3,1,2,0:T(8,128)(2,1)S(1)}, bf16[2,1024,2,256]{3,1,2,0:T(8,128)(2,1)S(1)}, u32[]{:S(2)}, u32[]{:S(2)}) collective-permute-start(bf16[2,1024,2,256]{3,1,2,0:T(8,128)(2,1)S(1)} %slice.92), channel_id=1, source_target_pairs={{8,0},{16,8},{24,16},{9,1},{17,9},{25,17},{10,2},{18,10},{26,18},{... | collective-permute-start | bytes 6291464 | tf_op jit(solution)/shard_map/ppermute | solution.py:24
  1335.8 216.9 %all-gather.54.cloned.1.call-start = ((), (), s32[]{:S(2)}) async-start(), calls=%async_computation.23 | async-start | bytes 4718592 | tf_op jit(solution)/shard_map/all_gather | solution.py:173
  1336.4 219.8 %all-gather.62.cloned.1.call-start = ((), (), s32[]{:S(2)}) async-start(), calls=%async_computation.27 | async-start | bytes 4718592 | tf_op jit(solution)/shard_map/all_gather | solution.py:173
  1337.1 231.5 %all-gather.46.cloned.1.call-start = ((), (), s32[]{:S(2)}) async-start(), calls=%async_computation.19 | async-start | bytes 4718592 | tf_op jit(solution)/shard_map/all_gather | solution.py:173
  1349.2 278.3 %all-gather.60.cloned.1.call-start = ((), (), s32[]{:S(2)}) async-start(), calls=%async_computation.26 | async-start | bytes 4718592 | tf_op jit(solution)/shard_map/all_gather | solution.py:173
  1349.8 336.2 %all-gather.52.cloned.1.call-start = ((), (), s32[]{:S(2)}) async-start(), calls=%async_computation.22 | async-start | bytes 4718592 | tf_op jit(solution)/shard_map/all_gather | solution.py:173
  1350.3 359.7 %all-gather.48.cloned.1.call-start = ((), (), s32[]{:S(2)}) async-start(), calls=%async_computation.20 | async-start | bytes 1179648 | tf_op jit(solution)/shard_map/all_gather | solution.py:173
  1374.0 360.1 %all-gather.50.cloned.1.call-start = ((), (), s32[]{:S(2)}) async-start(), calls=%async_computation.21 | async-start | bytes 1179648 | tf_op jit(solution)/shard_map/all_gather | solution.py:173
  1374.9 510.6 %all-gather.56.cloned.1.call-start = ((), (), s32[]{:S(2)}) async-start(), calls=%async_computation.24 | async-start | bytes 18874368 | tf_op jit(solution)/shard_map/all_gather | solution.py:173
  1375.6 661.3 %all-gather.58.cloned.1.call-start = ((), (), s32[]{:S(2)}) async-start(), calls=%async_computation.25 | async-start | bytes 18874368 | tf_op jit(solution)/shard_map/all_gather | solution.py:173
  1376.2 8.9 all-to-all-start.2
  1385.2 33.2 %all-to-all-start = ((bf16[128,8,256]{2,0,1:T(8,128)(2,1)}), bf16[128,8,256]{2,0,1:T(8,128)(2,1)S(1)}, u32[]{:S(2)}, u32[]{:S(2)}) async-start(bf16[128,8,256]{2,0,1:T(8,128)(2,1)} %bitcast.255), calls=%async_computation.1 | async-start | bytes 1048576 | tf_op jit(solution)/shard_map/all_to_all | solution.py:172
  1418.4 9.8 all-to-all-start.6
  1428.2 26.0 %all-to-all-start.5 = ((bf16[128,8,256]{2,0,1:T(8,128)(2,1)}), bf16[128,8,256]{2,0,1:T(8,128)(2,1)}, u32[]{:S(2)}, u32[]{:S(2)}) async-start(bf16[128,8,256]{2,0,1:T(8,128)(2,1)} %bitcast.256), calls=%async_computation.6 | async-start | bytes 1048576 | tf_op jit(solution)/shard_map/all_to_all | solution.py:172
  1454.3 118.8 %all-to-all-start.4 = ((bf16[128,8,1024]{2,0,1:T(8,128)(2,1)}), bf16[128,8,1024]{2,0,1:T(8,128)(2,1)}, u32[]{:S(2)}, u32[]{:S(2)}) async-start(bf16[128,8,1024]{2,0,1:T(8,128)(2,1)} %bitcast.239), calls=%async_computation.5 | async-start | bytes 4194304 | tf_op jit(solution)/shard_map/all_to_all | solution.py:172
  1458.8 646.4 %all-reduce.13.cloned.1.call-start = ((), (), s32[]{:S(2)}) async-start(), calls=%async_computation.28 | async-start | bytes 131072 | tf_op jit(solution)/shard_map/psum | solution.py:174
  1573.1 63.8 %all-to-all-start.1 = ((bf16[128,8,256]{2,0,1:T(8,128)(2,1)}), bf16[128,8,256]{2,0,1:T(8,128)(2,1)S(1)}, u32[]{:S(2)}, u32[]{:S(2)}) async-start(bf16[128,8,256]{2,0,1:T(8,128)(2,1)} %copy.245), calls=%async_computation.2 | async-start | bytes 1048576 | tf_op jit(solution)/shard_map/all_to_all | solution.py:172
  1636.9 99.7 %all-to-all-start.3 = ((bf16[128,8,256]{2,0,1:T(8,128)(2,1)}), bf16[128,8,256]{2,0,1:T(8,128)(2,1)S(1)}, u32[]{:S(2)}, u32[]{:S(2)}) async-start(bf16[128,8,256]{2,0,1:T(8,128)(2,1)} %bitcast.223), calls=%async_computation.4 | async-start | bytes 1048576 | tf_op jit(solution)/shard_map/all_to_all | solution.py:172
  1640.4 740.2 %all-reduce.15.cloned.1.call-start = ((), (), s32[]{:S(2)}) async-start(), calls=%async_computation.29 | async-start | bytes 30932992 | tf_op jit(solution)/shard_map/psum | solution.py:174
  (122 other events, 1933.7 us)
Sparse Core Ops, SparseCore 0:
  10.2 32.0 all-gather.27
  44.5 28.6 all-gather.25
  77.2 28.5 all-gather.29
  107.8 85.7 all-gather.31
  195.6 80.6 all-gather.33
  278.4 287.1 all-gather.35
  567.8 286.7 all-gather.37
  856.2 286.8 all-gather.39
  1145.3 20.2 all-gather.41
  1167.6 21.7 all-gather.43
  1335.9 35.3 reduce-scatter.1
  1373.3 58.8 all-gather.53
  1434.4 82.1 all-gather.61
  1518.1 50.5 all-gather.45
  1570.1 57.2 all-gather.59
  1628.9 57.0 all-gather.51
  1687.4 22.6 all-gather.47
  1711.5 22.5 all-gather.49
  1735.7 149.7 all-gather.55
  1887.5 149.3 all-gather.57
  2040.9 39.7 all-reduce.12
  2087.9 292.6 all-reduce.14
where the time goes:
time: 2420 us; the launch traced here: 2410 us
  waiting for transfers between devices  1770 us (73%)
  blocking collectives  240 us (10%)
  matrix products  222 us (9%)
  other arithmetic  93.3 us (4%)
  local copies, waits for them, and re-layouts  34.7 us (1%)
  starting transfers between devices  32.2 us (1%)
    all_gather x9, waiting for transfers between devices, settle(): lax.all_gather(grad_low, 'fsdp', axis=0, tiled=True)  435 us
    all_gather x1, waiting for transfers between devices, local(): lax.all_gather(w_gate.astype(bfloat), 'fsdp', axis=0, tiled=True)  281 us
    psum x2, waiting for transfers between devices, settle(): return lax.psum(shard_rows.astype(jnp.bfloat16), 'ctx').astype(jnp.float32)  273 us
    all_gather x1, waiting for transfers between devices, local(): lax.all_gather(w_up.astype(bfloat), 'fsdp', axis=0, tiled=True)  269 us
    all_gather x1, waiting for transfers between devices, local(): lax.all_gather(w_down.astype(bfloat), 'fsdp', axis=0, tiled=True)  268 us
    all_gather x2, blocking collectives, settle(): lax.all_gather(grad_low, 'fsdp', axis=0, tiled=True)  88.8 us
    dot_general x11, matrix products, matmul_nt(): lax.dot_general(left_mat, right_mat, (((1,), (1,)), ((), ())), preferred_...  78.4 us
    dot_general x11, matrix products, matmul(): return jnp.dot(left_mat, right_mat, preferred_element_type=jnp.float32)  75.4 us
  transfers between devices with their start and end apart: 31, of which 21 were waited for; matrix products, arithmetic and copies ran while one was open for 9% of the time, Pallas kernels for 0%

commit v1 on v0

--- a/solution.py
+++ b/solution.py
@@ -403,6 +403,284 @@
         wide_part(sum_gple),
     )
 
+def to_columns(pieces, ctx_count):
+    packed = jnp.concatenate(pieces, axis=2)
+    quarter = packed.shape[0] // ctx_count
+    start = lax.axis_index("ctx") * quarter
+    mine = lax.dynamic_slice_in_dim(packed, start, quarter, 0).astype(jnp.bfloat16)
+    spread = lax.all_to_all(mine, "fsdp", split_axis=1, concat_axis=0, tiled=False)
+    whole = lax.all_gather(spread, "ctx", axis=1, tiled=True)
+    return whole.reshape(-1, whole.shape[-1])
+
+
+def to_rows(partial, fsdp_count):
+    parts = partial.astype(jnp.bfloat16).reshape(fsdp_count, -1, partial.shape[-1])
+    summed = lax.psum_scatter(parts, "ctx", scatter_dimension=1, tiled=True)
+    swapped = lax.all_to_all(summed, "fsdp", split_axis=0, concat_axis=1, tiled=False)
+    return swapped
+
+
+def gather_rows(part):
+    return lax.all_gather(part, "ctx", axis=0, tiled=True).astype(jnp.float32)
+
+
+def scatter_tokens(partial):
+    return lax.psum_scatter(
+        partial.astype(jnp.bfloat16), "fsdp", scatter_dimension=0, tiled=True
+    ).astype(jnp.float32)
+
+
+def gather_tokens(part):
+    return lax.all_gather(part, "fsdp", axis=0, tiled=True)
+
+
+def small_sum(partial):
+    rows = lax.psum_scatter(partial.astype(jnp.bfloat16), "fsdp", scatter_dimension=0, tiled=True)
+    return lax.psum(rows, "ctx").astype(jnp.float32)
+
+
+def row_sum(partial):
+    return lax.psum(partial.astype(jnp.bfloat16), "ctx").astype(jnp.float32)
+
+
+def head_rope(cosine, sine_part, lin, gain_vec):
+    return rotate(rms_norm(lin, gain_vec), cosine, sine_part)
+
+
+def by_heads(
+    tokens,
+    per_layer,
+    cotangent,
+    doc_lengths,
+    positions,
+    w_query,
+    w_key,
+    w_value,
+    w_out,
+    laurel_left,
+    laurel_right,
+    w_gate,
+    w_up,
+    w_down,
+    ple_gate,
+    ple_proj,
+    attn_in_gain,
+    query_gain,
+    key_gain,
+    attn_out_gain,
+    laurel_gain,
+    ffn_in_gain,
+    ffn_out_gain,
+    ple_gain,
+):
+    bfloat = jnp.bfloat16
+    ctx_count = lax.axis_size("ctx")
+    fsdp_count = lax.axis_size("fsdp")
+    tok_count = tokens.shape[0]
+    block_len = tok_count * fsdp_count
+    rows = w_query.shape[0]
+    ff_part = w_gate.shape[1] // fsdp_count
+    scale_factor = 1.0 / math.sqrt(HD)
+    ctx_at = lax.axis_index("ctx")
+    fsdp_at = lax.axis_index("fsdp")
+
+    gain_list = [
+        attn_in_gain,
+        query_gain,
+        key_gain,
+        attn_out_gain,
+        laurel_gain,
+        ffn_in_gain,
+        ffn_out_gain,
+        ple_gain,
+    ]
+    gain_sizes = [g.shape[0] for g in gain_list]
+    gain_offsets = [sum(gain_sizes[:n]) for n in range(len(gain_sizes) + 1)]
+    all_gains = lax.all_gather(jnp.concatenate(gain_list), "fsdp", axis=0, tiled=False)
+    gain_in, gain_query, gain_key, gain_post, gain_laurel, gain_ffin, gain_ffout, gain_ple = (
+        all_gains[:, gain_offsets[n] : gain_offsets[n + 1]].reshape(-1) for n in range(8)
+    )
+    block_positions = lax.all_gather(positions, "fsdp", axis=0, tiled=True)
+    cosine, sine_part = rope_tables(block_positions, HD)
+    cosine, sine_part = cosine[:, 0], sine_part[:, 0]
+
+    query_parts = w_query.reshape(rows, fsdp_count, HD)
+    group_size = HQ // KV
+    key_parts = jnp.repeat(w_key.reshape(rows, KV, HD), group_size, axis=1)
+    value_parts = jnp.repeat(w_value.reshape(rows, KV, HD), group_size, axis=1)
+    col_qkv = to_columns([query_parts, key_parts, value_parts], ctx_count)
+    col_gateup = to_columns(
+        [w_gate.reshape(rows, fsdp_count, ff_part), w_up.reshape(rows, fsdp_count, ff_part)],
+        ctx_count,
+    )
+    out_low = w_out.astype(bfloat)
+    down_low = w_down.astype(bfloat)
+    full_left, full_right, full_pgate, full_pproj = (
+        lax.all_gather(w.astype(bfloat), "fsdp", axis=0, tiled=True)
+        for w in (laurel_left, laurel_right, ple_gate, ple_proj)
+    )
+
+    inputs = tokens.astype(jnp.float32)
+    ple_input = per_layer.astype(jnp.float32)
+    normed, norm_back = jax.vjp(rms_norm, inputs, gain_in)
+    normed_low = normed.astype(bfloat)
+    normed_all = gather_tokens(normed_low)
+    qkv_lin = matmul(normed_all, col_qkv)
+    query_lin, key_lin, value_lin = qkv_lin[:, :HD], qkv_lin[:, HD : 2 * HD], qkv_lin[:, 2 * HD :]
+    rope_here = functools.partial(head_rope, cosine, sine_part)
+    query_rot, query_back = jax.vjp(rope_here, query_lin, gain_query)
+    key_rot, key_back = jax.vjp(rope_here, key_lin, gain_key)
+    query_low = query_rot.astype(bfloat)
+    own_kv = jnp.stack([key_rot.astype(bfloat), value_lin.astype(bfloat)])
+    before_kv = passed_along(own_kv[:, block_len - WINDOW :], "ctx", 1)
+    span_kv = jnp.concatenate([before_kv, own_kv], axis=1)
+
+    chunk = 256
+    span_len = WINDOW + chunk
+    block_start = ctx_at * block_len
+    prob_list, attended_list = [], []
+    for begin in range(0, block_len, chunk):
+        visible = visibility(
+            doc_lengths, block_start + begin, block_start + begin - WINDOW, chunk, span_len
+        )
+        keys = span_kv[0, begin : begin + span_len]
+        values = span_kv[1, begin : begin + span_len]
+        scores = matmul_nt(query_low[begin : begin + chunk], keys) * scale_factor
+        scores = jnp.where(visible, scores, NEGATIVE)
+        shifted = jnp.exp(scores - jnp.max(scores, axis=-1, keepdims=True))
+        probs = shifted / jnp.sum(shifted, axis=-1, keepdims=True)
+        prob_list.append(probs)
+        attended_list.append(matmul(probs.astype(bfloat), values))
+    attended_low = jnp.concatenate(attended_list, axis=0).astype(bfloat)
+    projected = scatter_tokens(matmul(attended_low, out_low))
+    narrow_low = matmul(normed_low, full_left).astype(bfloat)
+    widened = matmul(narrow_low, full_right)
+    mixed, mix_back = jax.vjp(mix_piece, inputs, normed, projected, widened, gain_post, gain_laurel)
+    ffn_normed, ffn_norm_back = jax.vjp(rms_norm, mixed, gain_ffin)
+    ffn_all = gather_tokens(ffn_normed.astype(bfloat))
+    gateup = matmul(ffn_all, col_gateup)
+    hidden, geglu_back = jax.vjp(geglu, gateup[:, :ff_part], gateup[:, ff_part:])
+    hidden_low = hidden.astype(bfloat)
+    down_lin = scatter_tokens(matmul(hidden_low, down_low))
+    layer_mid, ffn_out_back = jax.vjp(ffn_out_piece, mixed, down_lin, gain_ffout)
+    layer_low = layer_mid.astype(bfloat)
+    ple_lin = matmul(layer_low, full_pgate)
+    ple_mid, ple_back = jax.vjp(ple_act, ple_lin, ple_input)
+    ple_low = ple_mid.astype(bfloat)
+    ple_wide = matmul(ple_low, full_pproj)
+    out_full, final_back = jax.vjp(final_piece, layer_mid, ple_wide, gain_ple)
+
+    grad_layer, grad_pwide, grad_gple = final_back(cotangent.astype(jnp.float32))
+    grad_pwide_low = grad_pwide.astype(bfloat)
+    grad_pproj = small_sum(matmul_tn(ple_low, grad_pwide_low))
+    grad_plemid = matmul_nt(grad_pwide_low, full_pproj)
+    grad_plelin, grad_pleinput = ple_back(grad_plemid)
+    grad_plelin_low = grad_plelin.astype(bfloat)
+    grad_pgate = small_sum(matmul_tn(layer_low, grad_plelin_low))
+    grad_layer = grad_layer + matmul_nt(grad_plelin_low, full_pgate)
+    grad_mixed, grad_down, grad_gffout = ffn_out_back(grad_layer)
+    grad_down_all = gather_tokens(grad_down.astype(bfloat))
+    grad_wdown = row_sum(matmul_tn(hidden_low, grad_down_all))
+    grad_hidden = matmul_nt(grad_down_all, down_low)
+    grad_gate, grad_up = geglu_back(grad_hidden)
+    grad_gateup_low = jnp.concatenate([grad_gate, grad_up], axis=1).astype(bfloat)
+    gateup_rows = to_rows(matmul_tn(ffn_all, grad_gateup_low), fsdp_count)
+    gateup_rows = gather_rows(gateup_rows)
+    grad_wgate = gateup_rows[:, :, :ff_part].reshape(rows, -1)
+    grad_wup = gateup_rows[:, :, ff_part:].reshape(rows, -1)
+    grad_ffn = scatter_tokens(matmul_nt(grad_gateup_low, col_gateup))
+    grad_mixed_more, grad_gffin = ffn_norm_back(grad_ffn)
+    grad_mixed = grad_mixed + grad_mixed_more
+    grad_in_first, grad_normed, grad_proj, grad_lwide, grad_gpost, grad_glaurel = mix_back(
+        grad_mixed
+    )
+    grad_proj_all = gather_tokens(grad_proj.astype(bfloat))
+    grad_wout = row_sum(matmul_tn(attended_low, grad_proj_all))
+    grad_att_low = matmul_nt(grad_proj_all, out_low).astype(bfloat)
+    grad_lwide_low = grad_lwide.astype(bfloat)
+    grad_wright = small_sum(matmul_tn(narrow_low, grad_lwide_low))
+    grad_narrow_low = matmul_nt(grad_lwide_low, full_right).astype(bfloat)
+    grad_wleft = small_sum(matmul_tn(normed_low, grad_narrow_low))
+    grad_normed = grad_normed + matmul_nt(grad_narrow_low, full_left)
+
+    grad_query_list = []
+    grad_keys = jnp.zeros((WINDOW + block_len, HD), jnp.float32)
+    grad_values = jnp.zeros((WINDOW + block_len, HD), jnp.float32)
+    for at, begin in enumerate(range(0, block_len, chunk)):
+        keys = span_kv[0, begin : begin + span_len]
+        values = span_kv[1, begin : begin + span_len]
+        probs = prob_list[at]
+        grad_rows = grad_att_low[begin : begin + chunk]
+        grad_probs = matmul_nt(grad_rows, values)
+        inner_sum = jnp.sum(probs * grad_probs, axis=-1, keepdims=True)
+        grad_scores = (probs * (grad_probs - inner_sum)).astype(bfloat)
+        grad_query_list.append(matmul(grad_scores, keys) * scale_factor)
+        grad_keys = grad_keys.at[begin : begin + span_len].add(
+            matmul_tn(grad_scores, query_low[begin : begin + chunk]) * scale_factor
+        )
+        grad_values = grad_values.at[begin : begin + span_len].add(
+            matmul_tn(probs.astype(bfloat), grad_rows)
+        )
+    returned = passed_along(
+        jnp.stack([grad_keys[:WINDOW], grad_values[:WINDOW]]).astype(bfloat), "ctx", -1
+    ).astype(jnp.float32)
+    returned = jnp.pad(returned, ((0, 0), (block_len - WINDOW, 0), (0, 0)))
+    grad_qlin, grad_gquery = query_back(jnp.concatenate(grad_query_list, axis=0))
+    grad_klin, grad_gkey = key_back(grad_keys[WINDOW:] + returned[0])
+    grad_vlin = grad_values[WINDOW:] + returned[1]
+    grad_qkv_low = jnp.concatenate([grad_qlin, grad_klin, grad_vlin], axis=1).astype(bfloat)
+    qkv_rows = to_rows(matmul_tn(normed_all, grad_qkv_low), fsdp_count)
+    kv_rows = qkv_rows[:, :, HD:].astype(jnp.float32)
+    kv_rows = jnp.sum(kv_rows.reshape(kv_rows.shape[0], KV, group_size, 2 * HD), axis=2)
+    quarter = rows // ctx_count
+    qkv_rows = gather_rows(
+        jnp.concatenate(
+            [
+                qkv_rows[:, :, :HD].reshape(quarter, HQ * HD),
+                kv_rows[:, :, :HD].reshape(quarter, KV * HD).astype(bfloat),
+                kv_rows[:, :, HD:].reshape(quarter, KV * HD).astype(bfloat),
+            ],
+            axis=1,
+        )
+    )
+    grad_wquery = qkv_rows[:, : HQ * HD]
+    grad_wkey = qkv_rows[:, HQ * HD : (HQ + KV) * HD]
+    grad_wvalue = qkv_rows[:, (HQ + KV) * HD :]
+    grad_normed = grad_normed + scatter_tokens(matmul_nt(grad_qkv_low, col_qkv))
+    grad_in_second, grad_gin = norm_back(grad_normed)
+    grad_tokens = grad_in_first + grad_in_second
+
+    grad_gains = [
+        grad_gin,
+        grad_gquery,
+        grad_gkey,
+        grad_gpost,
+        grad_glaurel,
+        grad_gffin,
+        grad_gffout,
+        grad_gple,
+    ]
+    gain_rows = jnp.concatenate([g.reshape(fsdp_count, -1) for g in grad_gains], axis=1)
+    gain_sums = lax.psum(gain_rows, ("ctx", "fsdp"))
+    gain_sums = lax.dynamic_index_in_dim(gain_sums, fsdp_at, 0, keepdims=False)
+    return (
+        out_full.astype(bfloat),
+        grad_tokens,
+        grad_pleinput,
+        grad_wquery,
+        grad_wkey,
+        grad_wvalue,
+        grad_wout,
+        grad_wleft,
+        grad_wright,
+        grad_wgate,
+        grad_wup,
+        grad_wdown,
+        grad_pgate,
+        grad_pproj,
+        *(gain_sums[gain_offsets[n] : gain_offsets[n + 1]] for n in range(8)),
+    )
+
 
 def solution(mesh):
     in_specs = (
@@ -455,4 +733,5 @@
         P("fsdp"),
         P("fsdp"),
     )
-    return jax.shard_map(local, mesh=mesh, in_specs=in_specs, out_specs=out_specs, check_vma=False)
+    run = by_heads if mesh.shape["fsdp"] == HQ else local
+    return jax.shard_map(run, mesh=mesh, in_specs=in_specs, out_specs=out_specs, check_vma=False)

time: 2420 us -> 1410 us (0.58)
  waiting for transfers between devices: 1770 us -> 841 us
  matrix products: 222 us -> 129 us
  local copies, waits for them, and re-layouts: 34.7 us -> 120 us
  blocking collectives: 240 us -> 207 us
  other arithmetic: 93.3 us -> 66.7 us
    all_gather x19 -> x10, waiting for transfers between devices: 1370 us -> 331 us  [the longest x4 169 us: gather_tokens(): return lax.all_gather(part, 'fsdp', axis=0, tiled=True)]
    reduce_scatter x1 -> x10, waiting for transfers between devices: 20.9 us -> 302 us  [the longest x4 135 us: scatter_tokens(): lax.psum_scatter(partial.astype(jnp.bfloat16), 'fsdp', scatter_dimension=...]
    psum x2, waiting for transfers between devices: 273 us -> 114 us  [the longest x1 114 us: row_sum(): return lax.psum(partial.astype(jnp.bfloat16), 'ctx').astype(jnp.float32)]
    all_gather x10 -> x3, blocking collectives: 182 us -> 45.9 us  [the longest x2 37.6 us: by_heads(): lax.all_gather(w.astype(bfloat), 'fsdp', axis=0, tiled=True)]
    all_to_all x0 -> x2, blocking collectives: none -> 95.8 us  [to_columns(): lax.all_to_all(mine, 'fsdp', split_axis=1, concat_axis=0, tiled=False)]
    unnamed x255 -> x291, local copies, waits for them, and re-layouts: 18.4 us -> 57.1 us
    dot_general x11 -> x16, matrix products: 75.4 us -> 38.5 us  [matmul(): return jnp.dot(left_mat, right_mat, preferred_element_type=jnp.float32)]
    dot_general x11 -> x16, matrix products: 78.4 us -> 47.1 us  [matmul_nt(): lax.dot_general(left_mat, right_mat, (((1,), (1,)), ((), ())), preferred_...]
  transfers between devices with their start and end apart: 31 -> 26, of which waited for: 21 -> 20; matrix products, arithmetic and copies ran while one was open for 9% -> 11% of each run, Pallas kernels for 0% -> 0%
where the time goes in v1:
time: 1410 us; the launch traced here: 1400 us
  waiting for transfers between devices  841 us (60%)
  blocking collectives  207 us (15%)
  matrix products  129 us (9%)
  local copies, waits for them, and re-layouts  120 us (9%)
  other arithmetic  66.7 us (5%)
  starting transfers between devices  17.3 us (1%)
  between operations  17.2 us (1%)
    all_gather x4, waiting for transfers between devices, gather_tokens(): return lax.all_gather(part, 'fsdp', axis=0, tiled=True)  169 us
    reduce_scatter x4, waiting for transfers between devices, scatter_tokens(): lax.psum_scatter(partial.astype(jnp.bfloat16), 'fsdp', scatter_dimension=...  135 us
    reduce_scatter x2, waiting for transfers between devices, to_rows(): summed = lax.psum_scatter(parts, 'ctx', scatter_dimension=1, tiled=True)  123 us
    psum x1, waiting for transfers between devices, row_sum(): return lax.psum(partial.astype(jnp.bfloat16), 'ctx').astype(jnp.float32)  114 us
    all_to_all x2, blocking collectives, to_columns(): lax.all_to_all(mine, 'fsdp', split_axis=1, concat_axis=0, tiled=False)  95.8 us
    all_gather x2, waiting for transfers between devices, gather_rows(): return lax.all_gather(part, 'ctx', axis=0, tiled=True).astype(jnp.float32)  74.3 us
    unnamed x291, local copies, waits for them, and re-layouts  57.1 us
    all_to_all x2, waiting for transfers between devices, to_rows(): lax.all_to_all(summed, 'fsdp', split_axis=0, concat_axis=1, tiled=False)  48.1 us
  transfers between devices with their start and end apart: 26, of which 20 were waited for; matrix products, arithmetic and copies ran while one was open for 11% of the time, Pallas kernels for 0%

profile of v1, /device:TPU:0, one launch (start us, length us, event | category | flops | bytes accessed | tf_op | source)
XLA Modules:
  0.0 1398.2 jit_solution(5142673943209958447)
XLA Ops:
  12.8 27.2 %all_to_all.60 = bf16[1,64,8,768]{3,1,0,2:T(8,128)(2,1)S(1)} all-to-all(bf16[1,64,8,768]{3,1,0,2:T(8,128)(2,1)S(1)} %copy.149), channel_id=1, replica_groups=mesh['ctx'=4,'fsdp'=8] {'fsdp'}, dimensions={2} | all-to-all | bytes 1572864 | tf_op jit(solution)/shard_map/all_to_all | solution.py:411
  43.2 27.2 %all-reduce.6 = f32[12800]{0:T(1024)S(1)} all-reduce(f32[12800]{0:T(1024)S(1)} %dynamic-update-slice.24), channel_id=2, replica_groups=mesh['ctx'=4,'fsdp'=8] {'fsdp'}, use_global_device_ids=true, to_apply=%add.6 | all-reduce | flops 12800 | bytes 102400
  88.6 45.2 %all-gather.16.cloned.1.call-done = bf16[1024,2048]{1,0:T(8,128)(2,1)} async-done(((bf16[128,2048]{1,0:T(8,128)(2,1)}), bf16[1024,2048]{1,0:T(8,128)(2,1)}) %all-gather.16.cloned.1.call-update) | async-done | bytes 4194320 | tf_op jit(solution)/shard_map/all_gather | solution.py:434
  150.0 20.9 %collective-permute-done = bf16[2,1024,256]{1,2,0:T(8,128)(2,1)} collective-permute-done((bf16[2,1024,256]{1,2,0:T(8,128)(2,1)S(1)}, bf16[2,1024,256]{1,2,0:T(8,128)(2,1)}, u32[]{:S(2)}, u32[]{:S(2)}) %collective-permute-start) | collective-permute-done | bytes 1048608 | tf_op jit(solution)/shard_map/ppermute | solution.py:24
  209.2 68.6 %all_to_all.61 = bf16[1,64,8,2048]{3,1,0,2:T(8,128)(2,1)S(1)} all-to-all(bf16[1,64,8,2048]{3,1,0,2:T(8,128)(2,1)} %copy.154), channel_id=1, replica_groups=mesh['ctx'=4,'fsdp'=8] {'fsdp'}, dimensions={2} | all-to-all | bytes 4194304 | tf_op jit(solution)/shard_map/all_to_all | solution.py:411
  281.2 14.2 %all_gather.50 = bf16[2048,64]{0,1:T(8,128)(2,1)S(1)} all-gather(bf16[256,64]{0,1:T(8,128)(2,1)S(1)} %convert_element_type.247), channel_id=1, replica_groups=mesh['ctx'=4,'fsdp'=8] {'fsdp'}, dimensions={0}, use_global_device_ids=true | all-gather | bytes 294912 | tf_op jit(solution)/shard_map/all_gather | solution.py:519
  295.4 23.4 %all_gather.51 = bf16[64,2048]{1,0:T(8,128)(2,1)S(1)} all-gather(bf16[8,2048]{1,0:T(8,128)(2,1)S(1)} %convert_element_type.249), channel_id=1, replica_groups=mesh['ctx'=4,'fsdp'=8] {'fsdp'}, dimensions={0}, use_global_device_ids=true | all-gather | bytes 294912 | tf_op jit(solution)/shard_map/all_gather | solution.py:519
  324.8 41.9 %all-gather.32.cloned.1.call-done = bf16[8,1,256,1,2048]{4,0,3,1,2:T(8,128)(2,1)} async-done(((bf16[8,1,64,1,2048]{4,0,3,1,2:T(8,128)(2,1)}), bf16[8,1,256,1,2048]{4,0,3,1,2:T(8,128)(2,1)}) %all-gather.32.cloned.1.call-update) | async-done | bytes 8388624 | tf_op jit(solution)/shard_map/all_gather | solution.py:412
  366.7 11.4 copy.156
  378.1 37.8 %all-gather.18.cloned.1.call-done = bf16[1024,2048]{1,0:T(8,128)(2,1)} async-done(((bf16[128,2048]{1,0:T(8,128)(2,1)}), bf16[1024,2048]{1,0:T(8,128)(2,1)}) %all-gather.18.cloned.1.call-update) | async-done | bytes 4194320 | tf_op jit(solution)/shard_map/all_gather | solution.py:434
  415.9 12.5 fusion.198
  447.5 45.4 %reduce-scatter.13.cloned.1.call-done = bf16[128,2048]{1,0:T(8,128)(2,1)} async-done(((bf16[1024,2048]{1,0:T(8,128)(2,1)}), bf16[128,2048]{1,0:T(8,128)(2,1)}) %reduce-scatter.13.cloned.1.call-update) | async-done | bytes 524304 | tf_op jit(solution)/shard_map/reduce_scatter | solution.py:428
  495.5 19.8 %all-gather.20.cloned.1.call-done = bf16[2048,256]{1,0:T(8,128)(2,1)} async-done(((bf16[256,256]{1,0:T(8,128)(2,1)}), bf16[2048,256]{1,0:T(8,128)(2,1)}) %all-gather.20.cloned.1.call-update) | async-done | bytes 1048592 | tf_op jit(solution)/shard_map/all_gather | solution.py:519
  516.9 22.4 %all-gather.22.cloned.1.call-done = bf16[256,2048]{1,0:T(8,128)(2,1)} async-done(((bf16[32,2048]{1,0:T(8,128)(2,1)}), bf16[256,2048]{1,0:T(8,128)(2,1)}) %all-gather.22.cloned.1.call-update) | async-done | bytes 1048592 | tf_op jit(solution)/shard_map/all_gather | solution.py:519
  548.2 46.9 %all-gather.24.cloned.1.call-done = bf16[1024,2048]{1,0:T(8,128)(2,1)} async-done(((bf16[128,2048]{1,0:T(8,128)(2,1)}), bf16[1024,2048]{1,0:T(8,128)(2,1)}) %all-gather.24.cloned.1.call-update) | async-done | bytes 4194320 | tf_op jit(solution)/shard_map/all_gather | solution.py:434
  595.1 12.7 fusion.8
  609.8 12.6 convolution_convert_fusion.1
  623.7 47.6 %reduce-scatter.15.cloned.1.call-done = bf16[128,2048]{1,0:T(8,128)(2,1)} async-done(((bf16[1024,2048]{1,0:T(8,128)(2,1)}), bf16[128,2048]{1,0:T(8,128)(2,1)}) %reduce-scatter.15.cloned.1.call-update) | async-done | bytes 524304 | tf_op jit(solution)/shard_map/reduce_scatter | solution.py:428
  685.1 38.7 %all-gather.26.cloned.1.call-done = bf16[1024,2048]{1,0:T(8,128)(2,1)} async-done(((bf16[128,2048]{1,0:T(8,128)(2,1)}), bf16[1024,2048]{1,0:T(8,128)(2,1)}) %all-gather.26.cloned.1.call-update) | async-done | bytes 4194320 | tf_op jit(solution)/shard_map/all_gather | solution.py:434
  745.1 24.1 %collective-permute-done.1 = bf16[2,1024,256]{1,2,0:T(8,128)(2,1)S(1)} collective-permute-done((bf16[2,1024,256]{1,2,0:T(8,128)(2,1)S(1)}, bf16[2,1024,256]{1,2,0:T(8,128)(2,1)S(1)}, u32[]{:S(2)}, u32[]{:S(2)}) %collective-permute-start.1) | collective-permute-done | bytes 1048608 | tf_op jit(solution)/shard_map/ppermute | solution.py:24
  780.5 14.1 %convolution_convert_fusion = bf16[2048,2048]{1,0:T(8,128)(2,1)} fusion(bf16[1024,2048]{1,0:T(8,128)(2,1)} %all-gather.18.cloned.1.call-done, bf16[1024,1024]{1,0:T(8,128)(2,1)} %copy-done.136, bf16[1024,1024]{1,0:T(8,128)(2,1)} %copy-done.135), kind=kOutput, calls=%fused_computation.5 | convolution fusion | flops 8602517504 | bytes 16777216 | tf_op jit(solution)/shard_map/dot_general | solution.py:32
  809.1 11.2 reduce-scatter.27.cloned.1.call-done
  820.4 32.8 %reduce-scatter.29.cloned.1.call-done = bf16[32,2048]{1,0:T(8,128)(2,1)} async-done(((bf16[256,2048]{1,0:T(8,128)(2,1)}), bf16[32,2048]{1,0:T(8,128)(2,1)}) %reduce-scatter.29.cloned.1.call-update) | async-done | bytes 131088 | tf_op jit(solution)/shard_map/reduce_scatter | solution.py:438
  860.2 38.0 %reduce-scatter.19.cloned.1.call-done = bf16[8,64,768]{2,1,0:T(8,128)(2,1)} async-done(((bf16[8,256,768]{2,1,0:T(8,128)(2,1)}), bf16[8,64,768]{2,1,0:T(8,128)(2,1)}) %reduce-scatter.19.cloned.1.call-update) | async-done | bytes 786448 | tf_op jit(solution)/shard_map/reduce_scatter | solution.py:418
  902.8 85.3 %reduce-scatter.25.cloned.1.call-done = bf16[8,64,2048]{2,1,0:T(8,128)(2,1)} async-done(((bf16[8,256,2048]{2,1,0:T(8,128)(2,1)}), bf16[8,64,2048]{2,1,0:T(8,128)(2,1)}) %reduce-scatter.25.cloned.1.call-update) | async-done | bytes 2097168 | tf_op jit(solution)/shard_map/reduce_scatter | solution.py:418
  993.8 48.1 %all-to-all-done.3 = bf16[8,64,1,2048]{3,1,2,0:T(8,128)(2,1)} async-done(((bf16[8,64,1,2048]{3,1,2,0:T(8,128)(2,1)}), bf16[8,64,1,2048]{3,1,2,0:T(8,128)(2,1)}, u32[]{:S(2)}, u32[]{:S(2)}) %all-to-all-start.3) | async-done | bytes 2097184 | tf_op jit(solution)/shard_map/all_to_all | solution.py:419
  1050.2 113.9 %all-reduce.14.cloned.1.call-done = (bf16[256,2048]{1,0:T(8,128)(2,1)}, bf16[1024,2048]{1,0:T(8,128)(2,1)}, bf16[256,256]{1,0:T(8,128)(2,1)}, bf16[32,2048]{1,0:T(8,128)(2,1)}) async-done(((bf16[256,2048]{1,0:T(8,128)(2,1)}, bf16[1024,2048]{1,0:T(8,128)(2,1)}, bf16[256,256]{1,0:T(8,128)(2,1)}, bf16[32,2048]{1,0:T(8,128)(2,1)}), (bf16[256,2048]{1,0:T(8,128)(2,1)}, bf16[1024,2048]{1,0:T(8,128)(2,1)}, ...) | async-done | bytes 5505040 | tf_op jit(solution)/shard_map/psum | solution.py:443
  1175.1 41.7 %reduce-scatter.17.cloned.1.call-done = bf16[128,2048]{1,0:T(8,128)(2,1)} async-done(((bf16[1024,2048]{1,0:T(8,128)(2,1)}), bf16[128,2048]{1,0:T(8,128)(2,1)}) %reduce-scatter.17.cloned.1.call-update) | async-done | bytes 524304 | tf_op jit(solution)/shard_map/reduce_scatter | solution.py:428
  1218.7 38.5 %psum.55 = f32[8,1600]{1,0:T(8,128)S(1)} all-reduce(f32[8,1600]{1,0:T(8,128)S(1)} %concatenate.81), channel_id=1, replica_groups=mesh['ctx'=4,'fsdp'=8] {'ctx','fsdp'}, use_global_device_ids=true, to_apply=%region_62.63 | all-reduce | flops 12800 | bytes 102400 | tf_op jit(solution)/shard_map/psum | solution.py:664
  1263.9 74.3 %all-gather.34.cloned.1.call-done = bf16[1,256,8,1,2048]{4,2,3,0,1:T(8,128)(2,1)} async-done(((bf16[1,64,8,1,2048]{4,2,3,0,1:T(8,128)(2,1)}), bf16[1,256,8,1,2048]{4,2,3,0,1:T(8,128)(2,1)}) %all-gather.34.cloned.1.call-update) | async-done | bytes 8388624 | tf_op jit(solution)/shard_map/all_gather | solution.py:424
  1338.2 12.8 copy.167
  1361.7 11.7 fusion.189
  (515 shorter events, 258.0 us)
Async XLA Ops:
  7.2 77.3 %all-gather.30.cloned.1.call-start = ((), (), s32[]{:S(2)}) async-start(), calls=%async_computation.31 | async-start | bytes 3932160 | tf_op jit(solution)/shard_map/all_gather | solution.py:412
  41.4 92.4 %all-gather.16.cloned.1.call-start = ((), (), s32[]{:S(2)}) async-start(), calls=%async_computation.14 | async-start | bytes 4718592 | tf_op jit(solution)/shard_map/all_gather | solution.py:434
  70.6 250.9 %copy-start.44 = (f32[1,2,8,128]{3,1,2,0:T(2,128)}, f32[1,2,8,128]{3,1,2,0:T(2,128)S(1)}, u32[]{:S(2)}) copy-start(f32[1,2,8,128]{3,1,2,0:T(2,128)S(1)} %copy.180) | copy-start | bytes 24580
  70.8 250.7 %copy-start.85 = (f32[128]{0:T(128)}, f32[128]{0:T(128)S(1)}, u32[]{:S(2)}) copy-start(f32[128]{0:T(128)S(1)} %fusion.158) | copy-start | bytes 1540
  71.8 247.7 %reduce-scatter.11.cloned.1.call-start = ((), (), s32[]{:S(2)}) async-start(), calls=%async_computation.15 | async-start | bytes 4718592 | tf_op jit(solution)/shard_map/reduce_scatter | solution.py:428
  72.0 69.6 %copy-start.81 = (f32[256]{0:T(256)}, f32[256]{0:T(256)S(1)}, u32[]{:S(2)}) copy-start(f32[256]{0:T(256)S(1)} %mul.723) | copy-start | bytes 3076
  72.1 69.6 %copy-start.83 = (f32[256]{0:T(256)}, f32[256]{0:T(256)S(1)}, u32[]{:S(2)}) copy-start(f32[256]{0:T(256)S(1)} %mul.738) | copy-start | bytes 3076
  80.5 61.8 %copy-start.70 = (f32[8,1,128]{2,1,0:T(1,128)}, f32[8,1,128]{2,1,0:T(1,128)S(1)}, u32[]{:S(2)}) copy-start(f32[8,1,128]{2,1,0:T(1,128)S(1)} %convert_element_type.298) | copy-start | bytes 12292
  144.8 26.2 %collective-permute-start = (bf16[2,1024,256]{1,2,0:T(8,128)(2,1)S(1)}, bf16[2,1024,256]{1,2,0:T(8,128)(2,1)}, u32[]{:S(2)}, u32[]{:S(2)}) collective-permute-start(bf16[2,1024,256]{1,2,0:T(8,128)(2,1)S(1)} %pad_maximum_fusion.4), channel_id=1, source_target_pairs={{0,8},{8,16},{16,24},{1,9},{9,17},{17,25},{2,10},{10,18},{18,26},{... | collective-permute-start | bytes 3145736 | tf_op jit(solution)/shard_map/ppermute | solution.py:24
  184.3 182.4 %all-gather.32.cloned.1.call-start = ((), (), s32[]{:S(2)}) async-start(), calls=%async_computation.32 | async-start | bytes 10485760 | tf_op jit(solution)/shard_map/all_gather | solution.py:412
  280.3 135.6 %all-gather.18.cloned.1.call-start = ((), (), s32[]{:S(2)}) async-start(), calls=%async_computation.16 | async-start | bytes 4718592 | tf_op jit(solution)/shard_map/all_gather | solution.py:434
  324.7 168.2 %reduce-scatter.13.cloned.1.call-start = ((), (), s32[]{:S(2)}) async-start(), calls=%async_computation.17 | async-start | bytes 4718592 | tf_op jit(solution)/shard_map/reduce_scatter | solution.py:428
  444.1 71.3 %all-gather.20.cloned.1.call-start = ((), (), s32[]{:S(2)}) async-start(), calls=%async_computation.18 | async-start | bytes 1179648 | tf_op jit(solution)/shard_map/all_gather | solution.py:519
  445.7 93.6 %all-gather.22.cloned.1.call-start = ((), (), s32[]{:S(2)}) async-start(), calls=%async_computation.19 | async-start | bytes 1179648 | tf_op jit(solution)/shard_map/all_gather | solution.py:519
  446.4 148.7 %all-gather.24.cloned.1.call-start = ((), (), s32[]{:S(2)}) async-start(), calls=%async_computation.20 | async-start | bytes 4718592 | tf_op jit(solution)/shard_map/all_gather | solution.py:434
  548.2 123.1 %reduce-scatter.15.cloned.1.call-start = ((), (), s32[]{:S(2)}) async-start(), calls=%async_computation.21 | async-start | bytes 4718592 | tf_op jit(solution)/shard_map/reduce_scatter | solution.py:428
  622.4 101.3 %all-gather.26.cloned.1.call-start = ((), (), s32[]{:S(2)}) async-start(), calls=%async_computation.22 | async-start | bytes 4718592 | tf_op jit(solution)/shard_map/all_gather | solution.py:434
  678.4 126.2 %reduce-scatter.21.cloned.1.call-start = ((), (), s32[]{:S(2)}) async-start(), calls=%async_computation.26 | async-start | bytes 294912 | tf_op jit(solution)/shard_map/reduce_scatter | solution.py:438
  680.9 123.7 %reduce-scatter.23.cloned.1.call-start = ((), (), s32[]{:S(2)}) async-start(), calls=%async_computation.27 | async-start | bytes 294912 | tf_op jit(solution)/shard_map/reduce_scatter | solution.py:438
  681.9 138.5 %reduce-scatter.27.cloned.1.call-start = ((), (), s32[]{:S(2)}) async-start(), calls=%async_computation.29 | async-start | bytes 1179648 | tf_op jit(solution)/shard_map/reduce_scatter | solution.py:438
  683.4 169.7 %reduce-scatter.29.cloned.1.call-start = ((), (), s32[]{:S(2)}) async-start(), calls=%async_computation.30 | async-start | bytes 1179648 | tf_op jit(solution)/shard_map/reduce_scatter | solution.py:438
  685.0 213.2 %reduce-scatter.19.cloned.1.call-start = ((), (), s32[]{:S(2)}) async-start(), calls=%async_computation.24 | async-start | bytes 3932160 | tf_op jit(solution)/shard_map/reduce_scatter | solution.py:418
  741.9 27.2 %collective-permute-start.1 = (bf16[2,1024,256]{1,2,0:T(8,128)(2,1)S(1)}, bf16[2,1024,256]{1,2,0:T(8,128)(2,1)S(1)}, u32[]{:S(2)}, u32[]{:S(2)}) collective-permute-start(bf16[2,1024,256]{1,2,0:T(8,128)(2,1)S(1)} %pad_maximum_fusion.6), channel_id=1, source_target_pairs={{8,0},{16,8},{24,16},{9,1},{17,9},{25,17},{10,2},{18,10},{26,18},{... | collective-permute-start | bytes 3145736 | tf_op jit(solution)/shard_map/ppermute | solution.py:24
  780.5 207.7 %reduce-scatter.25.cloned.1.call-start = ((), (), s32[]{:S(2)}) async-start(), calls=%async_computation.28 | async-start | bytes 10485760 | tf_op jit(solution)/shard_map/reduce_scatter | solution.py:418
  794.7 252.6 %all-reduce.12.cloned.1.call-start = ((), (), s32[]{:S(2)}) async-start(), calls=%async_computation.34 | async-start | bytes 131072 | tf_op jit(solution)/shard_map/psum | solution.py:439
  804.6 359.5 %all-reduce.14.cloned.1.call-start = ((), (), s32[]{:S(2)}) async-start(), calls=%async_computation.35 | async-start | bytes 11010048 | tf_op jit(solution)/shard_map/psum | solution.py:443
  853.1 363.7 %reduce-scatter.17.cloned.1.call-start = ((), (), s32[]{:S(2)}) async-start(), calls=%async_computation.23 | async-start | bytes 4718592 | tf_op jit(solution)/shard_map/reduce_scatter | solution.py:428
  898.2 89.9 %all-to-all-start.2 = ((bf16[8,64,1,768]{3,1,2,0:T(8,128)(2,1)}), bf16[8,64,1,768]{3,1,2,0:T(8,128)(2,1)S(1)}, u32[]{:S(2)}, u32[]{:S(2)}) async-start(bf16[8,64,1,768]{3,1,2,0:T(8,128)(2,1)} %bitcast.216), calls=%async_computation.7 | async-start | bytes 1572864 | tf_op jit(solution)/shard_map/all_to_all | solution.py:419
  988.1 53.8 %all-to-all-start.3 = ((bf16[8,64,1,2048]{3,1,2,0:T(8,128)(2,1)}), bf16[8,64,1,2048]{3,1,2,0:T(8,128)(2,1)}, u32[]{:S(2)}, u32[]{:S(2)}) async-start(bf16[8,64,1,2048]{3,1,2,0:T(8,128)(2,1)} %bitcast.212), calls=%async_computation.11 | async-start | bytes 4194304 | tf_op jit(solution)/shard_map/all_to_all | solution.py:419
  992.7 267.0 %all-gather.28.cloned.1.call-start = ((), (), s32[]{:S(2)}) async-start(), calls=%async_computation.25 | async-start | bytes 1966080 | tf_op jit(solution)/shard_map/all_gather | solution.py:424
  993.7 344.4 %all-gather.34.cloned.1.call-start = ((), (), s32[]{:S(2)}) async-start(), calls=%async_computation.33 | async-start | bytes 10485760 | tf_op jit(solution)/shard_map/all_gather | solution.py:424
  1174.4 84.0 %copy-start.122 = (f32[128]{0:T(128)S(1)}, f32[128]{0:T(128)}, u32[]{:S(2)}) copy-start(f32[128]{0:T(128)} %copy-done.121) | copy-start | bytes 1540
  (131 other events, 1445.5 us)
Sparse Core Ops, SparseCore 0:
  41.5 42.9 all-gather.29
  86.7 47.1 all-gather.15
  184.4 64.4 reduce-scatter.10
  280.4 86.2 all-gather.31
  368.7 47.1 all-gather.17
  444.2 48.7 reduce-scatter.12
  495.1 20.2 all-gather.19
  517.6 21.7 all-gather.21
  548.3 46.7 all-gather.23
  622.5 48.7 reduce-scatter.14
  678.5 45.2 all-gather.25
  726.4 29.1 reduce-scatter.20
  758.5 28.5 reduce-scatter.22
  789.8 30.5 reduce-scatter.26
  822.5 30.5 reduce-scatter.28
  856.0 42.1 reduce-scatter.18
  901.7 86.3 reduce-scatter.24
  991.1 41.5 all-reduce.11
  1037.6 126.4 all-reduce.13
  1166.8 50.0 reduce-scatter.16
  1219.3 29.3 all-gather.27
  1250.5 87.5 all-gather.33

commit v2 on v1

--- a/solution.py
+++ b/solution.py
@@ -4,6 +4,8 @@
 import jax
 import jax.numpy as jnp
 from jax import lax
+from jax.experimental import pallas as pl
+from jax.experimental.pallas import tpu as pltpu
 from jax.sharding import PartitionSpec as P
 
 HQ = 8
@@ -16,6 +18,9 @@
 NEGATIVE = -1e30
 ROPE_BASE = 10000.0
 HALF_ROOT = 1.0 / math.sqrt(2.0)
+GELU_ROOT = math.sqrt(2.0 / math.pi)
+GELU_CUBE = 0.044715
+KERNEL_VMEM = 56 << 20
 
 
 def passed_along(block, axis, distance):
@@ -403,6 +408,515 @@
         wide_part(sum_gple),
     )
 
+def remote(src, dst, send_sem, recv_sem, place):
+    return pltpu.make_async_remote_copy(
+        src_ref=src,
+        dst_ref=dst,
+        send_sem=send_sem,
+        recv_sem=recv_sem,
+        device_id={"fsdp": place},
+        device_id_type=pl.DeviceIdType.MESH,
+    )
+
+
+def dot_nn(left_mat, right_mat):
+    return jnp.dot(left_mat, right_mat, preferred_element_type=jnp.float32)
+
+
+def dot_nt(left_mat, right_mat):
+    return lax.dot_general(
+        left_mat, right_mat, (((1,), (1,)), ((), ())), preferred_element_type=jnp.float32
+    )
+
+
+PIECES = 4
+
+
+def line_scratch(chips, tok_count, width):
+    dma = pltpu.SemaphoreType.DMA
+    shard = (tok_count, width)
+    return [
+        pltpu.VMEM((chips, 2) + shard, jnp.bfloat16),
+        dma((chips, 2)),
+        dma((chips, 3)),
+        dma,
+        pltpu.VMEM((chips, 2) + shard, jnp.bfloat16),
+        pltpu.VMEM((chips,) + shard, jnp.bfloat16),
+        pltpu.VMEM((chips,) + shard, jnp.bfloat16),
+        pltpu.VMEM((chips,) + shard, jnp.bfloat16),
+        dma((chips,)),
+        dma((chips,)),
+        dma((chips, PIECES)),
+        dma((chips, PIECES)),
+        dma((chips, PIECES)),
+    ]
+
+
+LINE_REFS = 13
+
+
+class Line:
+    def __init__(self, chips, refs):
+        (
+            self.slots,
+            self.slot_recv,
+            self.slot_send,
+            self.own_sem,
+            self.parts,
+            self.from_core,
+            self.from_left,
+            self.from_right,
+            self.core_send,
+            self.core_recv,
+            self.flow_send,
+            self.left_recv,
+            self.right_recv,
+        ) = refs
+        self.chips = chips
+        me = lax.axis_index("fsdp")
+        self.chip = me // 2
+        self.core = me % 2
+        self.tok = self.slots.shape[2]
+        self.piece = self.tok // PIECES
+
+    def place(self, chip, core):
+        return chip * 2 + core
+
+    def order(self, step):
+        picked = 0
+        for chip in range(self.chips):
+            near = sorted(range(self.chips), key=lambda other: (abs(other - chip), other))
+            picked = picked + jnp.where(self.chip == chip, near[step], 0)
+        return picked
+
+    def barrier(self):
+        sem = pltpu.get_barrier_semaphore()
+
+        def greet(place):
+            pl.semaphore_signal(
+                sem, inc=1, device_id={"fsdp": place}, device_id_type=pl.DeviceIdType.MESH
+            )
+
+        greet(self.place(self.chip, 1 - self.core))
+
+        @pl.when(self.chip > 0)
+        def _():
+            greet(self.place(self.chip - 1, self.core))
+
+        @pl.when(self.chip < self.chips - 1)
+        def _():
+            greet(self.place(self.chip + 1, self.core))
+
+        ends = jnp.where(self.chip == 0, 1, 0) + jnp.where(self.chip == self.chips - 1, 1, 0)
+        pl.semaphore_wait(sem, 3 - ends)
+
+    def slot_copy(self, src, chip, way):
+        place = (
+            self.place(self.chip + 1, self.core),
+            self.place(self.chip - 1, self.core),
+            self.place(self.chip, 1 - self.core),
+        )[way]
+        return remote(
+            src,
+            self.slots.at[chip, self.core],
+            self.slot_send.at[chip, way],
+            self.slot_recv.at[chip, self.core],
+            place,
+        )
+
+    def own_copy(self, own_ref):
+        return pltpu.make_async_copy(own_ref, self.slots.at[self.chip, self.core], self.own_sem)
+
+    def gather_begin(self, own_ref):
+        @pl.when(self.chip < self.chips - 1)
+        def _():
+            self.slot_copy(own_ref, self.chip, 0).start()
+
+        @pl.when(self.chip > 0)
+        def _():
+            self.slot_copy(own_ref, self.chip, 1).start()
+
+        self.slot_copy(own_ref, self.chip, 2).start()
+        self.own_copy(own_ref).start()
+
+    def gather_step(self, distance):
+        for chip, there, way, onward in (
+            (self.chip - distance, self.chip >= distance, 0, self.chip < self.chips - 1),
+            (self.chip + distance, self.chip + distance < self.chips, 1, self.chip > 0),
+        ):
+
+            @pl.when(there)
+            def _(chip=chip, way=way, onward=onward):
+                src = self.slots.at[chip, self.core]
+                self.slot_copy(src, chip, way).wait_recv()
+
+                @pl.when(onward)
+                def _():
+                    self.slot_copy(src, chip, way).start()
+
+                self.slot_copy(src, chip, 2).start()
+
+    def gather_other(self, chip):
+        dst = self.slots.at[chip, 1 - self.core]
+        remote(
+            dst,
+            dst,
+            self.slot_send.at[chip, 2],
+            self.slot_recv.at[chip, 1 - self.core],
+            self.place(self.chip, 1 - self.core),
+        ).wait_recv()
+
+    def gather_end(self):
+        for chip in range(self.chips):
+            src = self.slots.at[chip, self.core]
+
+            @pl.when((self.chip >= chip) & (self.chip < self.chips - 1))
+            def _(src=src, chip=chip):
+                self.slot_copy(src, chip, 0).wait_send()
+
+            @pl.when((self.chip <= chip) & (self.chip > 0))
+            def _(src=src, chip=chip):
+                self.slot_copy(src, chip, 1).wait_send()
+
+            self.slot_copy(src, chip, 2).wait_send()
+
+    def core_copy(self, chip):
+        return remote(
+            self.parts.at[chip, 1 - self.core],
+            self.from_core.at[chip],
+            self.core_send.at[chip],
+            self.core_recv.at[chip],
+            self.place(self.chip, 1 - self.core),
+        )
+
+    def flow_copy(self, chip, piece, right):
+        rows = pl.ds(piece * self.piece, self.piece)
+        return remote(
+            self.parts.at[chip, self.core, rows],
+            (self.from_left if right else self.from_right).at[chip, rows],
+            self.flow_send.at[chip, piece],
+            (self.left_recv if right else self.right_recv).at[chip, piece],
+            self.place(self.chip + (1 if right else -1), self.core),
+        )
+
+    def flow(self, chip, right, incoming):
+        self.core_copy(chip).wait_recv()
+
+        @pl.loop(0, PIECES)
+        def _(piece):
+            rows = pl.ds(pl.multiple_of(piece * self.piece, self.piece), self.piece)
+            total = self.parts[chip, self.core, rows].astype(jnp.float32)
+            total = total + self.from_core[chip, rows].astype(jnp.float32)
+            if incoming:
+                self.flow_copy(chip, piece, right).wait_recv()
+                source = self.from_left if right else self.from_right
+                total = total + source[chip, rows].astype(jnp.float32)
+            self.parts[chip, self.core, rows] = total.astype(jnp.bfloat16)
+            self.flow_copy(chip, piece, right).start()
+
+    def scatter_first(self, chip):
+        @pl.when((self.chip == 0) & (chip > 0))
+        def _():
+            self.flow(chip, True, False)
+
+        @pl.when((self.chip == self.chips - 1) & (chip < self.chips - 1))
+        def _():
+            self.flow(chip, False, False)
+
+    def scatter_rest(self, result_ref):
+        for rank in range(3, 2 * self.chips - 2):
+            right = rank - self.chip
+
+            @pl.when((self.chip > 0) & (right > self.chip) & (right < self.chips))
+            def _(right=right):
+                self.flow(right, True, True)
+
+            left = 2 * (self.chips - 1) - self.chip - rank
+
+            @pl.when((self.chip < self.chips - 1) & (left < self.chip) & (left >= 0))
+            def _(left=left):
+                self.flow(left, False, True)
+
+        own = self.chip
+        self.core_copy(own).wait_recv()
+
+        @pl.loop(0, PIECES)
+        def _(piece):
+            rows = pl.ds(pl.multiple_of(piece * self.piece, self.piece), self.piece)
+            total = self.parts[own, self.core, rows].astype(jnp.float32)
+            total = total + self.from_core[own, rows].astype(jnp.float32)
+            result_ref[rows] = total
+
+        @pl.when(own > 0)
+        def _():
+            @pl.loop(0, PIECES)
+            def _(piece):
+                rows = pl.ds(pl.multiple_of(piece * self.piece, self.piece), self.piece)
+                self.flow_copy(own, piece, True).wait_recv()
+                result_ref[rows] += self.from_left[own, rows].astype(jnp.float32)
+
+        @pl.when(own < self.chips - 1)
+        def _():
+            @pl.loop(0, PIECES)
+            def _(piece):
+                rows = pl.ds(pl.multiple_of(piece * self.piece, self.piece), self.piece)
+                self.flow_copy(own, piece, False).wait_recv()
+                result_ref[rows] += self.from_right[own, rows].astype(jnp.float32)
+
+        for chip in range(self.chips):
+            self.core_copy(chip).wait_send()
+
+            @pl.when(self.chip != chip)
+            def _(chip=chip):
+                for piece in range(PIECES):
+                    self.flow_copy(chip, piece, True).wait_send()
+
+
+def ffn_forward_kernel(
+    chips,
+    own_ref,
+    gateup_hbm,
+    down_hbm,
+    result_ref,
+    all_hbm,
+    hidden_hbm,
+    act_hbm,
+    slope_hbm,
+    *scratch,
+):
+    line = Line(chips, scratch[:LINE_REFS])
+    gateup, down, hidden, act, slope, load_sems, store_sems = scratch[LINE_REFS:]
+    ff_part = down.shape[0]
+    width = down.shape[1]
+    pair = 2 * line.tok
+    load_gateup = pltpu.make_async_copy(gateup_hbm, gateup, load_sems.at[0])
+    load_down = pltpu.make_async_copy(down_hbm, down, load_sems.at[1])
+    load_gateup.start()
+    load_down.start()
+    line.barrier()
+    line.gather_begin(own_ref)
+    line.own_copy(own_ref).wait()
+
+    def stores(chip):
+        rows = pl.ds(pl.multiple_of(chip * pair, pair), pair)
+        return [
+            pltpu.make_async_copy(line.slots.at[chip], all_hbm.at[chip], store_sems.at[chip, 0]),
+            pltpu.make_async_copy(hidden.at[rows], hidden_hbm.at[rows], store_sems.at[chip, 1]),
+            pltpu.make_async_copy(act.at[rows], act_hbm.at[rows], store_sems.at[chip, 2]),
+            pltpu.make_async_copy(slope.at[rows], slope_hbm.at[rows], store_sems.at[chip, 3]),
+        ]
+
+    tile = 256
+    for step in range(chips):
+        if step > 0:
+            line.gather_step(step)
+        chip = line.order(step)
+        line.gather_other(chip)
+        if step == 0:
+            load_gateup.wait()
+            load_down.wait()
+        rows = pl.ds(pl.multiple_of(chip * pair, pair), pair)
+
+        @pl.loop(0, ff_part // tile)
+        def _(at, chip=chip, rows=rows):
+            inputs = line.slots[chip].reshape(pair, width)
+            gate_cols = pl.ds(pl.multiple_of(at * tile, tile), tile)
+            up_cols = pl.ds(pl.multiple_of(ff_part + at * tile, tile), tile)
+            gate = dot_nn(inputs, gateup[:, gate_cols])
+            up = dot_nn(inputs, gateup[:, up_cols])
+            square = gate * gate
+            bent = jnp.tanh(GELU_ROOT * gate * (1.0 + GELU_CUBE * square))
+            half = 0.5 + 0.5 * bent
+            activated = gate * half
+            rise = half + 0.5 * gate * (1.0 - bent * bent) * (
+                GELU_ROOT * (1.0 + 3.0 * GELU_CUBE * square)
+            )
+            hidden[rows, gate_cols] = (activated * up).astype(jnp.bfloat16)
+            act[rows, gate_cols] = activated.astype(jnp.bfloat16)
+            slope[rows, gate_cols] = (rise * up).astype(jnp.bfloat16)
+
+        for copy in stores(chip):
+            copy.start()
+
+        wide = 512
+
+        @pl.loop(0, width // wide)
+        def _(at, chip=chip, rows=rows):
+            cols = pl.ds(pl.multiple_of(at * wide, wide), wide)
+            sums = dot_nn(hidden[rows, :], down[:, cols]).astype(jnp.bfloat16)
+            line.parts[chip, :, :, cols] = sums.reshape(2, line.tok, wide)
+
+        line.core_copy(chip).start()
+        if step > 0:
+            line.scatter_first(line.order(step - 1))
+    line.scatter_first(line.order(chips - 1))
+    line.scatter_rest(result_ref)
+    line.gather_end()
+    for chip in range(chips):
+        for copy in stores(chip):
+            copy.wait()
+
+
+def ffn_forward(own, gateup, down, chips):
+    tok_count, width = own.shape
+    ff_part = down.shape[0]
+    block = 2 * chips * tok_count
+    bfloat = jnp.bfloat16
+    anywhere = pl.BlockSpec(memory_space=pl.ANY)
+    vmem = pl.BlockSpec(memory_space=pltpu.VMEM)
+    part = jax.ShapeDtypeStruct((block, ff_part), bfloat)
+    result, gathered, hidden, act, slope = pl.pallas_call(
+        functools.partial(ffn_forward_kernel, chips),
+        out_shape=[
+            jax.ShapeDtypeStruct((tok_count, width), jnp.float32),
+            jax.ShapeDtypeStruct((chips, 2, tok_count, width), bfloat),
+            part,
+            part,
+            part,
+        ],
+        in_specs=[vmem, anywhere, anywhere],
+        out_specs=[vmem, anywhere, anywhere, anywhere, anywhere],
+        scratch_shapes=line_scratch(chips, tok_count, width)
+        + [
+            pltpu.VMEM(gateup.shape, bfloat),
+            pltpu.VMEM(down.shape, bfloat),
+            pltpu.VMEM((block, ff_part), bfloat),
+            pltpu.VMEM((block, ff_part), bfloat),
+            pltpu.VMEM((block, ff_part), bfloat),
+            pltpu.SemaphoreType.DMA((2,)),
+            pltpu.SemaphoreType.DMA((chips, 4)),
+        ],
+        compiler_params=pltpu.CompilerParams(
+            collective_id=1, has_side_effects=True, vmem_limit_bytes=KERNEL_VMEM
+        ),
+        cost_estimate=pl.CostEstimate(
+            flops=6 * block * width * ff_part,
+            bytes_accessed=40 << 20,
+            transcendentals=block * ff_part,
+        ),
+        name="ffn_forward",
+    )(own, gateup, down)
+    return result, gathered.reshape(block, width), hidden, act, slope
+
+
+def ffn_backward_kernel(
+    chips,
+    own_ref,
+    gateup_hbm,
+    down_hbm,
+    act_hbm,
+    slope_hbm,
+    result_ref,
+    all_hbm,
+    grad_hbm,
+    *scratch,
+):
+    line = Line(chips, scratch[:LINE_REFS])
+    gateup, down, act, slope, grad, load_sems, store_sems = scratch[LINE_REFS:]
+    ff_part = down.shape[0]
+    width = down.shape[1]
+    pair = 2 * line.tok
+    loads = [
+        pltpu.make_async_copy(down_hbm, down, load_sems.at[0]),
+        pltpu.make_async_copy(act_hbm, act, load_sems.at[1]),
+        pltpu.make_async_copy(slope_hbm, slope, load_sems.at[2]),
+        pltpu.make_async_copy(gateup_hbm, gateup, load_sems.at[3]),
+    ]
+    for load in loads:
+        load.start()
+    line.barrier()
+    line.gather_begin(own_ref)
+    line.own_copy(own_ref).wait()
+
+    def stores(chip):
+        rows = pl.ds(pl.multiple_of(chip * pair, pair), pair)
+        return [
+            pltpu.make_async_copy(line.slots.at[chip], all_hbm.at[chip], store_sems.at[chip, 0]),
+            pltpu.make_async_copy(grad.at[rows], grad_hbm.at[rows], store_sems.at[chip, 1]),
+        ]
+
+    tile = 256
+    for step in range(chips):
+        if step > 0:
+            line.gather_step(step)
+        chip = line.order(step)
+        line.gather_other(chip)
+        if step == 0:
+            for load in loads:
+                load.wait()
+        rows = pl.ds(pl.multiple_of(chip * pair, pair), pair)
+
+        @pl.loop(0, ff_part // tile)
+        def _(at, chip=chip, rows=rows):
+            grads = line.slots[chip].reshape(pair, width)
+            gate_cols = pl.ds(pl.multiple_of(at * tile, tile), tile)
+            up_cols = pl.ds(pl.multiple_of(ff_part + at * tile, tile), tile)
+            grad_hidden = dot_nt(grads, down[gate_cols, :])
+            grad[rows, gate_cols] = (
+                grad_hidden * slope[rows, gate_cols].astype(jnp.float32)
+            ).astype(jnp.bfloat16)
+            grad[rows, up_cols] = (grad_hidden * act[rows, gate_cols].astype(jnp.float32)).astype(
+                jnp.bfloat16
+            )
+
+        for copy in stores(chip):
+            copy.start()
+
+        wide = 512
+
+        @pl.loop(0, width // wide)
+        def _(at, chip=chip, rows=rows):
+            cols = pl.ds(pl.multiple_of(at * wide, wide), wide)
+            sums = dot_nt(grad[rows, :], gateup[cols, :]).astype(jnp.bfloat16)
+            line.parts[chip, :, :, cols] = sums.reshape(2, line.tok, wide)
+
+        line.core_copy(chip).start()
+        if step > 0:
+            line.scatter_first(line.order(step - 1))
+    line.scatter_first(line.order(chips - 1))
+    line.scatter_rest(result_ref)
+    line.gather_end()
+    for chip in range(chips):
+        for copy in stores(chip):
+            copy.wait()
+
+
+def ffn_backward(own, gateup, down, act, slope, chips):
+    tok_count, width = own.shape
+    ff_part = down.shape[0]
+    block = 2 * chips * tok_count
+    bfloat = jnp.bfloat16
+    anywhere = pl.BlockSpec(memory_space=pl.ANY)
+    vmem = pl.BlockSpec(memory_space=pltpu.VMEM)
+    result, gathered, grad = pl.pallas_call(
+        functools.partial(ffn_backward_kernel, chips),
+        out_shape=[
+            jax.ShapeDtypeStruct((tok_count, width), jnp.float32),
+            jax.ShapeDtypeStruct((chips, 2, tok_count, width), bfloat),
+            jax.ShapeDtypeStruct((block, 2 * ff_part), bfloat),
+        ],
+        in_specs=[vmem] + [anywhere] * 4,
+        out_specs=[vmem, anywhere, anywhere],
+        scratch_shapes=line_scratch(chips, tok_count, width)
+        + [
+            pltpu.VMEM(gateup.shape, bfloat),
+            pltpu.VMEM(down.shape, bfloat),
+            pltpu.VMEM((block, ff_part), bfloat),
+            pltpu.VMEM((block, ff_part), bfloat),
+            pltpu.VMEM((block, 2 * ff_part), bfloat),
+            pltpu.SemaphoreType.DMA((4,)),
+            pltpu.SemaphoreType.DMA((chips, 2)),
+        ],
+        compiler_params=pltpu.CompilerParams(
+            collective_id=2, has_side_effects=True, vmem_limit_bytes=KERNEL_VMEM
+        ),
+        cost_estimate=pl.CostEstimate(
+            flops=6 * block * width * ff_part, bytes_accessed=40 << 20, transcendentals=0
+        ),
+        name="ffn_backward",
+    )(own, gateup, down, act, slope)
+    return result, gathered.reshape(block, width), grad
+
 def to_columns(pieces, ctx_count):
     packed = jnp.concatenate(pieces, axis=2)
     quarter = packed.shape[0] // ctx_count
@@ -478,6 +992,7 @@
     fsdp_count = lax.axis_size("fsdp")
     tok_count = tokens.shape[0]
     block_len = tok_count * fsdp_count
+    chips = fsdp_count // 2
     rows = w_query.shape[0]
     ff_part = w_gate.shape[1] // fsdp_count
     scale_factor = 1.0 / math.sqrt(HD)
@@ -557,11 +1072,9 @@
     widened = matmul(narrow_low, full_right)
     mixed, mix_back = jax.vjp(mix_piece, inputs, normed, projected, widened, gain_post, gain_laurel)
     ffn_normed, ffn_norm_back = jax.vjp(rms_norm, mixed, gain_ffin)
-    ffn_all = gather_tokens(ffn_normed.astype(bfloat))
-    gateup = matmul(ffn_all, col_gateup)
-    hidden, geglu_back = jax.vjp(geglu, gateup[:, :ff_part], gateup[:, ff_part:])
-    hidden_low = hidden.astype(bfloat)
-    down_lin = scatter_tokens(matmul(hidden_low, down_low))
+    down_lin, ffn_all, hidden_low, act_low, slope_low = ffn_forward(
+        ffn_normed.astype(bfloat), col_gateup, down_low, chips
+    )
     layer_mid, ffn_out_back = jax.vjp(ffn_out_piece, mixed, down_lin, gain_ffout)
     layer_low = layer_mid.astype(bfloat)
     ple_lin = matmul(layer_low, full_pgate)
@@ -579,16 +1092,14 @@
     grad_pgate = small_sum(matmul_tn(layer_low, grad_plelin_low))
     grad_layer = grad_layer + matmul_nt(grad_plelin_low, full_pgate)
     grad_mixed, grad_down, grad_gffout = ffn_out_back(grad_layer)
-    grad_down_all = gather_tokens(grad_down.astype(bfloat))
+    grad_ffn, grad_down_all, grad_gateup_low = ffn_backward(
+        grad_down.astype(bfloat), col_gateup, down_low, act_low, slope_low, chips
+    )
     grad_wdown = row_sum(matmul_tn(hidden_low, grad_down_all))
-    grad_hidden = matmul_nt(grad_down_all, down_low)
-    grad_gate, grad_up = geglu_back(grad_hidden)
-    grad_gateup_low = jnp.concatenate([grad_gate, grad_up], axis=1).astype(bfloat)
     gateup_rows = to_rows(matmul_tn(ffn_all, grad_gateup_low), fsdp_count)
     gateup_rows = gather_rows(gateup_rows)
     grad_wgate = gateup_rows[:, :, :ff_part].reshape(rows, -1)
     grad_wup = gateup_rows[:, :, ff_part:].reshape(rows, -1)
-    grad_ffn = scatter_tokens(matmul_nt(grad_gateup_low, col_gateup))
     grad_mixed_more, grad_gffin = ffn_norm_back(grad_ffn)
     grad_mixed = grad_mixed + grad_mixed_more
     grad_in_first, grad_normed, grad_proj, grad_lwide, grad_gpost, grad_glaurel = mix_back(

time: 1410 us -> 1300 us (0.922)
  waiting for transfers between devices: 841 us -> 595 us
  Pallas kernels: 0 us -> 184 us
  matrix products: 129 us -> 83 us
  local copies, waits for them, and re-layouts: 120 us -> 98.7 us
  blocking collectives: 207 us -> 225 us
    pallas_call x0 -> x2, Pallas kernels: none -> 184 us  [the longest x1 100 us: ffn_forward(): pl.pallas_call(functools.partial(ffn_forward_kernel, chips), out_shape=[j...]
    reduce_scatter x4 -> x2, waiting for transfers between devices: 135 us -> 40 us  [scatter_tokens(): lax.psum_scatter(partial.astype(jnp.bfloat16), 'fsdp', scatter_dimension=...]
    all_gather x4 -> x2, waiting for transfers between devices: 169 us -> 82.6 us  [gather_tokens(): return lax.all_gather(part, 'fsdp', axis=0, tiled=True)]
    all_gather x2, waiting for transfers between devices: 42.2 us -> 0.02 us  [by_heads(): lax.all_gather(w.astype(bfloat), 'fsdp', axis=0, tiled=True)]
    all_to_all x0 -> x1, blocking collectives: none -> 25.6 us  [to_rows(): lax.all_to_all(summed, 'fsdp', split_axis=0, concat_axis=1, tiled=False)]
    dot_general x16 -> x14, matrix products: 47.1 us -> 21.6 us  [matmul_nt(): lax.dot_general(left_mat, right_mat, (((1,), (1,)), ((), ())), preferred_...]
    dot_general x16 -> x14, matrix products: 38.5 us -> 16.7 us  [matmul(): return jnp.dot(left_mat, right_mat, preferred_element_type=jnp.float32)]
    reduce_scatter x2, waiting for transfers between devices: 123 us -> 103 us  [to_rows(): summed = lax.psum_scatter(parts, 'ctx', scatter_dimension=1, tiled=True)]
  transfers between devices with their start and end apart: 26 -> 21, of which waited for: 20 -> 14; matrix products, arithmetic and copies ran while one was open for 11% -> 11% of each run, Pallas kernels for 0% -> 8%
where the time goes in v2:
time: 1300 us; the launch traced here: 1290 us
  waiting for transfers between devices  595 us (46%)
  blocking collectives  225 us (17%)
  Pallas kernels  184 us (14%)
  local copies, waits for them, and re-layouts  98.7 us (8%)
  matrix products  83 us (6%)
  other arithmetic  72.8 us (6%)
  between operations  17.4 us (1%)
    psum x1, waiting for transfers between devices, row_sum(): return lax.psum(partial.astype(jnp.bfloat16), 'ctx').astype(jnp.float32)  114 us
    reduce_scatter x2, waiting for transfers between devices, to_rows(): summed = lax.psum_scatter(parts, 'ctx', scatter_dimension=1, tiled=True)  103 us
    pallas_call x1, Pallas kernels, ffn_forward(): pl.pallas_call(functools.partial(ffn_forward_kernel, chips), out_shape=[j...  100 us
    all_to_all x2, blocking collectives, to_columns(): lax.all_to_all(mine, 'fsdp', split_axis=1, concat_axis=0, tiled=False)  97 us
    pallas_call x1, Pallas kernels, ffn_backward(): pl.pallas_call(functools.partial(ffn_backward_kernel, chips), out_shape=[...  84.1 us
    all_gather x2, waiting for transfers between devices, gather_tokens(): return lax.all_gather(part, 'fsdp', axis=0, tiled=True)  82.6 us
    all_gather x2, waiting for transfers between devices, gather_rows(): return lax.all_gather(part, 'ctx', axis=0, tiled=True).astype(jnp.float32)  73.9 us
    unnamed x281, local copies, waits for them, and re-layouts  50.4 us
  transfers between devices with their start and end apart: 21, of which 14 were waited for; matrix products, arithmetic and copies ran while one was open for 11% of the time, Pallas kernels for 8%

profile of v2, /device:TPU:0, one launch (start us, length us, event | category | flops | bytes accessed | tf_op | source)
XLA Modules:
  0.0 1288.2 jit_solution(15061666754822214605)
XLA Ops:
  12.7 27.1 %all_to_all.60 = bf16[1,64,8,768]{3,1,0,2:T(8,128)(2,1)S(1)} all-to-all(bf16[1,64,8,768]{3,1,0,2:T(8,128)(2,1)S(1)} %copy.131), channel_id=1, replica_groups=mesh['ctx'=4,'fsdp'=8] {'fsdp'}, dimensions={2} | all-to-all | bytes 1572864 | tf_op jit(solution)/shard_map/all_to_all | solution.py:925
  43.1 27.2 %all-reduce.6 = f32[12800]{0:T(1024)S(1)} all-reduce(f32[12800]{0:T(1024)S(1)} %dynamic-update-slice.24), channel_id=2, replica_groups=mesh['ctx'=4,'fsdp'=8] {'fsdp'}, use_global_device_ids=true, to_apply=%add.6 | all-reduce | flops 12800 | bytes 102400
  72.3 8.4 all-gather.4
  88.5 45.2 %all-gather.14.cloned.1.call-done = bf16[1024,2048]{1,0:T(8,128)(2,1)} async-done(((bf16[128,2048]{1,0:T(8,128)(2,1)}), bf16[1024,2048]{1,0:T(8,128)(2,1)}) %all-gather.14.cloned.1.call-update) | async-done | bytes 4194320 | tf_op jit(solution)/shard_map/all_gather | solution.py:948
  149.8 21.1 %collective-permute-done = bf16[2,1024,256]{1,2,0:T(8,128)(2,1)} collective-permute-done((bf16[2,1024,256]{1,2,0:T(8,128)(2,1)S(1)}, bf16[2,1024,256]{1,2,0:T(8,128)(2,1)}, u32[]{:S(2)}, u32[]{:S(2)}) %collective-permute-start) | collective-permute-done | bytes 1048608 | tf_op jit(solution)/shard_map/ppermute | solution.py:29
  184.8 7.5 copy.134
  192.2 7.2 copy.135
  208.5 69.9 %all_to_all.61 = bf16[1,64,8,2048]{3,1,0,2:T(8,128)(2,1)} all-to-all(bf16[1,64,8,2048]{3,1,0,2:T(8,128)(2,1)S(1)} %copy.136), channel_id=1, replica_groups=mesh['ctx'=4,'fsdp'=8] {'fsdp'}, dimensions={2} | all-to-all | bytes 4194304 | tf_op jit(solution)/shard_map/all_to_all | solution.py:925
  282.7 14.2 %all_gather.45 = bf16[64,2048]{1,0:T(8,128)(2,1)S(1)} all-gather(bf16[8,2048]{1,0:T(8,128)(2,1)S(1)} %convert_element_type.233), channel_id=1, replica_groups=mesh['ctx'=4,'fsdp'=8] {'fsdp'}, dimensions={0}, use_global_device_ids=true | all-gather | bytes 294912 | tf_op jit(solution)/shard_map/all_gather | solution.py:1034
  296.9 14.4 %all_gather.44 = bf16[2048,64]{0,1:T(8,128)(2,1)S(1)} all-gather(bf16[256,64]{0,1:T(8,128)(2,1)S(1)} %convert_element_type.231), channel_id=1, replica_groups=mesh['ctx'=4,'fsdp'=8] {'fsdp'}, dimensions={0}, use_global_device_ids=true | all-gather | bytes 294912 | tf_op jit(solution)/shard_map/all_gather | solution.py:1034
  323.9 41.0 %all-gather.26.cloned.1.call-done = bf16[8,1,256,1,2048]{4,2,0,3,1:T(8,128)(2,1)} async-done(((bf16[8,1,64,1,2048]{4,2,0,3,1:T(8,128)(2,1)}), bf16[8,1,256,1,2048]{4,2,0,3,1:T(8,128)(2,1)}) %all-gather.26.cloned.1.call-update) | async-done | bytes 8388624 | tf_op jit(solution)/shard_map/all_gather | solution.py:926
  364.8 100.2 %ffn_forward.1 = (f32[128,2048]{1,0:T(8,128)}, bf16[4,2,128,2048]{3,2,1,0:T(8,128)(2,1)}, bf16[1024,1024]{1,0:T(8,128)(2,1)}, bf16[1024,1024]{1,0:T(8,128)(2,1)}, bf16[1024,1024]{1,0:T(8,128)(2,1)}) custom-call(bf16[128,2048]{1,0:T(8,128)(2,1)} %multiply_convert_fusion.4.own_ref, bf16[2048,2048]{1,0:T(8,128)(2,1)} %bitcast.238, ...), custom_call_target="tpu_custom_call" | custom-call | flops 12884901888 | bytes 41943040 | tf_op jit(solution)/shard_map/ffn_forward/pallas_call | solution.py:768
  476.4 84.1 %ffn_backward.1 = (f32[128,2048]{1,0:T(8,128)}, bf16[4,2,128,2048]{3,2,1,0:T(8,128)(2,1)}, bf16[1024,2048]{1,0:T(8,128)(2,1)}) custom-call(bf16[128,2048]{1,0:T(8,128)(2,1)} %fusion.53.own_ref, bf16[2048,2048]{1,0:T(8,128)(2,1)} %bitcast.239, bf16[1024,2048]{1,0:T(8,128)(2,1)} %convert_element_type.236.down_hbm, ...), custom_call_target="tpu_custom_call" | custom-call | flops 12884901888 | bytes 41943040 | tf_op jit(solution)/shard_map/ffn_backward/pallas_call | solution.py:891
  576.1 37.4 %all-gather.20.cloned.1.call-done = bf16[1024,2048]{1,0:T(8,128)(2,1)} async-done(((bf16[128,2048]{1,0:T(8,128)(2,1)}), bf16[1024,2048]{1,0:T(8,128)(2,1)}) %all-gather.20.cloned.1.call-update) | async-done | bytes 4194320 | tf_op jit(solution)/shard_map/all_gather | solution.py:948
  634.9 24.1 %collective-permute-done.1 = bf16[2,1024,256]{1,2,0:T(8,128)(2,1)S(1)} collective-permute-done((bf16[2,1024,256]{1,2,0:T(8,128)(2,1)S(1)}, bf16[2,1024,256]{1,2,0:T(8,128)(2,1)S(1)}, u32[]{:S(2)}, u32[]{:S(2)}) %collective-permute-start.1) | collective-permute-done | bytes 1048608 | tf_op jit(solution)/shard_map/ppermute | solution.py:29
  670.4 14.0 %convolution_convert_fusion = bf16[2048,2048]{1,0:T(8,128)(2,1)} fusion(bf16[1024,2048]{1,0:T(8,128)(2,1)} %bitcast.241, bf16[1024,2048]{1,0:T(8,128)(2,1)} %get-tuple-element.131), kind=kOutput, calls=%fused_computation.5 | convolution fusion | flops 8594128896 | bytes 16777216 | tf_op jit(solution)/shard_map/dot_general | solution.py:37
  684.8 9.5 convolution_convert_fusion.3
  698.8 11.3 reduce-scatter.21.cloned.1.call-done
  710.1 32.9 %reduce-scatter.23.cloned.1.call-done = bf16[32,2048]{1,0:T(8,128)(2,1)} async-done(((bf16[256,2048]{1,0:T(8,128)(2,1)}), bf16[32,2048]{1,0:T(8,128)(2,1)}) %reduce-scatter.23.cloned.1.call-update) | async-done | bytes 131088 | tf_op jit(solution)/shard_map/reduce_scatter | solution.py:952
  750.1 38.1 %reduce-scatter.13.cloned.1.call-done = bf16[8,64,768]{2,1,0:T(8,128)(2,1)} async-done(((bf16[8,256,768]{2,1,0:T(8,128)(2,1)}), bf16[8,64,768]{2,1,0:T(8,128)(2,1)}) %reduce-scatter.13.cloned.1.call-update) | async-done | bytes 786448 | tf_op jit(solution)/shard_map/reduce_scatter | solution.py:932
  788.2 25.6 %all_to_all.62 = bf16[8,64,1,768]{3,1,2,0:T(8,128)(2,1)S(1)} all-to-all(bf16[8,64,1,768]{3,1,2,0:T(8,128)(2,1)} %bitcast.210), channel_id=1, replica_groups=mesh['ctx'=4,'fsdp'=8] {'fsdp'}, dimensions={0} | all-to-all | bytes 1572864 | tf_op jit(solution)/shard_map/all_to_all | solution.py:933
  813.7 64.5 %reduce-scatter.19.cloned.1.call-done = bf16[8,64,2048]{2,1,0:T(8,128)(2,1)} async-done(((bf16[8,256,2048]{2,1,0:T(8,128)(2,1)}), bf16[8,64,2048]{2,1,0:T(8,128)(2,1)}) %reduce-scatter.19.cloned.1.call-update) | async-done | bytes 2097168 | tf_op jit(solution)/shard_map/reduce_scatter | solution.py:932
  883.9 48.1 %all-to-all-done.3 = bf16[8,64,1,2048]{3,1,2,0:T(8,128)(2,1)} async-done(((bf16[8,64,1,2048]{3,1,2,0:T(8,128)(2,1)}), bf16[8,64,1,2048]{3,1,2,0:T(8,128)(2,1)}, u32[]{:S(2)}, u32[]{:S(2)}) %all-to-all-start.3) | async-done | bytes 2097184 | tf_op jit(solution)/shard_map/all_to_all | solution.py:933
  940.4 113.7 %all-reduce.14.cloned.1.call-done = (bf16[256,2048]{1,0:T(8,128)(2,1)}, bf16[1024,2048]{1,0:T(8,128)(2,1)}, bf16[256,256]{1,0:T(8,128)(2,1)}, bf16[32,2048]{1,0:T(8,128)(2,1)}) async-done(((bf16[256,2048]{1,0:T(8,128)(2,1)}, bf16[1024,2048]{1,0:T(8,128)(2,1)}, bf16[256,256]{1,0:T(8,128)(2,1)}, bf16[32,2048]{1,0:T(8,128)(2,1)}), (bf16[256,2048]{1,0:T(8,128)(2,1)}, bf16[1024,2048]{1,0:T(8,128)(2,1)}, ...) | async-done | bytes 5505040 | tf_op jit(solution)/shard_map/psum | solution.py:957
  1066.8 40.0 %reduce-scatter.11.cloned.1.call-done = bf16[128,2048]{1,0:T(8,128)(2,1)} async-done(((bf16[1024,2048]{1,0:T(8,128)(2,1)}), bf16[128,2048]{1,0:T(8,128)(2,1)}) %reduce-scatter.11.cloned.1.call-update) | async-done | bytes 524304 | tf_op jit(solution)/shard_map/reduce_scatter | solution.py:942
  1108.6 38.6 %psum.55 = f32[8,1600]{1,0:T(8,128)S(1)} all-reduce(f32[8,1600]{1,0:T(8,128)S(1)} %concatenate.76), channel_id=1, replica_groups=mesh['ctx'=4,'fsdp'=8] {'ctx','fsdp'}, use_global_device_ids=true, to_apply=%region_60.61 | all-reduce | flops 12800 | bytes 102400 | tf_op jit(solution)/shard_map/psum | solution.py:1175
  1153.9 73.9 %all-gather.28.cloned.1.call-done = bf16[1,256,8,1,2048]{4,2,3,0,1:T(8,128)(2,1)} async-done(((bf16[1,64,8,1,2048]{4,2,3,0,1:T(8,128)(2,1)}), bf16[1,256,8,1,2048]{4,2,3,0,1:T(8,128)(2,1)}) %all-gather.28.cloned.1.call-update) | async-done | bytes 8388624 | tf_op jit(solution)/shard_map/all_gather | solution.py:938
  1227.8 12.8 copy.145
  1240.7 10.7 bitcast_convert_fusion
  1251.4 11.7 fusion.169
  1263.1 8.9 copy.147
  1272.0 8.9 copy.146
  (488 shorter events, 178.7 us)
Async XLA Ops:
  7.2 77.2 %all-gather.24.cloned.1.call-start = ((), (), s32[]{:S(2)}) async-start(), calls=%async_computation.25 | async-start | bytes 3932160 | tf_op jit(solution)/shard_map/all_gather | solution.py:926
  41.3 92.4 %all-gather.14.cloned.1.call-start = ((), (), s32[]{:S(2)}) async-start(), calls=%async_computation.12 | async-start | bytes 4718592 | tf_op jit(solution)/shard_map/all_gather | solution.py:948
  72.2 247.0 %reduce-scatter.9.cloned.1.call-start = ((), (), s32[]{:S(2)}) async-start(), calls=%async_computation.13 | async-start | bytes 4718592 | tf_op jit(solution)/shard_map/reduce_scatter | solution.py:942
  80.7 61.5 %copy-start.61 = (f32[8,1,128]{2,1,0:T(1,128)}, f32[8,1,128]{2,1,0:T(1,128)S(1)}, u32[]{:S(2)}) copy-start(f32[8,1,128]{2,1,0:T(1,128)S(1)} %convert_element_type.277) | copy-start | bytes 12292
  80.8 59.4 %copy-start.76 = (f32[256]{0:T(256)}, f32[256]{0:T(256)S(1)}, u32[]{:S(2)}) copy-start(f32[256]{0:T(256)S(1)} %mul.670) | copy-start | bytes 3076
  80.9 59.4 %copy-start.78 = (f32[256]{0:T(256)}, f32[256]{0:T(256)S(1)}, u32[]{:S(2)}) copy-start(f32[256]{0:T(256)S(1)} %mul.685) | copy-start | bytes 3076
  80.9 61.3 %copy-start.105 = (f32[128]{0:T(128)}, f32[128]{0:T(128)S(1)}, u32[]{:S(2)}) copy-start(f32[128]{0:T(128)S(1)} %multiply_exponential_fusion) | copy-start | bytes 1540
  144.7 26.2 %collective-permute-start = (bf16[2,1024,256]{1,2,0:T(8,128)(2,1)S(1)}, bf16[2,1024,256]{1,2,0:T(8,128)(2,1)}, u32[]{:S(2)}, u32[]{:S(2)}) collective-permute-start(bf16[2,1024,256]{1,2,0:T(8,128)(2,1)S(1)} %pad_maximum_fusion.1), channel_id=1, source_target_pairs={{0,8},{8,16},{16,24},{1,9},{9,17},{17,25},{2,10},{10,18},{18,26},{... | collective-permute-start | bytes 3145736 | tf_op jit(solution)/shard_map/ppermute | solution.py:29
  184.7 180.1 %all-gather.26.cloned.1.call-start = ((), (), s32[]{:S(2)}) async-start(), calls=%async_computation.26 | async-start | bytes 10485760 | tf_op jit(solution)/shard_map/all_gather | solution.py:926
  278.5 188.6 %all-gather.16.cloned.1.call-start = ((), (), s32[]{:S(2)}) async-start(), calls=%async_computation.14 | async-start | bytes 1179648 | tf_op jit(solution)/shard_map/all_gather | solution.py:1034
  280.0 188.7 %all-gather.18.cloned.1.call-start = ((), (), s32[]{:S(2)}) async-start(), calls=%async_computation.15 | async-start | bytes 1179648 | tf_op jit(solution)/shard_map/all_gather | solution.py:1034
  280.8 332.7 %all-gather.20.cloned.1.call-start = ((), (), s32[]{:S(2)}) async-start(), calls=%async_computation.16 | async-start | bytes 4718592 | tf_op jit(solution)/shard_map/all_gather | solution.py:948
  281.5 185.1 %copy-start.50 = (f32[1,2,8,128]{3,1,2,0:T(2,128)}, f32[1,2,8,128]{3,1,2,0:T(2,128)S(1)}, u32[]{:S(2)}) copy-start(f32[1,2,8,128]{3,1,2,0:T(2,128)S(1)} %copy.161) | copy-start | bytes 24580
  322.4 142.7 %copy-start.127 = (f32[128]{0:T(128)}, f32[128]{0:T(128)S(1)}, u32[]{:S(2)}) copy-start(f32[128]{0:T(128)S(1)} %get-tuple-element.237) | copy-start | bytes 1540
  322.9 142.2 %copy-start.107 = (f32[128]{0:T(128)}, f32[128]{0:T(128)S(1)}, u32[]{:S(2)}) copy-start(f32[128]{0:T(128)S(1)} %get-tuple-element.286) | copy-start | bytes 1540
  476.4 84.2 %copy-start.108 = (f32[128]{0:T(128)S(1)}, f32[128]{0:T(128)}, u32[]{:S(2)}) copy-start(f32[128]{0:T(128)} %copy-done.107) | copy-start | bytes 1540
  567.2 127.1 %reduce-scatter.15.cloned.1.call-start = ((), (), s32[]{:S(2)}) async-start(), calls=%async_computation.20 | async-start | bytes 294912 | tf_op jit(solution)/shard_map/reduce_scatter | solution.py:952
  570.1 124.2 %reduce-scatter.17.cloned.1.call-start = ((), (), s32[]{:S(2)}) async-start(), calls=%async_computation.21 | async-start | bytes 294912 | tf_op jit(solution)/shard_map/reduce_scatter | solution.py:952
  571.8 138.3 %reduce-scatter.21.cloned.1.call-start = ((), (), s32[]{:S(2)}) async-start(), calls=%async_computation.23 | async-start | bytes 1179648 | tf_op jit(solution)/shard_map/reduce_scatter | solution.py:952
  574.2 168.8 %reduce-scatter.23.cloned.1.call-start = ((), (), s32[]{:S(2)}) async-start(), calls=%async_computation.24 | async-start | bytes 1179648 | tf_op jit(solution)/shard_map/reduce_scatter | solution.py:952
  575.9 212.3 %reduce-scatter.13.cloned.1.call-start = ((), (), s32[]{:S(2)}) async-start(), calls=%async_computation.18 | async-start | bytes 3932160 | tf_op jit(solution)/shard_map/reduce_scatter | solution.py:932
  631.8 27.2 %collective-permute-start.1 = (bf16[2,1024,256]{1,2,0:T(8,128)(2,1)S(1)}, bf16[2,1024,256]{1,2,0:T(8,128)(2,1)S(1)}, u32[]{:S(2)}, u32[]{:S(2)}) collective-permute-start(bf16[2,1024,256]{1,2,0:T(8,128)(2,1)S(1)} %pad_maximum_fusion.3), channel_id=1, source_target_pairs={{8,0},{16,8},{24,16},{9,1},{17,9},{25,17},{10,2},{18,10},{26,18},{... | collective-permute-start | bytes 3145736 | tf_op jit(solution)/shard_map/ppermute | solution.py:29
  670.3 207.9 %reduce-scatter.19.cloned.1.call-start = ((), (), s32[]{:S(2)}) async-start(), calls=%async_computation.22 | async-start | bytes 10485760 | tf_op jit(solution)/shard_map/reduce_scatter | solution.py:932
  684.4 253.0 %all-reduce.12.cloned.1.call-start = ((), (), s32[]{:S(2)}) async-start(), calls=%async_computation.28 | async-start | bytes 131072 | tf_op jit(solution)/shard_map/psum | solution.py:953
  694.3 359.8 %all-reduce.14.cloned.1.call-start = ((), (), s32[]{:S(2)}) async-start(), calls=%async_computation.29 | async-start | bytes 11010048 | tf_op jit(solution)/shard_map/psum | solution.py:957
  743.0 363.8 %reduce-scatter.11.cloned.1.call-start = ((), (), s32[]{:S(2)}) async-start(), calls=%async_computation.17 | async-start | bytes 4718592 | tf_op jit(solution)/shard_map/reduce_scatter | solution.py:942
  878.2 53.8 %all-to-all-start.3 = ((bf16[8,64,1,2048]{3,1,2,0:T(8,128)(2,1)}), bf16[8,64,1,2048]{3,1,2,0:T(8,128)(2,1)}, u32[]{:S(2)}, u32[]{:S(2)}) async-start(bf16[8,64,1,2048]{3,1,2,0:T(8,128)(2,1)} %bitcast.206), calls=%async_computation.9 | async-start | bytes 4194304 | tf_op jit(solution)/shard_map/all_to_all | solution.py:933
  882.8 267.0 %all-gather.22.cloned.1.call-start = ((), (), s32[]{:S(2)}) async-start(), calls=%async_computation.19 | async-start | bytes 1966080 | tf_op jit(solution)/shard_map/all_gather | solution.py:938
  883.8 344.0 %all-gather.28.cloned.1.call-start = ((), (), s32[]{:S(2)}) async-start(), calls=%async_computation.27 | async-start | bytes 10485760 | tf_op jit(solution)/shard_map/all_gather | solution.py:938
  1060.1 46.7 %copy-start.40 = (bf16[128,64]{0,1:T(8,128)(2,1)S(1)}, bf16[128,64]{0,1:T(8,128)(2,1)}, u32[]{:S(2)}) copy-start(bf16[128,64]{0,1:T(8,128)(2,1)} %copy-done.39) | copy-start | bytes 49156
  1060.1 46.7 %copy-start.82 = (f32[128]{0:T(128)S(1)}, f32[128]{0:T(128)}, u32[]{:S(2)}) copy-start(f32[128]{0:T(128)} %copy-done.80) | copy-start | bytes 1540
  1066.8 81.7 %copy-start.118 = (f32[128]{0:T(128)S(1)}, f32[128]{0:T(128)}, u32[]{:S(2)}) copy-start(f32[128]{0:T(128)} %copy-done.117) | copy-start | bytes 1540
  (121 other events, 653.8 us)
Sparse Core Ops, SparseCore 0:
  41.4 42.9 all-gather.23
  86.5 47.1 all-gather.13
  184.8 67.9 reduce-scatter.8
  278.6 86.2 all-gather.25
  366.9 25.9 all-gather.15
  394.9 24.1 all-gather.17
  567.3 46.1 all-gather.19
  616.3 29.0 reduce-scatter.14
  648.3 28.5 reduce-scatter.16
  679.6 30.4 reduce-scatter.20
  712.4 30.5 reduce-scatter.22
  745.9 42.2 reduce-scatter.12
  791.8 86.3 reduce-scatter.18
  881.2 41.5 all-reduce.11
  927.5 126.4 all-reduce.13
  1056.8 50.0 reduce-scatter.10
  1109.1 29.3 all-gather.21
  1140.2 87.5 all-gather.27

commit v3 on v2

--- a/solution.py
+++ b/solution.py
@@ -917,6 +917,319 @@
     )(own, gateup, down, act, slope)
     return result, gathered.reshape(block, width), grad
 
+class Share:
+    def __init__(self, refs, columns):
+        self.columns = columns
+        self.source, self.final, self.kept, self.taken, self.last = refs[:5]
+        self.load_sem, self.sum_send, self.sum_recv, self.spread_send, self.spread_recv = refs[5:10]
+        if columns:
+            self.swap_send, self.swap_recv, self.swap_own = refs[10:13]
+        at = lax.axis_index("ctx")
+        self.at_x, self.at_y = at % 2, at // 2
+        self.beside = (at + 1 - 2 * (at % 2), (at + 2) % 4)
+        self.me = lax.axis_index("fsdp")
+        self.members = lax.axis_size("fsdp")
+        self.half = self.source.shape[-2] // 2
+        self.quarter = self.half // 2
+        self.eighth = self.half // 4
+
+    def rows(self, ref, start, size):
+        start = pl.multiple_of(start, size)
+        return ref.at[:, pl.ds(start, size)] if self.columns else ref.at[pl.ds(start, size)]
+
+    def sides(self, half):
+        return (self.at_x, self.at_y) if half == 0 else (self.at_y, self.at_x)
+
+    def kept_start(self, half):
+        return half * self.half + self.sides(half)[0] * self.quarter
+
+    def given_start(self, half):
+        return half * self.half + (1 - self.sides(half)[0]) * self.quarter
+
+    def own_start(self, half):
+        return self.kept_start(half) + self.sides(half)[1] * self.eighth
+
+    def copy(self, src, dst, send_sem, recv_sem, half, stage):
+        return pltpu.make_async_remote_copy(
+            src_ref=src,
+            dst_ref=dst,
+            send_sem=send_sem.at[half, stage],
+            recv_sem=recv_sem.at[half, stage],
+            device_id={"ctx": self.beside[(half + stage) % 2]},
+            device_id_type=pl.DeviceIdType.MESH,
+        )
+
+    def load(self, half):
+        return pltpu.make_async_copy(
+            self.rows(self.source, self.kept_start(half), self.quarter),
+            self.kept.at[half],
+            self.load_sem.at[half],
+        )
+
+    def first(self, half):
+        return self.copy(
+            self.rows(self.source, self.given_start(half), self.quarter),
+            self.taken.at[half],
+            self.sum_send,
+            self.sum_recv,
+            half,
+            0,
+        )
+
+    def second(self, half):
+        other = (1 - self.sides(half)[1]) * self.eighth
+        return self.copy(
+            self.rows(self.kept.at[half], other, self.eighth),
+            self.last.at[half],
+            self.sum_send,
+            self.sum_recv,
+            half,
+            1,
+        )
+
+    def begin(self):
+        for half in (0, 1):
+            self.first(half).start()
+            self.load(half).start()
+
+    def add(self, half, start, more, more_start):
+        step = min(32, self.eighth)
+        blocks = self.eighth // step
+        layers = self.source.shape[0] if self.columns else 1
+
+        @pl.loop(0, layers * blocks)
+        def _(at):
+            layer, block = at // blocks, at % blocks
+            here = pl.ds(pl.multiple_of(start + block * step, step), step)
+            there = pl.ds(pl.multiple_of(more_start + block * step, step), step)
+            if self.columns:
+                total = self.kept[half, layer, here].astype(jnp.float32)
+                total = total + more[half, layer, there].astype(jnp.float32)
+                self.kept[half, layer, here] = total.astype(jnp.bfloat16)
+            else:
+                total = self.kept[half, here].astype(jnp.float32)
+                total = total + more[half, there].astype(jnp.float32)
+                self.kept[half, here] = total.astype(jnp.bfloat16)
+
+    def middle(self):
+        for half in (0, 1):
+            self.load(half).wait()
+            self.first(half).wait_recv()
+            side = self.sides(half)[1]
+            other = (1 - side) * self.eighth
+            self.add(half, other, self.taken, other)
+            self.second(half).start()
+            mine = side * self.eighth
+            self.add(half, mine, self.taken, mine)
+
+    def finish(self):
+        for half in (0, 1):
+            self.second(half).wait_recv()
+            self.add(half, self.sides(half)[1] * self.eighth, self.last, 0)
+
+    def own_rows(self, half):
+        return self.rows(self.kept.at[half], self.sides(half)[1] * self.eighth, self.eighth)
+
+    def place(self, half):
+        return pltpu.make_async_copy(
+            self.own_rows(half),
+            self.rows(self.final, self.own_start(half), self.eighth),
+            self.load_sem.at[half],
+        )
+
+    def swap_copy(self, half, hop, src_member):
+        target = lax.rem(self.me + hop, self.members)
+        side = self.sides(half)[1] * self.eighth
+        rows = pl.ds(pl.multiple_of(side, self.eighth), self.eighth)
+        final_rows = pl.ds(pl.multiple_of(self.own_start(half), self.eighth), self.eighth)
+        return remote(
+            self.kept.at[half, target, rows],
+            self.final.at[src_member, final_rows],
+            self.swap_send.at[hop, half],
+            self.swap_recv.at[hop, half],
+            target,
+        )
+
+    def swap_local(self, half):
+        side = self.sides(half)[1] * self.eighth
+        rows = pl.ds(pl.multiple_of(side, self.eighth), self.eighth)
+        final_rows = pl.ds(pl.multiple_of(self.own_start(half), self.eighth), self.eighth)
+        return pltpu.make_async_copy(
+            self.kept.at[half, self.me, rows],
+            self.final.at[self.me, final_rows],
+            self.swap_own.at[half],
+        )
+
+    def swap_begin(self):
+        for half in (0, 1):
+            for hop in range(1, self.members):
+                self.swap_copy(half, hop, self.me).start()
+            self.swap_local(half).start()
+
+    def swap_end(self):
+        for half in (0, 1):
+            for hop in range(1, self.members):
+                source = lax.rem(self.me + self.members - hop, self.members)
+                self.swap_copy(half, hop, source).wait_recv()
+            self.swap_local(half).wait()
+
+    def spread_copy(self, half, stage):
+        if stage == 0:
+            rows = self.rows(self.final, self.own_start(half), self.eighth)
+        else:
+            rows = self.rows(self.final, self.kept_start(half), self.quarter)
+        return self.copy(rows, rows, self.spread_send, self.spread_recv, half, 1 - stage)
+
+    def spread_wait(self, half, stage):
+        side = self.sides(half)[1]
+        if stage == 0:
+            start = self.kept_start(half) + (1 - side) * self.eighth
+            rows = self.rows(self.final, start, self.eighth)
+        else:
+            rows = self.rows(self.final, self.given_start(half), self.quarter)
+        self.copy(rows, rows, self.spread_send, self.spread_recv, half, 1 - stage).wait_recv()
+
+    def spread_begin(self):
+        for half in (0, 1):
+            self.spread_copy(half, 0).start()
+
+    def spread_on(self):
+        for half in (0, 1):
+            self.spread_wait(half, 0)
+            self.spread_copy(half, 1).start()
+
+    def spread_end(self):
+        for half in (0, 1):
+            self.spread_wait(half, 1)
+
+    def sent(self):
+        for half in (0, 1):
+            self.first(half).wait_send()
+            self.second(half).wait_send()
+            self.spread_copy(half, 0).wait_send()
+            self.spread_copy(half, 1).wait_send()
+            if self.columns:
+                for hop in range(1, self.members):
+                    self.swap_copy(half, hop, self.me).wait_send()
+
+
+def share_scratch(shape, columns):
+    dma = pltpu.SemaphoreType.DMA
+    rows, width = shape[-2:]
+    lead = shape[:-2]
+
+    def buffer(count):
+        return pltpu.VMEM((2,) + lead + (count, width), jnp.bfloat16)
+
+    scratch = [
+        pltpu.VMEM(shape, jnp.bfloat16),
+        buffer(rows // 4),
+        buffer(rows // 4),
+        buffer(rows // 8),
+        dma((2,)),
+        dma((2, 2)),
+        dma((2, 2)),
+        dma((2, 2)),
+        dma((2, 2)),
+    ]
+    if columns:
+        scratch += [dma((shape[0], 2)), dma((shape[0], 2)), dma((2,))]
+    return scratch
+
+
+def gradient_sum_kernel(columns, *refs):
+    count = len(columns)
+    sources, results = refs[:count], refs[count : 2 * count + 1]
+    scratch = list(refs[2 * count + 1 :])
+    store_sem = scratch.pop()
+    shares = []
+    for source, by_column in zip(sources, columns):
+        size = 12 if by_column else 9
+        shares.append(Share([source] + scratch[:size], by_column))
+        del scratch[:size]
+
+    ctx_at = lax.axis_index("ctx")
+    fsdp_at = lax.axis_index("fsdp")
+    members = lax.axis_size("fsdp")
+    sem = pltpu.get_barrier_semaphore()
+    mesh_id = pl.DeviceIdType.MESH
+    for beside in shares[0].beside:
+        pl.semaphore_signal(sem, inc=1, device_id={"ctx": beside}, device_id_type=mesh_id)
+    for hop in range(1, members):
+        other = lax.rem(fsdp_at + hop, members)
+        pl.semaphore_signal(sem, inc=1, device_id={"fsdp": other}, device_id_type=mesh_id)
+    pl.semaphore_wait(sem, members + 1)
+
+    def stores(at):
+        share = shares[at]
+        if at > 0:
+            return [pltpu.make_async_copy(share.final, results[at + 1], store_sem.at[0, at])]
+        part = share.final.shape[2] // 2
+        return [
+            pltpu.make_async_copy(
+                share.final.at[member, :, pl.ds(side * part, part)],
+                results[side].at[:, pl.ds(member * part, part)],
+                store_sem.at[1 + side, member],
+            )
+            for member in range(share.final.shape[0])
+            for side in (0, 1)
+        ]
+
+    for share in shares:
+        share.begin()
+    for share in shares:
+        share.middle()
+    for share in shares:
+        share.finish()
+        if share.columns:
+            share.swap_begin()
+        else:
+            for half in (0, 1):
+                share.place(half).start()
+                share.place(half).wait()
+            share.spread_begin()
+    for share in shares:
+        if share.columns:
+            share.swap_end()
+            share.spread_begin()
+        else:
+            share.spread_on()
+    for share in shares:
+        if share.columns:
+            share.spread_on()
+    for at, share in enumerate(shares):
+        share.spread_end()
+        for store in stores(at):
+            store.start()
+    for share in shares:
+        share.sent()
+    for at in range(count):
+        for store in stores(at):
+            store.wait()
+
+
+def gradient_sum(grads):
+    members, rows, width = grads[0].shape
+    wide = jax.ShapeDtypeStruct((rows, members * width // 2), jnp.bfloat16)
+    columns = [grad.ndim == 3 for grad in grads]
+    anywhere = pl.BlockSpec(memory_space=pl.ANY)
+    scratch = []
+    for grad, by_column in zip(grads, columns):
+        scratch += share_scratch(grad.shape, by_column)
+    return pl.pallas_call(
+        functools.partial(gradient_sum_kernel, columns),
+        out_shape=[wide, wide]
+        + [jax.ShapeDtypeStruct(grad.shape, jnp.bfloat16) for grad in grads[1:]],
+        in_specs=[anywhere] * len(grads),
+        out_specs=[anywhere] * (len(grads) + 1),
+        scratch_shapes=scratch + [pltpu.SemaphoreType.DMA((3, members))],
+        compiler_params=pltpu.CompilerParams(
+            collective_id=3, has_side_effects=True, vmem_limit_bytes=KERNEL_VMEM
+        ),
+        cost_estimate=pl.CostEstimate(flops=0, bytes_accessed=300 << 20, transcendentals=0),
+        name="gradient_sum",
+    )(*grads)
+
 def to_columns(pieces, ctx_count):
     packed = jnp.concatenate(pieces, axis=2)
     quarter = packed.shape[0] // ctx_count
@@ -927,17 +1240,6 @@
     return whole.reshape(-1, whole.shape[-1])
 
 
-def to_rows(partial, fsdp_count):
-    parts = partial.astype(jnp.bfloat16).reshape(fsdp_count, -1, partial.shape[-1])
-    summed = lax.psum_scatter(parts, "ctx", scatter_dimension=1, tiled=True)
-    swapped = lax.all_to_all(summed, "fsdp", split_axis=0, concat_axis=1, tiled=False)
-    return swapped
-
-
-def gather_rows(part):
-    return lax.all_gather(part, "ctx", axis=0, tiled=True).astype(jnp.float32)
-
-
 def scatter_tokens(partial):
     return lax.psum_scatter(
         partial.astype(jnp.bfloat16), "fsdp", scatter_dimension=0, tiled=True
@@ -946,15 +1248,6 @@
 
 def gather_tokens(part):
     return lax.all_gather(part, "fsdp", axis=0, tiled=True)
-
-
-def small_sum(partial):
-    rows = lax.psum_scatter(partial.astype(jnp.bfloat16), "fsdp", scatter_dimension=0, tiled=True)
-    return lax.psum(rows, "ctx").astype(jnp.float32)
-
-
-def row_sum(partial):
-    return lax.psum(partial.astype(jnp.bfloat16), "ctx").astype(jnp.float32)
 
 
 def head_rope(cosine, sine_part, lin, gain_vec):
@@ -1085,33 +1378,30 @@
 
     grad_layer, grad_pwide, grad_gple = final_back(cotangent.astype(jnp.float32))
     grad_pwide_low = grad_pwide.astype(bfloat)
-    grad_pproj = small_sum(matmul_tn(ple_low, grad_pwide_low))
+    part_pproj = matmul_tn(ple_low, grad_pwide_low)
     grad_plemid = matmul_nt(grad_pwide_low, full_pproj)
     grad_plelin, grad_pleinput = ple_back(grad_plemid)
     grad_plelin_low = grad_plelin.astype(bfloat)
-    grad_pgate = small_sum(matmul_tn(layer_low, grad_plelin_low))
+    part_pgate = matmul_tn(layer_low, grad_plelin_low)
     grad_layer = grad_layer + matmul_nt(grad_plelin_low, full_pgate)
     grad_mixed, grad_down, grad_gffout = ffn_out_back(grad_layer)
     grad_ffn, grad_down_all, grad_gateup_low = ffn_backward(
         grad_down.astype(bfloat), col_gateup, down_low, act_low, slope_low, chips
     )
-    grad_wdown = row_sum(matmul_tn(hidden_low, grad_down_all))
-    gateup_rows = to_rows(matmul_tn(ffn_all, grad_gateup_low), fsdp_count)
-    gateup_rows = gather_rows(gateup_rows)
-    grad_wgate = gateup_rows[:, :, :ff_part].reshape(rows, -1)
-    grad_wup = gateup_rows[:, :, ff_part:].reshape(rows, -1)
+    part_wdown = matmul_tn(hidden_low, grad_down_all).astype(bfloat)
+    part_gateup = matmul_tn(ffn_all, grad_gateup_low).astype(bfloat).reshape(fsdp_count, rows, -1)
     grad_mixed_more, grad_gffin = ffn_norm_back(grad_ffn)
     grad_mixed = grad_mixed + grad_mixed_more
     grad_in_first, grad_normed, grad_proj, grad_lwide, grad_gpost, grad_glaurel = mix_back(
         grad_mixed
     )
     grad_proj_all = gather_tokens(grad_proj.astype(bfloat))
-    grad_wout = row_sum(matmul_tn(attended_low, grad_proj_all))
+    part_wout = matmul_tn(attended_low, grad_proj_all).astype(bfloat)
     grad_att_low = matmul_nt(grad_proj_all, out_low).astype(bfloat)
     grad_lwide_low = grad_lwide.astype(bfloat)
-    grad_wright = small_sum(matmul_tn(narrow_low, grad_lwide_low))
+    part_right = matmul_tn(narrow_low, grad_lwide_low)
     grad_narrow_low = matmul_nt(grad_lwide_low, full_right).astype(bfloat)
-    grad_wleft = small_sum(matmul_tn(normed_low, grad_narrow_low))
+    part_left = matmul_tn(normed_low, grad_narrow_low)
     grad_normed = grad_normed + matmul_nt(grad_narrow_low, full_left)
 
     grad_query_list = []
@@ -1140,23 +1430,20 @@
     grad_klin, grad_gkey = key_back(grad_keys[WINDOW:] + returned[0])
     grad_vlin = grad_values[WINDOW:] + returned[1]
     grad_qkv_low = jnp.concatenate([grad_qlin, grad_klin, grad_vlin], axis=1).astype(bfloat)
-    qkv_rows = to_rows(matmul_tn(normed_all, grad_qkv_low), fsdp_count)
-    kv_rows = qkv_rows[:, :, HD:].astype(jnp.float32)
-    kv_rows = jnp.sum(kv_rows.reshape(kv_rows.shape[0], KV, group_size, 2 * HD), axis=2)
-    quarter = rows // ctx_count
-    qkv_rows = gather_rows(
-        jnp.concatenate(
-            [
-                qkv_rows[:, :, :HD].reshape(quarter, HQ * HD),
-                kv_rows[:, :, :HD].reshape(quarter, KV * HD).astype(bfloat),
-                kv_rows[:, :, HD:].reshape(quarter, KV * HD).astype(bfloat),
-            ],
-            axis=1,
-        )
-    )
-    grad_wquery = qkv_rows[:, : HQ * HD]
-    grad_wkey = qkv_rows[:, HQ * HD : (HQ + KV) * HD]
-    grad_wvalue = qkv_rows[:, (HQ + KV) * HD :]
+    part_qkv = matmul_tn(normed_all, grad_qkv_low).astype(bfloat).reshape(fsdp_count, rows, -1)
+    small_parts = [
+        part.astype(bfloat).reshape(fsdp_count, -1, inputs.shape[1])
+        for part in (part_pgate, part_pproj, part_left, part_right)
+    ]
+    small_sizes = [part.shape[1] for part in small_parts]
+    small_total = sum(small_sizes)
+    small_rows = -(-small_total // 128) * 128
+    small_parts.append(
+        jnp.zeros((fsdp_count, small_rows - small_total, inputs.shape[1]), bfloat)
+    )
+    small = lax.psum_scatter(
+        jnp.concatenate(small_parts, axis=1), "fsdp", scatter_dimension=0, tiled=False
+    )
     grad_normed = grad_normed + scatter_tokens(matmul_nt(grad_qkv_low, col_qkv))
     grad_in_second, grad_gin = norm_back(grad_normed)
     grad_tokens = grad_in_first + grad_in_second
@@ -1171,9 +1458,30 @@
         grad_gffout,
         grad_gple,
     ]
-    gain_rows = jnp.concatenate([g.reshape(fsdp_count, -1) for g in grad_gains], axis=1)
-    gain_sums = lax.psum(gain_rows, ("ctx", "fsdp"))
-    gain_sums = lax.dynamic_index_in_dim(gain_sums, fsdp_at, 0, keepdims=False)
+    gain_parts = jnp.concatenate([g.reshape(fsdp_count, -1) for g in grad_gains], axis=1)
+    gain_parts = jnp.pad(gain_parts, ((0, 0), (0, 128 * 128 - gain_parts.shape[1])))
+    gain_parts = gain_parts.astype(bfloat).reshape(fsdp_count, 128, 128)
+
+    sum_wgate, sum_wup, sum_wdown, sum_wout, sum_qkv, sum_small, sum_gains = gradient_sum(
+        [part_gateup, part_wdown, part_wout, part_qkv, small, gain_parts]
+    )
+    gain_sums = jnp.sum(sum_gains.astype(jnp.float32), axis=0).reshape(-1)
+    grad_wgate = sum_wgate.astype(jnp.float32)
+    grad_wup = sum_wup.astype(jnp.float32)
+    grad_wdown = sum_wdown.astype(jnp.float32)
+    grad_wout = sum_wout.astype(jnp.float32)
+    sum_qkv = sum_qkv.astype(jnp.float32)
+    grad_wquery = jnp.transpose(sum_qkv[:, :, :HD], (1, 0, 2)).reshape(rows, -1)
+    sum_kv = jnp.sum(sum_qkv[:, :, HD:].reshape(KV, group_size, rows, 2 * HD), axis=1)
+    sum_kv = jnp.transpose(sum_kv, (1, 0, 2))
+    grad_wkey = sum_kv[:, :, :HD].reshape(rows, -1)
+    grad_wvalue = sum_kv[:, :, HD:].reshape(rows, -1)
+    sum_small = sum_small.astype(jnp.float32)
+    small_ends = [sum(small_sizes[:n]) for n in range(5)]
+    grad_pgate, grad_pproj, grad_wleft, grad_wright = (
+        sum_small[small_ends[n] : small_ends[n + 1]].reshape(weight.shape)
+        for n, weight in enumerate((ple_gate, ple_proj, laurel_left, laurel_right))
+    )
     return (
         out_full.astype(bfloat),
         grad_tokens,
@@ -1244,5 +1552,5 @@
         P("fsdp"),
         P("fsdp"),
     )
-    run = by_heads if mesh.shape["fsdp"] == HQ else local
+    run = by_heads if mesh.shape["fsdp"] == HQ and mesh.shape["ctx"] == 4 else local
     return jax.shard_map(run, mesh=mesh, in_specs=in_specs, out_specs=out_specs, check_vma=False)

time: 1300 us -> 1130 us (0.87)
  waiting for transfers between devices: 595 us -> 231 us
  Pallas kernels: 184 us -> 481 us
  blocking collectives: 225 us -> 161 us
  local copies, waits for them, and re-layouts: 98.7 us -> 75.6 us
    pallas_call x0 -> x1, Pallas kernels: none -> 297 us  [gradient_sum(): pl.pallas_call(functools.partial(gradient_sum_kernel, columns), out_shape...]
    psum x2 -> x0, waiting for transfers between devices: 114 us -> none  [the longest x1 114 us: row_sum(): return lax.psum(partial.astype(jnp.bfloat16), 'ctx').astype(jnp.float32)]
    reduce_scatter x6 -> x1, waiting for transfers between devices: 147 us -> 47 us  [by_heads(): lax.psum_scatter(jnp.concatenate(small_parts, axis=1), 'fsdp', scatter_di...]
    all_gather x2 -> x0, waiting for transfers between devices: 73.9 us -> none  [gather_rows(): return lax.all_gather(part, 'ctx', axis=0, tiled=True).astype(jnp.float32)]
    all_to_all x1 -> x0, waiting for transfers between devices: 48.1 us -> none  [to_rows(): lax.all_to_all(summed, 'fsdp', split_axis=0, concat_axis=1, tiled=False)]
    psum x1 -> x0, blocking collectives: 38.6 us -> none  [by_heads(): gain_sums = lax.psum(gain_rows, ('ctx', 'fsdp'))]
    reduce_scatter x2, waiting for transfers between devices: 40 us -> 3.16 us  [scatter_tokens(): lax.psum_scatter(partial.astype(jnp.bfloat16), 'fsdp', scatter_dimension=...]
    all_to_all x1 -> x0, blocking collectives: 25.6 us -> none  [to_rows(): lax.all_to_all(summed, 'fsdp', split_axis=0, concat_axis=1, tiled=False)]
  transfers between devices with their start and end apart: 21 -> 11, of which waited for: 14 -> 8; matrix products, arithmetic and copies ran while one was open for 11% -> 9% of each run, Pallas kernels for 8% -> 9%
where the time goes in v3:
time: 1130 us; the launch traced here: 1110 us
  Pallas kernels  481 us (43%)
  waiting for transfers between devices  231 us (20%)
  blocking collectives  161 us (14%)
  local copies, waits for them, and re-layouts  75.6 us (7%)
  matrix products  73.3 us (6%)
  other arithmetic  67.9 us (6%)
  between operations  17.1 us (2%)
    pallas_call x1, Pallas kernels, gradient_sum(): pl.pallas_call(functools.partial(gradient_sum_kernel, columns), out_shape...  297 us
    pallas_call x1, Pallas kernels, ffn_forward(): pl.pallas_call(functools.partial(ffn_forward_kernel, chips), out_shape=[j...  100 us
    all_to_all x2, blocking collectives, to_columns(): lax.all_to_all(mine, 'fsdp', split_axis=1, concat_axis=0, tiled=False)  97 us
    all_gather x2, waiting for transfers between devices, gather_tokens(): return lax.all_gather(part, 'fsdp', axis=0, tiled=True)  91.5 us
    pallas_call x1, Pallas kernels, ffn_backward(): pl.pallas_call(functools.partial(ffn_backward_kernel, chips), out_shape=[...  84.1 us
    reduce_scatter x1, waiting for transfers between devices, by_heads(): lax.psum_scatter(jnp.concatenate(small_parts, axis=1), 'fsdp', scatter_di...  47 us
    ppermute x2, waiting for transfers between devices, passed_along(): return lax.ppermute(block, axis, route)  45.1 us
    all_gather x2, waiting for transfers between devices, to_columns(): whole = lax.all_gather(spread, 'ctx', axis=1, tiled=True)  44.4 us
  transfers between devices with their start and end apart: 11, of which 8 were waited for; matrix products, arithmetic and copies ran while one was open for 9% of the time, Pallas kernels for 9%

profile of v3, /device:TPU:0, one launch (start us, length us, event | category | flops | bytes accessed | tf_op | source)
XLA Modules:
  0.0 1114.1 jit_solution(4909389487044995282)
XLA Ops:
  12.7 27.1 %all_to_all.30 = bf16[1,64,8,768]{3,1,0,2:T(8,128)(2,1)S(1)} all-to-all(bf16[1,64,8,768]{3,1,0,2:T(8,128)(2,1)S(1)} %copy.118), channel_id=1, replica_groups=mesh['ctx'=4,'fsdp'=8] {'fsdp'}, dimensions={2} | all-to-all | bytes 1572864 | tf_op jit(solution)/shard_map/all_to_all | solution.py:1238
  43.1 27.2 %all-reduce.7 = f32[12800]{0:T(1024)S(1)} all-reduce(f32[12800]{0:T(1024)S(1)} %dynamic-update-slice.24), channel_id=2, replica_groups=mesh['ctx'=4,'fsdp'=8] {'fsdp'}, use_global_device_ids=true, to_apply=%add.7 | all-reduce | flops 12800 | bytes 102400
  71.7 8.4 all-gather.3
  80.5 3.9 all-gather.19.cloned.1.call-done
  84.3 4.1 copy.120
  88.5 45.2 %all-gather.11.cloned.1.call-done = bf16[1024,2048]{1,0:T(8,128)(2,1)} async-done(((bf16[128,2048]{1,0:T(8,128)(2,1)}), bf16[1024,2048]{1,0:T(8,128)(2,1)}) %all-gather.11.cloned.1.call-update) | async-done | bytes 4194320 | tf_op jit(solution)/shard_map/all_gather | solution.py:1250
  133.7 6.2 fusion.181
  144.7 4.6 collective-permute-start
  149.8 21.1 %collective-permute-done = bf16[2,1024,256]{1,2,0:T(8,128)(2,1)} collective-permute-done((bf16[2,1024,256]{1,2,0:T(8,128)(2,1)S(1)}, bf16[2,1024,256]{1,2,0:T(8,128)(2,1)}, u32[]{:S(2)}, u32[]{:S(2)}) %collective-permute-start) | collective-permute-done | bytes 1048608 | tf_op jit(solution)/shard_map/ppermute | solution.py:29
  184.1 7.5 copy.121
  191.6 7.2 copy.122
  198.8 5.4 fusion.2
  204.3 3.5 copy.123
  207.8 69.9 %all_to_all.31 = bf16[1,64,8,2048]{3,1,0,2:T(8,128)(2,1)} all-to-all(bf16[1,64,8,2048]{3,1,0,2:T(8,128)(2,1)S(1)} %copy.123), channel_id=1, replica_groups=mesh['ctx'=4,'fsdp'=8] {'fsdp'}, dimensions={2} | all-to-all | bytes 4194304 | tf_op jit(solution)/shard_map/all_to_all | solution.py:1238
  282.1 14.2 %all_gather.39 = bf16[64,2048]{1,0:T(8,128)(2,1)S(1)} all-gather(bf16[8,2048]{1,0:T(8,128)(2,1)S(1)} %convert_element_type.224), channel_id=1, replica_groups=mesh['ctx'=4,'fsdp'=8] {'fsdp'}, dimensions={0}, use_global_device_ids=true | all-gather | bytes 294912 | tf_op jit(solution)/shard_map/all_gather | solution.py:1327
  296.3 14.4 %all_gather.38 = bf16[2048,64]{0,1:T(8,128)(2,1)S(1)} all-gather(bf16[256,64]{0,1:T(8,128)(2,1)S(1)} %convert_element_type.222), channel_id=1, replica_groups=mesh['ctx'=4,'fsdp'=8] {'fsdp'}, dimensions={0}, use_global_device_ids=true | all-gather | bytes 294912 | tf_op jit(solution)/shard_map/all_gather | solution.py:1327
  312.6 6.5 convert_element_type.227.down_hbm
  323.6 40.5 %all-gather.21.cloned.1.call-done = bf16[8,1,256,1,2048]{4,2,0,3,1:T(8,128)(2,1)} async-done(((bf16[8,1,64,1,2048]{4,2,0,3,1:T(8,128)(2,1)}), bf16[8,1,256,1,2048]{4,2,0,3,1:T(8,128)(2,1)}) %all-gather.21.cloned.1.call-update) | async-done | bytes 8388624 | tf_op jit(solution)/shard_map/all_gather | solution.py:1239
  364.2 100.2 %ffn_forward.1 = (f32[128,2048]{1,0:T(8,128)}, bf16[4,2,128,2048]{3,2,1,0:T(8,128)(2,1)}, bf16[1024,1024]{1,0:T(8,128)(2,1)}, bf16[1024,1024]{1,0:T(8,128)(2,1)}, bf16[1024,1024]{1,0:T(8,128)(2,1)}) custom-call(bf16[128,2048]{1,0:T(8,128)(2,1)} %multiply_convert_fusion.4.own_ref, bf16[2048,2048]{1,0:T(8,128)(2,1)} %bitcast.218, ...), custom_call_target="tpu_custom_call" | custom-call | flops 12884901888 | bytes 41943040 | tf_op jit(solution)/shard_map/ffn_forward/pallas_call | solution.py:768
  475.7 84.1 %ffn_backward.1 = (f32[128,2048]{1,0:T(8,128)}, bf16[4,2,128,2048]{3,2,1,0:T(8,128)(2,1)}, bf16[1024,2048]{1,0:T(8,128)(2,1)}) custom-call(bf16[128,2048]{1,0:T(8,128)(2,1)} %fusion.55.own_ref, bf16[2048,2048]{1,0:T(8,128)(2,1)} %bitcast.219, bf16[1024,2048]{1,0:T(8,128)(2,1)} %convert_element_type.227.down_hbm, ...), custom_call_target="tpu_custom_call" | custom-call | flops 12884901888 | bytes 41943040 | tf_op jit(solution)/shard_map/ffn_backward/pallas_call | solution.py:891
  566.7 46.3 %all-gather.17.cloned.1.call-done = bf16[1024,2048]{1,0:T(8,128)(2,1)} async-done(((bf16[128,2048]{1,0:T(8,128)(2,1)}), bf16[1024,2048]{1,0:T(8,128)(2,1)}) %all-gather.17.cloned.1.call-update) | async-done | bytes 4194320 | tf_op jit(solution)/shard_map/all_gather | solution.py:1250
  613.0 4.2 convolution_convert_fusion.10
  633.3 24.1 %collective-permute-done.1 = bf16[2,1024,256]{1,2,0:T(8,128)(2,1)S(1)} collective-permute-done((bf16[2,1024,256]{1,2,0:T(8,128)(2,1)S(1)}, bf16[2,1024,256]{1,2,0:T(8,128)(2,1)S(1)}, u32[]{:S(2)}, u32[]{:S(2)}) %collective-permute-start.1) | collective-permute-done | bytes 1048608 | tf_op jit(solution)/shard_map/ppermute | solution.py:29
  664.2 5.0 convolution_convert_fusion.2
  684.6 8.6 convolution_convert_fusion.3.refs_1_
  693.2 11.6 %convolution_convert_fusion = bf16[2048,2048]{1,0:T(8,128)(2,1)} fusion(bf16[1024,2048]{1,0:T(8,128)(2,1)S(1)} %bitcast.221, bf16[1024,2048]{1,0:T(8,128)(2,1)S(1)} %copy-done.150), kind=kOutput, calls=%fused_computation.4 | convolution fusion | flops 8594128896 | bytes 16777216 | tf_op jit(solution)/shard_map/dot_general | solution.py:37
  707.4 7.5 convolution_convert_fusion.4
  721.6 47.0 %reduce-scatter.8.cloned.1.call-done = bf16[1,128,2048]{2,1,0:T(8,128)(2,1)} async-done(((bf16[8,128,2048]{2,1,0:T(8,128)(2,1)}), bf16[1,128,2048]{2,1,0:T(8,128)(2,1)}) %reduce-scatter.8.cloned.1.call-update) | async-done | bytes 524304 | tf_op jit(solution)/shard_map/reduce_scatter | solution.py:1444
  768.6 296.6 %gradient_sum.1 = (bf16[256,8192]{1,0:T(8,128)(2,1)}, bf16[256,8192]{1,0:T(8,128)(2,1)}, bf16[1024,2048]{1,0:T(8,128)(2,1)}, bf16[256,2048]{1,0:T(8,128)(2,1)}, ...) custom-call(bf16[8,256,2048]{2,1,0:T(8,128)(2,1)} %bitcast.179, ...), custom_call_target="tpu_custom_call" | custom-call | bytes 314572800 | tf_op jit(solution)/shard_map/gradient_sum/pallas_call | solution.py:1219
  1090.1 6.7 convert_element_type.260
  1096.9 4.4 convert_element_type.261
  1101.3 4.4 convert_element_type.262
  (505 shorter events, 129.1 us)
Async XLA Ops:
  7.2 77.2 %all-gather.19.cloned.1.call-start = ((), (), s32[]{:S(2)}) async-start(), calls=%async_computation.12 | async-start | bytes 3932160 | tf_op jit(solution)/shard_map/all_gather | solution.py:1239
  39.9 30.5 %copy-start.5 = (bf16[128,2048]{1,0:T(8,128)(2,1)S(1)}, bf16[128,2048]{1,0:T(8,128)(2,1)}, u32[]{:S(2)}) copy-start(bf16[128,2048]{1,0:T(8,128)(2,1)} %param.40) | copy-start | bytes 1572868
  41.2 30.5 %copy-start.142 = (s32[128]{0:T(128)S(1)}, s32[128]{0:T(128)}, u32[]{:S(2)}) copy-start(s32[128]{0:T(128)} %param.44) | copy-start | bytes 1540
  41.3 92.4 %all-gather.11.cloned.1.call-start = ((), (), s32[]{:S(2)}) async-start(), calls=%async_computation.5 | async-start | bytes 4718592 | tf_op jit(solution)/shard_map/all_gather | solution.py:1250
  70.6 17.9 %copy-start.133 = (f32[128]{0:T(128)}, f32[128]{0:T(128)S(1)}, u32[]{:S(2)}) copy-start(f32[128]{0:T(128)S(1)} %fusion.64) | copy-start | bytes 1540
  70.6 17.9 %copy-start.92 = (f32[128]{0:T(128)}, f32[128]{0:T(128)S(1)}, u32[]{:S(2)}) copy-start(f32[128]{0:T(128)S(1)} %fusion.142) | copy-start | bytes 1540
  71.6 247.5 %reduce-scatter.4.cloned.1.call-start = ((), (), s32[]{:S(2)}) async-start(), calls=%async_computation.6 | async-start | bytes 4718592 | tf_op jit(solution)/shard_map/reduce_scatter | solution.py:1244
  80.1 62.1 %copy-start.74 = (f32[8,1,128]{2,1,0:T(1,128)}, f32[8,1,128]{2,1,0:T(1,128)S(1)}, u32[]{:S(2)}) copy-start(f32[8,1,128]{2,1,0:T(1,128)S(1)} %convert_element_type.264) | copy-start | bytes 12292
  80.2 60.0 %copy-start.88 = (f32[256]{0:T(256)}, f32[256]{0:T(256)S(1)}, u32[]{:S(2)}) copy-start(f32[256]{0:T(256)S(1)} %mul.670) | copy-start | bytes 3076
  80.3 60.0 %copy-start.90 = (f32[256]{0:T(256)}, f32[256]{0:T(256)S(1)}, u32[]{:S(2)}) copy-start(f32[256]{0:T(256)S(1)} %mul.685) | copy-start | bytes 3076
  80.3 61.8 %copy-start.119 = (f32[128]{0:T(128)}, f32[128]{0:T(128)S(1)}, u32[]{:S(2)}) copy-start(f32[128]{0:T(128)S(1)} %multiply_exponential_fusion) | copy-start | bytes 1540
  80.4 69.1 %copy-start.123 = (s32[256]{0:T(256)}, s32[256]{0:T(256)S(1)}, u32[]{:S(2)}) copy-start(s32[256]{0:T(256)S(1)} %iota_add_fusion.5) | copy-start | bytes 3076
  144.6 33.4 %copy-start.10 = (bf16[1024,128]{0,1:T(8,128)(2,1)}, bf16[1024,128]{0,1:T(8,128)(2,1)S(1)}, u32[]{:S(2)}) copy-start(bf16[1024,128]{0,1:T(8,128)(2,1)S(1)} %get-tuple-element.326) | copy-start | bytes 786436
  144.7 26.2 %collective-permute-start = (bf16[2,1024,256]{1,2,0:T(8,128)(2,1)S(1)}, bf16[2,1024,256]{1,2,0:T(8,128)(2,1)}, u32[]{:S(2)}, u32[]{:S(2)}) collective-permute-start(bf16[2,1024,256]{1,2,0:T(8,128)(2,1)S(1)} %pad_maximum_fusion.1), channel_id=1, source_target_pairs={{0,8},{8,16},{16,24},{1,9},{9,17},{17,25},{2,10},{10,18},{18,26},{... | collective-permute-start | bytes 3145736 | tf_op jit(solution)/shard_map/ppermute | solution.py:29
  149.8 22.5 %copy-start.43 = (bf16[256,256]{0,1:T(8,128)(2,1)}, bf16[256,256]{0,1:T(8,128)(2,1)S(1)}, u32[]{:S(2)}) copy-start(bf16[256,256]{0,1:T(8,128)(2,1)S(1)} %pad_maximum_fusion.7) | copy-start | bytes 393220
  184.1 180.1 %all-gather.21.cloned.1.call-start = ((), (), s32[]{:S(2)}) async-start(), calls=%async_computation.13 | async-start | bytes 10485760 | tf_op jit(solution)/shard_map/all_gather | solution.py:1239
  277.8 33.6 %copy-start.8 = (bf16[128,2048]{1,0:T(8,128)(2,1)S(1)}, bf16[128,2048]{1,0:T(8,128)(2,1)}, u32[]{:S(2)}) copy-start(bf16[128,2048]{1,0:T(8,128)(2,1)} %fusion.40) | copy-start | bytes 1572868
  277.8 188.7 %all-gather.13.cloned.1.call-start = ((), (), s32[]{:S(2)}) async-start(), calls=%async_computation.7 | async-start | bytes 1179648 | tf_op jit(solution)/shard_map/all_gather | solution.py:1327
  279.4 188.6 %all-gather.15.cloned.1.call-start = ((), (), s32[]{:S(2)}) async-start(), calls=%async_computation.8 | async-start | bytes 1179648 | tf_op jit(solution)/shard_map/all_gather | solution.py:1327
  280.2 332.8 %all-gather.17.cloned.1.call-start = ((), (), s32[]{:S(2)}) async-start(), calls=%async_computation.9 | async-start | bytes 4718592 | tf_op jit(solution)/shard_map/all_gather | solution.py:1250
  280.9 185.1 %copy-start.63 = (f32[1,2,8,128]{3,1,2,0:T(2,128)}, f32[1,2,8,128]{3,1,2,0:T(2,128)S(1)}, u32[]{:S(2)}) copy-start(f32[1,2,8,128]{3,1,2,0:T(2,128)S(1)} %copy.146) | copy-start | bytes 24580
  296.3 22.9 %copy-start.29 = (bf16[64,2048]{1,0:T(8,128)(2,1)}, bf16[64,2048]{1,0:T(8,128)(2,1)S(1)}, u32[]{:S(2)}) copy-start(bf16[64,2048]{1,0:T(8,128)(2,1)S(1)} %all_gather.39) | copy-start | bytes 786436
  322.2 142.3 %copy-start.143 = (f32[128]{0:T(128)}, f32[128]{0:T(128)S(1)}, u32[]{:S(2)}) copy-start(f32[128]{0:T(128)S(1)} %get-tuple-element.311) | copy-start | bytes 1540
  322.7 141.7 %copy-start.121 = (f32[128]{0:T(128)}, f32[128]{0:T(128)S(1)}, u32[]{:S(2)}) copy-start(f32[128]{0:T(128)S(1)} %get-tuple-element.359) | copy-start | bytes 1540
  475.7 84.2 %copy-start.122 = (f32[128]{0:T(128)S(1)}, f32[128]{0:T(128)}, u32[]{:S(2)}) copy-start(f32[128]{0:T(128)} %copy-done.121) | copy-start | bytes 1540
  566.4 50.8 %copy-start.114 = (f32[256]{0:T(256)S(1)}, f32[256]{0:T(256)}, u32[]{:S(2)}) copy-start(f32[256]{0:T(256)} %copy-done.113) | copy-start | bytes 3076
  566.4 50.8 %copy-start.116 = (f32[256]{0:T(256)S(1)}, f32[256]{0:T(256)}, u32[]{:S(2)}) copy-start(f32[256]{0:T(256)} %copy-done.115) | copy-start | bytes 3076
  566.4 151.7 %reduce-scatter.6.cloned.1.call-start = ((), (), s32[]{:S(2)}) async-start(), calls=%async_computation.10 | async-start | bytes 4718592 | tf_op jit(solution)/shard_map/reduce_scatter | solution.py:1244
  630.1 27.2 %collective-permute-start.1 = (bf16[2,1024,256]{1,2,0:T(8,128)(2,1)S(1)}, bf16[2,1024,256]{1,2,0:T(8,128)(2,1)S(1)}, u32[]{:S(2)}, u32[]{:S(2)}) collective-permute-start(bf16[2,1024,256]{1,2,0:T(8,128)(2,1)S(1)} %pad_maximum_fusion.3), channel_id=1, source_target_pairs={{8,0},{16,8},{24,16},{9,1},{17,9},{25,17},{10,2},{18,10},{26,18},{... | collective-permute-start | bytes 3145736 | tf_op jit(solution)/shard_map/ppermute | solution.py:29
  669.2 99.4 %reduce-scatter.8.cloned.1.call-start = ((), (), s32[]{:S(2)}) async-start(), calls=%async_computation.11 | async-start | bytes 4718592 | tf_op jit(solution)/shard_map/reduce_scatter | solution.py:1444
  693.1 11.7 %copy-start.58 = (bf16[256,256]{1,0:T(8,128)(2,1)S(1)}, bf16[256,256]{1,0:T(8,128)(2,1)}, u32[]{:S(2)}) copy-start(bf16[256,256]{1,0:T(8,128)(2,1)} %copy-done.57) | copy-start | bytes 393220
  693.1 11.7 %copy-start.60 = (bf16[256,256]{1,0:T(8,128)(2,1)S(1)}, bf16[256,256]{1,0:T(8,128)(2,1)}, u32[]{:S(2)}) copy-start(bf16[256,256]{1,0:T(8,128)(2,1)} %copy-done.59) | copy-start | bytes 393220
  (130 other events, 369.7 us)
Sparse Core Ops, SparseCore 0:
  41.4 42.9 all-gather.18
  86.5 47.1 all-gather.10
  184.2 68.0 reduce-scatter.3
  277.9 86.2 all-gather.20
  366.2 25.9 all-gather.12
  394.2 24.2 all-gather.14
  566.5 46.3 all-gather.16
  669.3 48.7 reduce-scatter.5
  720.4 48.1 reduce-scatter.7

commit v4 on v3

--- a/solution.py
+++ b/solution.py
@@ -20,7 +20,8 @@
 HALF_ROOT = 1.0 / math.sqrt(2.0)
 GELU_ROOT = math.sqrt(2.0 / math.pi)
 GELU_CUBE = 0.044715
-KERNEL_VMEM = 56 << 20
+SCORE_SCALE = 1.0 / math.sqrt(HD)
+KERNEL_VMEM = 60 << 20
 
 
 def passed_along(block, axis, distance):
@@ -429,6 +430,25 @@
     )
 
 
+def dot_tn(left_mat, right_mat):
+    return lax.dot_general(
+        left_mat, right_mat, (((0,), (0,)), ((), ())), preferred_element_type=jnp.float32
+    )
+
+
+def greet_all():
+    sem = pltpu.get_barrier_semaphore()
+    members, planes = lax.axis_size("fsdp"), lax.axis_size("ctx")
+    mesh_id = pl.DeviceIdType.MESH
+    for hop in range(1, planes):
+        other = lax.rem(lax.axis_index("ctx") + hop, planes)
+        pl.semaphore_signal(sem, inc=1, device_id={"ctx": other}, device_id_type=mesh_id)
+    for hop in range(1, members):
+        other = lax.rem(lax.axis_index("fsdp") + hop, members)
+        pl.semaphore_signal(sem, inc=1, device_id={"fsdp": other}, device_id_type=mesh_id)
+    pl.semaphore_wait(sem, members + planes - 2)
+
+
 PIECES = 4
 
 
@@ -917,21 +937,17 @@
     )(own, gateup, down, act, slope)
     return result, gathered.reshape(block, width), grad
 
-class Share:
-    def __init__(self, refs, columns):
+class Plane:
+    def locate(self, columns, rows):
         self.columns = columns
-        self.source, self.final, self.kept, self.taken, self.last = refs[:5]
-        self.load_sem, self.sum_send, self.sum_recv, self.spread_send, self.spread_recv = refs[5:10]
-        if columns:
-            self.swap_send, self.swap_recv, self.swap_own = refs[10:13]
         at = lax.axis_index("ctx")
         self.at_x, self.at_y = at % 2, at // 2
         self.beside = (at + 1 - 2 * (at % 2), (at + 2) % 4)
         self.me = lax.axis_index("fsdp")
         self.members = lax.axis_size("fsdp")
-        self.half = self.source.shape[-2] // 2
-        self.quarter = self.half // 2
-        self.eighth = self.half // 4
+        self.half = rows // 2
+        self.quarter = rows // 4
+        self.eighth = rows // 8
 
     def rows(self, ref, start, size):
         start = pl.multiple_of(start, size)
@@ -958,6 +974,13 @@
             device_id={"ctx": self.beside[(half + stage) % 2]},
             device_id_type=pl.DeviceIdType.MESH,
         )
+
+
+class Summed(Plane):
+    def __init__(self, source, refs, columns):
+        self.source = source
+        self.kept, self.taken, self.last, self.load_sem, self.sum_send, self.sum_recv = refs
+        self.locate(columns, source.shape[-2])
 
     def load(self, half):
         return pltpu.make_async_copy(
@@ -1030,20 +1053,53 @@
     def own_rows(self, half):
         return self.rows(self.kept.at[half], self.sides(half)[1] * self.eighth, self.eighth)
 
+    def held(self, half, member):
+        side = self.sides(half)[1] * self.eighth
+        return self.kept.at[half, member, pl.ds(pl.multiple_of(side, self.eighth), self.eighth)]
+
+    def sum_sent(self):
+        for half in (0, 1):
+            self.first(half).wait_send()
+            self.second(half).wait_send()
+
+
+class Held:
+    def __init__(self, kept):
+        self.kept = kept
+
+    def own_rows(self, half):
+        return self.kept.at[half]
+
+    def held(self, half, member):
+        return self.kept.at[half, member]
+
+
+class Spread(Plane):
+    def __init__(self, source, refs, columns):
+        self.own_rows, self.held = source.own_rows, source.held
+        self.final, self.spread_send, self.spread_recv, self.place_sem = refs[:4]
+        if columns:
+            self.swap_send, self.swap_recv = refs[4:]
+        self.locate(columns, self.final.shape[-2])
+
     def place(self, half):
         return pltpu.make_async_copy(
             self.own_rows(half),
             self.rows(self.final, self.own_start(half), self.eighth),
-            self.load_sem.at[half],
+            self.place_sem.at[half],
         )
+
+    def place_all(self):
+        for half in (0, 1):
+            self.place(half).start()
+        for half in (0, 1):
+            self.place(half).wait()
 
     def swap_copy(self, half, hop, src_member):
         target = lax.rem(self.me + hop, self.members)
-        side = self.sides(half)[1] * self.eighth
-        rows = pl.ds(pl.multiple_of(side, self.eighth), self.eighth)
         final_rows = pl.ds(pl.multiple_of(self.own_start(half), self.eighth), self.eighth)
         return remote(
-            self.kept.at[half, target, rows],
+            self.held(half, target),
             self.final.at[src_member, final_rows],
             self.swap_send.at[hop, half],
             self.swap_recv.at[hop, half],
@@ -1051,13 +1107,11 @@
         )
 
     def swap_local(self, half):
-        side = self.sides(half)[1] * self.eighth
-        rows = pl.ds(pl.multiple_of(side, self.eighth), self.eighth)
         final_rows = pl.ds(pl.multiple_of(self.own_start(half), self.eighth), self.eighth)
         return pltpu.make_async_copy(
-            self.kept.at[half, self.me, rows],
+            self.held(half, self.me),
             self.final.at[self.me, final_rows],
-            self.swap_own.at[half],
+            self.place_sem.at[half],
         )
 
     def swap_begin(self):
@@ -1102,10 +1156,8 @@
         for half in (0, 1):
             self.spread_wait(half, 1)
 
-    def sent(self):
+    def spread_sent(self):
         for half in (0, 1):
-            self.first(half).wait_send()
-            self.second(half).wait_send()
             self.spread_copy(half, 0).wait_send()
             self.spread_copy(half, 1).wait_send()
             if self.columns:
@@ -1113,146 +1165,673 @@
                     self.swap_copy(half, hop, self.me).wait_send()
 
 
-def share_scratch(shape, columns):
+def sum_scratch(shape):
     dma = pltpu.SemaphoreType.DMA
     rows, width = shape[-2:]
-    lead = shape[:-2]
 
     def buffer(count):
-        return pltpu.VMEM((2,) + lead + (count, width), jnp.bfloat16)
-
-    scratch = [
-        pltpu.VMEM(shape, jnp.bfloat16),
-        buffer(rows // 4),
-        buffer(rows // 4),
-        buffer(rows // 8),
-        dma((2,)),
-        dma((2, 2)),
-        dma((2, 2)),
-        dma((2, 2)),
-        dma((2, 2)),
-    ]
-    if columns:
-        scratch += [dma((shape[0], 2)), dma((shape[0], 2)), dma((2,))]
+        return pltpu.VMEM((2,) + shape[:-2] + (count, width), jnp.bfloat16)
+
+    buffers = [buffer(rows // 4), buffer(rows // 4), buffer(rows // 8)]
+    return buffers + [dma((2,)), dma((2, 2)), dma((2, 2))]
+
+
+SUM_REFS = 6
+
+
+def spread_scratch(shape):
+    dma = pltpu.SemaphoreType.DMA
+    scratch = [pltpu.VMEM(shape, jnp.bfloat16), dma((2, 2)), dma((2, 2)), dma((2,))]
+    if len(shape) == 3:
+        scratch += [dma((shape[0], 2)), dma((shape[0], 2))]
     return scratch
 
 
-def gradient_sum_kernel(columns, *refs):
-    count = len(columns)
-    sources, results = refs[:count], refs[count : 2 * count + 1]
-    scratch = list(refs[2 * count + 1 :])
+def spread_refs(columns):
+    return 6 if columns else 4
+
+
+def gradient_sum_kernel(held_columns, columns, *refs):
+    refs = list(refs)
+    helds, sources = refs[: len(held_columns)], refs[len(held_columns) :][: len(columns)]
+    count = len(helds) + len(sources)
+    results = refs[count : 2 * count + 1]
+    scratch = refs[2 * count + 1 :]
     store_sem = scratch.pop()
-    shares = []
+    sums, spreads = [], []
+    for kept, by_column in zip(helds, held_columns):
+        size = spread_refs(by_column)
+        spreads.append(Spread(Held(kept), scratch[:size], by_column))
+        del scratch[:size]
     for source, by_column in zip(sources, columns):
-        size = 12 if by_column else 9
-        shares.append(Share([source] + scratch[:size], by_column))
+        sums.append(Summed(source, scratch[:SUM_REFS], by_column))
+        del scratch[:SUM_REFS]
+        size = spread_refs(by_column)
+        spreads.append(Spread(sums[-1], scratch[:size], by_column))
         del scratch[:size]
-
-    ctx_at = lax.axis_index("ctx")
-    fsdp_at = lax.axis_index("fsdp")
-    members = lax.axis_size("fsdp")
-    sem = pltpu.get_barrier_semaphore()
-    mesh_id = pl.DeviceIdType.MESH
-    for beside in shares[0].beside:
-        pl.semaphore_signal(sem, inc=1, device_id={"ctx": beside}, device_id_type=mesh_id)
-    for hop in range(1, members):
-        other = lax.rem(fsdp_at + hop, members)
-        pl.semaphore_signal(sem, inc=1, device_id={"fsdp": other}, device_id_type=mesh_id)
-    pl.semaphore_wait(sem, members + 1)
+    early, late = spreads[: len(helds)], spreads[len(helds) :]
+    greet_all()
 
     def stores(at):
-        share = shares[at]
+        final = spreads[at].final
         if at > 0:
-            return [pltpu.make_async_copy(share.final, results[at + 1], store_sem.at[0, at])]
-        part = share.final.shape[2] // 2
+            return [pltpu.make_async_copy(final, results[at + 1], store_sem.at[0, at])]
+        part = final.shape[2] // 2
         return [
             pltpu.make_async_copy(
-                share.final.at[member, :, pl.ds(side * part, part)],
+                final.at[member, :, pl.ds(side * part, part)],
                 results[side].at[:, pl.ds(member * part, part)],
                 store_sem.at[1 + side, member],
             )
-            for member in range(share.final.shape[0])
+            for member in range(final.shape[0])
             for side in (0, 1)
         ]
 
-    for share in shares:
+    def launch(spread):
+        if spread.columns:
+            spread.swap_begin()
+        else:
+            spread.place_all()
+            spread.spread_begin()
+
+    for share in sums:
         share.begin()
-    for share in shares:
+    for spread in early:
+        launch(spread)
+    for share in sums:
         share.middle()
-    for share in shares:
+    for spread in early:
+        if spread.columns:
+            spread.swap_end()
+            spread.spread_begin()
+        else:
+            spread.spread_on()
+    for share, spread in zip(sums, late):
         share.finish()
-        if share.columns:
-            share.swap_begin()
+        launch(spread)
+    for spread in early:
+        if spread.columns:
+            spread.spread_on()
+    for spread in late:
+        if spread.columns:
+            spread.swap_end()
+            spread.spread_begin()
         else:
-            for half in (0, 1):
-                share.place(half).start()
-                share.place(half).wait()
-            share.spread_begin()
-    for share in shares:
-        if share.columns:
-            share.swap_end()
-            share.spread_begin()
-        else:
-            share.spread_on()
-    for share in shares:
-        if share.columns:
-            share.spread_on()
-    for at, share in enumerate(shares):
-        share.spread_end()
+            spread.spread_on()
+    for spread in late:
+        if spread.columns:
+            spread.spread_on()
+    for at, spread in enumerate(spreads):
+        spread.spread_end()
         for store in stores(at):
             store.start()
-    for share in shares:
-        share.sent()
+    for share in sums:
+        share.sum_sent()
+    for spread in spreads:
+        spread.spread_sent()
     for at in range(count):
         for store in stores(at):
             store.wait()
 
 
-def gradient_sum(grads):
-    members, rows, width = grads[0].shape
-    wide = jax.ShapeDtypeStruct((rows, members * width // 2), jnp.bfloat16)
+def gradient_sum(helds, grads):
+    held_shapes = [held.shape[1:-2] + (8 * held.shape[-2], held.shape[-1]) for held in helds]
+    members, rows, width = held_shapes[0]
+    wide = (rows, members * width // 2)
+    shapes = held_shapes + [grad.shape for grad in grads]
+    held_columns = [len(shape) == 3 for shape in held_shapes]
     columns = [grad.ndim == 3 for grad in grads]
     anywhere = pl.BlockSpec(memory_space=pl.ANY)
     scratch = []
-    for grad, by_column in zip(grads, columns):
-        scratch += share_scratch(grad.shape, by_column)
+    for shape in held_shapes:
+        scratch += spread_scratch(shape)
+    for grad in grads:
+        scratch += sum_scratch(grad.shape) + spread_scratch(grad.shape)
     return pl.pallas_call(
-        functools.partial(gradient_sum_kernel, columns),
-        out_shape=[wide, wide]
-        + [jax.ShapeDtypeStruct(grad.shape, jnp.bfloat16) for grad in grads[1:]],
-        in_specs=[anywhere] * len(grads),
-        out_specs=[anywhere] * (len(grads) + 1),
+        functools.partial(gradient_sum_kernel, held_columns, columns),
+        out_shape=[
+            jax.ShapeDtypeStruct(shape, jnp.bfloat16) for shape in [wide, wide] + shapes[1:]
+        ],
+        in_specs=[anywhere] * len(shapes),
+        out_specs=[anywhere] * (len(shapes) + 1),
         scratch_shapes=scratch + [pltpu.SemaphoreType.DMA((3, members))],
         compiler_params=pltpu.CompilerParams(
             collective_id=3, has_side_effects=True, vmem_limit_bytes=KERNEL_VMEM
         ),
         cost_estimate=pl.CostEstimate(flops=0, bytes_accessed=300 << 20, transcendentals=0),
         name="gradient_sum",
-    )(*grads)
-
-def to_columns(pieces, ctx_count):
-    packed = jnp.concatenate(pieces, axis=2)
-    quarter = packed.shape[0] // ctx_count
-    start = lax.axis_index("ctx") * quarter
-    mine = lax.dynamic_slice_in_dim(packed, start, quarter, 0).astype(jnp.bfloat16)
-    spread = lax.all_to_all(mine, "fsdp", split_axis=1, concat_axis=0, tiled=False)
-    whole = lax.all_gather(spread, "ctx", axis=1, tiled=True)
-    return whole.reshape(-1, whole.shape[-1])
-
-
-def scatter_tokens(partial):
-    return lax.psum_scatter(
-        partial.astype(jnp.bfloat16), "fsdp", scatter_dimension=0, tiled=True
-    ).astype(jnp.float32)
-
-
-def gather_tokens(part):
-    return lax.all_gather(part, "fsdp", axis=0, tiled=True)
-
-
-def head_rope(cosine, sine_part, lin, gain_vec):
-    return rotate(rms_norm(lin, gain_vec), cosine, sine_part)
-
+    )(*helds, *grads)
+
+def rope_norm(lin, gain, cosine, sine_part):
+    scale = lax.rsqrt(jnp.mean(lin * lin, axis=-1, keepdims=True) + EPSILON)
+    scaled = lin * scale * gain
+    first, second = scaled[:, : HD // 2], scaled[:, HD // 2 :]
+    return jnp.concatenate(
+        [first * cosine - second * sine_part, second * cosine + first * sine_part], axis=-1
+    )
+
+
+def attention_forward_kernel(
+    chips,
+    own_ref,
+    qkv_own,
+    gate_own,
+    up_own,
+    out_hbm,
+    cos_ref,
+    sin_ref,
+    gain_query_ref,
+    gain_key_ref,
+    query_docs_ref,
+    key_docs_ref,
+    result_ref,
+    all_hbm,
+    qkv_hbm,
+    gateup_hbm,
+    lin_hbm,
+    query_hbm,
+    span_hbm,
+    probs_hbm,
+    attended_hbm,
+    *scratch,
+):
+    scratch = list(scratch)
+    line = Line(chips, scratch[:LINE_REFS])
+    del scratch[:LINE_REFS]
+    spreads = []
+    for kept in (qkv_own, gate_own, up_own):
+        spreads.append(Spread(Held(kept), scratch[: spread_refs(True)], True))
+        del scratch[: spread_refs(True)]
+    qkv, gate, up = spreads
+    out, lin, query, span, probs, attended = scratch[:6]
+    load_sem, store_sem, span_send, span_recv = scratch[6:]
+    width = line.slots.shape[3]
+    pair = 2 * line.tok
+    block = chips * pair
+    ctx_at = lax.axis_index("ctx")
+    planes = lax.axis_size("ctx")
+    ff_part = gate.final.shape[2]
+    bfloat = jnp.bfloat16
+
+    load_out = pltpu.make_async_copy(out_hbm, out, load_sem)
+    load_out.start()
+    greet_all()
+    qkv.swap_begin()
+    line.gather_begin(own_ref)
+    line.gather_step(1)
+    qkv.swap_end()
+    qkv.spread_begin()
+    line.gather_step(2)
+    qkv.spread_on()
+    for distance in range(3, chips):
+        line.gather_step(distance)
+    gate.swap_begin()
+    up.swap_begin()
+    line.own_copy(own_ref).wait()
+    for chip in range(chips):
+        line.gather_other(chip)
+    qkv.spread_end()
+    stores = [
+        pltpu.make_async_copy(line.slots, all_hbm, store_sem.at[0]),
+        pltpu.make_async_copy(qkv.final, qkv_hbm, store_sem.at[1]),
+        pltpu.make_async_copy(lin, lin_hbm, store_sem.at[2]),
+        pltpu.make_async_copy(query, query_hbm, store_sem.at[3]),
+        pltpu.make_async_copy(span, span_hbm, store_sem.at[4]),
+        pltpu.make_async_copy(probs, probs_hbm, store_sem.at[5]),
+        pltpu.make_async_copy(attended, attended_hbm, store_sem.at[6]),
+        pltpu.make_async_copy(
+            gate.final, gateup_hbm.at[:, :, pl.ds(0, ff_part)], store_sem.at[7]
+        ),
+        pltpu.make_async_copy(
+            up.final, gateup_hbm.at[:, :, pl.ds(ff_part, ff_part)], store_sem.at[8]
+        ),
+    ]
+    stores[0].start()
+    stores[1].start()
+
+    @pl.loop(0, chips)
+    def _(chip):
+        rows = pl.ds(pl.multiple_of(chip * pair, pair), pair)
+        span_rows = pl.ds(pl.multiple_of(WINDOW + chip * pair, pair), pair)
+        inputs = line.slots[chip].reshape(pair, width)
+        weights = qkv.final[...].reshape(width, 3 * HD)
+        key_lin = dot_nn(inputs, weights[:, HD : 2 * HD])
+        lin[rows, HD : 2 * HD] = key_lin
+        span[0, span_rows] = rope_norm(
+            key_lin, gain_key_ref[...], cos_ref[rows], sin_ref[rows]
+        ).astype(bfloat)
+        span[1, span_rows] = dot_nn(inputs, weights[:, 2 * HD :]).astype(bfloat)
+
+    part = WINDOW // 2
+
+    def span_copy(start, to_start, way, device):
+        return pltpu.make_async_remote_copy(
+            src_ref=span.at[:, pl.ds(pl.multiple_of(start, part), part)],
+            dst_ref=span.at[:, pl.ds(pl.multiple_of(to_start, part), part)],
+            send_sem=span_send.at[way],
+            recv_sem=span_recv.at[way],
+            device_id=device,
+            device_id_type=pl.DeviceIdType.MESH,
+        )
+
+    mine = line.core * part
+    others = (1 - line.core) * part
+    onward = span_copy(block + mine, mine, 0, {"ctx": lax.rem(ctx_at + 1, planes)})
+    across = span_copy(mine, mine, 1, {"fsdp": line.place(line.chip, 1 - line.core)})
+    arrived = span_copy(others, others, 1, {"fsdp": line.place(line.chip, 1 - line.core)})
+
+    @pl.when(ctx_at < planes - 1)
+    def _():
+        onward.start()
+
+    @pl.when(ctx_at == 0)
+    def _():
+        span[:, pl.ds(0, WINDOW)] = jnp.zeros((2, WINDOW, HD), bfloat)
+
+    @pl.loop(0, chips)
+    def _(chip):
+        rows = pl.ds(pl.multiple_of(chip * pair, pair), pair)
+        inputs = line.slots[chip].reshape(pair, width)
+        weights = qkv.final[...].reshape(width, 3 * HD)
+        query_lin = dot_nn(inputs, weights[:, :HD])
+        lin[rows, :HD] = query_lin
+        rotated = rope_norm(query_lin, gain_query_ref[...], cos_ref[rows], sin_ref[rows])
+        query[rows] = (rotated.astype(bfloat).astype(jnp.float32) * SCORE_SCALE).astype(bfloat)
+
+    @pl.when(ctx_at > 0)
+    def _():
+        onward.wait_recv()
+        across.start()
+        arrived.wait_recv()
+
+    for store in stores[2:5]:
+        store.start()
+    load_out.wait()
+
+    span_len = WINDOW + pair
+    for step in range(chips):
+        chip = line.order(chips - 1 - step)
+        rows = pl.ds(pl.multiple_of(chip * pair, pair), pair)
+        span_rows = pl.ds(pl.multiple_of(chip * pair, pair), span_len)
+        scores = dot_nt(query[rows], span[0, span_rows])
+        distance = (
+            WINDOW
+            + lax.broadcasted_iota(jnp.int32, (pair, span_len), 0)
+            - lax.broadcasted_iota(jnp.int32, (pair, span_len), 1)
+        )
+        visible = (
+            (distance >= 0)
+            & (distance < WINDOW)
+            & (query_docs_ref[rows] == key_docs_ref[:, span_rows])
+        )
+        scores = jnp.where(visible, scores, NEGATIVE)
+        shifted = jnp.exp(scores - jnp.max(scores, axis=-1, keepdims=True))
+        prob = (shifted / jnp.sum(shifted, axis=-1, keepdims=True)).astype(bfloat)
+        probs[rows] = prob
+        attended[rows] = dot_nn(prob, span[1, span_rows]).astype(bfloat)
+
+        wide = 512
+
+        @pl.loop(0, width // wide)
+        def _(at, chip=chip, rows=rows):
+            cols = pl.ds(pl.multiple_of(at * wide, wide), wide)
+            sums = dot_nn(attended[rows], out[:, cols]).astype(bfloat)
+            line.parts[chip, :, :, cols] = sums.reshape(2, line.tok, wide)
+
+        line.core_copy(chip).start()
+        if step > 0:
+            line.scatter_first(line.order(chips - step))
+        if step == 1:
+            gate.swap_end()
+            gate.spread_begin()
+    line.scatter_first(line.order(0))
+    for store in stores[5:7]:
+        store.start()
+    gate.spread_on()
+    up.swap_end()
+    up.spread_begin()
+    line.scatter_rest(result_ref)
+    up.spread_on()
+    gate.spread_end()
+    stores[7].start()
+    up.spread_end()
+    stores[8].start()
+    line.gather_end()
+    for spread in spreads:
+        spread.spread_sent()
+
+    @pl.when(ctx_at < planes - 1)
+    def _():
+        onward.wait_send()
+
+    @pl.when(ctx_at > 0)
+    def _():
+        across.wait_send()
+
+    for store in stores:
+        store.wait()
+
+
+def attention_forward(
+    own, qkv_own, gate_own, up_own, out, cosine, sine_part, gain_query, gain_key, query_docs, key_docs
+):
+    tok_count, width = own.shape
+    members = qkv_own.shape[1]
+    chips = members // 2
+    block = members * tok_count
+    span_len = WINDOW + block
+    rows = 8 * qkv_own.shape[2]
+    ff_part = gate_own.shape[3]
+    bfloat = jnp.bfloat16
+    anywhere = pl.BlockSpec(memory_space=pl.ANY)
+    vmem = pl.BlockSpec(memory_space=pltpu.VMEM)
+    dma = pltpu.SemaphoreType.DMA
+    kept = [
+        ((block, 2 * HD), jnp.float32),
+        ((block, HD), bfloat),
+        ((2, span_len, HD), bfloat),
+        ((block, WINDOW + 2 * tok_count), bfloat),
+        ((block, HD), bfloat),
+    ]
+    outputs = [
+        ((tok_count, width), jnp.float32),
+        ((chips, 2, tok_count, width), bfloat),
+        ((members, rows, 3 * HD), bfloat),
+        ((members, rows, 2 * ff_part), bfloat),
+    ] + kept
+    return pl.pallas_call(
+        functools.partial(attention_forward_kernel, chips),
+        out_shape=[jax.ShapeDtypeStruct(*output) for output in outputs],
+        in_specs=[vmem] + [anywhere] * 4 + [vmem] * 6,
+        out_specs=[vmem] + [anywhere] * 8,
+        scratch_shapes=line_scratch(chips, tok_count, width)
+        + spread_scratch((members, rows, 3 * HD))
+        + spread_scratch((members, rows, ff_part))
+        + spread_scratch((members, rows, ff_part))
+        + [pltpu.VMEM(out.shape, bfloat)]
+        + [pltpu.VMEM(*one) for one in kept]
+        + [dma, dma((9,)), dma((2,)), dma((2,))],
+        compiler_params=pltpu.CompilerParams(
+            collective_id=4, has_side_effects=True, vmem_limit_bytes=KERNEL_VMEM
+        ),
+        cost_estimate=pl.CostEstimate(
+            flops=8 << 30, bytes_accessed=300 << 20, transcendentals=block * 1280
+        ),
+        name="attention_forward",
+    )(
+        own,
+        qkv_own,
+        gate_own,
+        up_own,
+        out,
+        cosine,
+        sine_part,
+        gain_query,
+        gain_key,
+        query_docs,
+        key_docs,
+    )
+
+def rope_norm_back(grad, lin, gain, cosine, sine_part):
+    first, second = grad[:, : HD // 2], grad[:, HD // 2 :]
+    turned = jnp.concatenate(
+        [first * cosine + second * sine_part, second * cosine - first * sine_part], axis=-1
+    )
+    scale = lax.rsqrt(jnp.mean(lin * lin, axis=-1, keepdims=True) + EPSILON)
+    scaled = turned * gain
+    along = jnp.mean(lin * scaled, axis=-1, keepdims=True)
+    grad_lin = scale * scaled - lin * (scale * scale * scale * along)
+    return grad_lin, jnp.sum(lin * scale * turned, axis=0, keepdims=True)
+
+
+def attention_backward_kernel(
+    chips,
+    own_ref,
+    out_hbm,
+    qkv_hbm,
+    lin_hbm,
+    query_hbm,
+    span_hbm,
+    probs_hbm,
+    cos_ref,
+    sin_ref,
+    gain_query_ref,
+    gain_key_ref,
+    gateup_hbm,
+    down_hbm,
+    result_ref,
+    all_hbm,
+    grad_hbm,
+    gains_ref,
+    gateup_kept,
+    down_kept,
+    *scratch,
+):
+    scratch = list(scratch)
+    line = Line(chips, scratch[:LINE_REFS])
+    del scratch[:LINE_REFS]
+    shares = []
+    for source, columns in ((gateup_hbm, True), (down_hbm, False)):
+        shares.append(Summed(source, scratch[:SUM_REFS], columns))
+        del scratch[:SUM_REFS]
+    gateup, down = shares
+    out, qkv, lin, query, span, probs, grad, grad_span, back, across, returned = scratch[:11]
+    load_sem, store_sem, back_send, back_recv, grad_out = scratch[11:]
+    width = line.slots.shape[3]
+    pair = 2 * line.tok
+    block = chips * pair
+    ctx_at = lax.axis_index("ctx")
+    planes = lax.axis_size("ctx")
+    bfloat = jnp.bfloat16
+    loads = [
+        pltpu.make_async_copy(src, dst, load_sem.at[at])
+        for at, (src, dst) in enumerate(
+            (
+                (out_hbm, out),
+                (span_hbm, span),
+                (probs_hbm, probs),
+                (lin_hbm, lin),
+                (query_hbm, query),
+                (qkv_hbm, qkv),
+            )
+        )
+    ]
+    for load in loads:
+        load.start()
+    greet_all()
+    line.gather_begin(own_ref)
+    gateup.begin()
+    grad_span[...] = jnp.zeros_like(grad_span)
+    gains_ref[...] = jnp.zeros_like(gains_ref)
+    line.own_copy(own_ref).wait()
+    for load in loads:
+        load.wait()
+
+    span_len = WINDOW + pair
+    for step in range(chips):
+        if step > 0:
+            line.gather_step(step)
+        chip = line.order(step)
+        line.gather_other(chip)
+        rows = pl.ds(pl.multiple_of(chip * pair, pair), pair)
+        span_rows = pl.ds(pl.multiple_of(chip * pair, pair), span_len)
+        grad_out[rows] = dot_nt(line.slots[chip].reshape(pair, width), out[...]).astype(bfloat)
+        grad_prob = dot_nt(grad_out[rows], span[1, span_rows])
+        prob = probs[rows].astype(jnp.float32)
+        inner = jnp.sum(prob * grad_prob, axis=-1, keepdims=True)
+        grad_score = (prob * (grad_prob - inner)).astype(bfloat)
+        grad_query = dot_nn(grad_score, span[0, span_rows]) * SCORE_SCALE
+        grad_lin, grad_gain = rope_norm_back(
+            grad_query, lin[rows, :HD], gain_query_ref[...], cos_ref[rows], sin_ref[rows]
+        )
+        grad[rows, :HD] = grad_lin.astype(bfloat)
+        gains_ref[0:1] += grad_gain
+        grad_span[0, span_rows] += dot_tn(grad_score, query[rows])
+        grad_span[1, span_rows] += dot_tn(probs[rows], grad_out[rows])
+
+    store_all = pltpu.make_async_copy(line.slots, all_hbm, store_sem.at[0])
+    store_all.start()
+
+    part = WINDOW // 2
+    mine, others = line.core * part, (1 - line.core) * part
+    back[...] = grad_span[:, pl.ds(pl.multiple_of(others, part), part)].astype(bfloat)
+    to_core = remote(
+        back, across, back_send.at[0], back_recv.at[0], line.place(line.chip, 1 - line.core)
+    )
+    to_core.start()
+    to_core.wait()
+    total = grad_span[:, pl.ds(pl.multiple_of(mine, part), part)]
+    back[...] = (total + across[...].astype(jnp.float32)).astype(bfloat)
+    to_before = pltpu.make_async_remote_copy(
+        src_ref=back,
+        dst_ref=returned,
+        send_sem=back_send.at[1],
+        recv_sem=back_recv.at[1],
+        device_id={"ctx": lax.rem(ctx_at + planes - 1, planes)},
+        device_id_type=pl.DeviceIdType.MESH,
+    )
+
+    @pl.when(ctx_at > 0)
+    def _():
+        to_before.start()
+
+    down.begin()
+
+    @pl.when(ctx_at < planes - 1)
+    def _():
+        to_before.wait_recv()
+        here = pl.ds(pl.multiple_of(block + mine, part), part)
+        grad_span[:, here] += returned[...].astype(jnp.float32)
+
+    for step in range(chips):
+        chip = line.order(chips - 1 - step)
+        rows = pl.ds(pl.multiple_of(chip * pair, pair), pair)
+        span_rows = pl.ds(pl.multiple_of(WINDOW + chip * pair, pair), pair)
+        grad_lin, grad_gain = rope_norm_back(
+            grad_span[0, span_rows], lin[rows, HD:], gain_key_ref[...], cos_ref[rows], sin_ref[rows]
+        )
+        grad[rows, HD : 2 * HD] = grad_lin.astype(bfloat)
+        gains_ref[1:2] += grad_gain
+        grad[rows, 2 * HD :] = grad_span[1, span_rows].astype(bfloat)
+        wide = 512
+
+        @pl.loop(0, width // wide)
+        def _(at, chip=chip, rows=rows):
+            cols = pl.ds(pl.multiple_of(at * wide, wide), wide)
+            sums = dot_nt(grad[rows], qkv[cols]).astype(bfloat)
+            line.parts[chip, :, :, cols] = sums.reshape(2, line.tok, wide)
+
+        line.core_copy(chip).start()
+        if step > 0:
+            line.scatter_first(line.order(chips - step))
+    line.scatter_first(line.order(0))
+    store_grad = pltpu.make_async_copy(grad, grad_hbm, store_sem.at[1])
+    store_grad.start()
+    gateup.middle()
+    line.scatter_rest(result_ref)
+    down.middle()
+    gateup.finish()
+    down.finish()
+    stores = []
+    for at, (share, kept) in enumerate(((gateup, gateup_kept), (down, down_kept))):
+        for half in (0, 1):
+            stores.append(
+                pltpu.make_async_copy(
+                    share.own_rows(half), kept.at[half], store_sem.at[2 + 2 * at + half]
+                )
+            )
+    for store in stores:
+        store.start()
+    line.gather_end()
+    for share in shares:
+        share.sum_sent()
+
+    @pl.when(ctx_at > 0)
+    def _():
+        to_before.wait_send()
+
+    store_all.wait()
+    store_grad.wait()
+    for store in stores:
+        store.wait()
+
+
+def attention_backward(
+    own,
+    out,
+    qkv,
+    lin,
+    query,
+    span,
+    probs,
+    cosine,
+    sine_part,
+    gain_query,
+    gain_key,
+    part_gateup,
+    part_down,
+):
+    tok_count, width = own.shape
+    members = part_gateup.shape[0]
+    chips = members // 2
+    block = members * tok_count
+    bfloat = jnp.bfloat16
+    anywhere = pl.BlockSpec(memory_space=pl.ANY)
+    vmem = pl.BlockSpec(memory_space=pltpu.VMEM)
+    dma = pltpu.SemaphoreType.DMA
+    eighth = part_gateup.shape[1] // 8
+    outputs = [
+        ((tok_count, width), jnp.float32),
+        ((chips, 2, tok_count, width), bfloat),
+        ((block, 3 * HD), bfloat),
+        ((2, HD), jnp.float32),
+        ((2, members, eighth, part_gateup.shape[2]), bfloat),
+        ((2, part_down.shape[0] // 8, part_down.shape[1]), bfloat),
+    ]
+    half_span = (2, WINDOW // 2, HD)
+    return pl.pallas_call(
+        functools.partial(attention_backward_kernel, chips),
+        out_shape=[jax.ShapeDtypeStruct(*output) for output in outputs],
+        in_specs=[vmem] + [anywhere] * 6 + [vmem] * 4 + [anywhere] * 2,
+        out_specs=[vmem, anywhere, anywhere, vmem, anywhere, anywhere],
+        scratch_shapes=line_scratch(chips, tok_count, width)
+        + sum_scratch(part_gateup.shape)
+        + sum_scratch(part_down.shape)
+        + [pltpu.VMEM(one.shape, one.dtype) for one in (out, qkv, lin, query, span, probs)]
+        + [
+            pltpu.VMEM((block, 3 * HD), bfloat),
+            pltpu.VMEM(span.shape, jnp.float32),
+            pltpu.VMEM(half_span, bfloat),
+            pltpu.VMEM(half_span, bfloat),
+            pltpu.VMEM(half_span, bfloat),
+            dma((6,)),
+            dma((6,)),
+            dma((2,)),
+            dma((2,)),
+            pltpu.VMEM((block, HD), bfloat),
+        ],
+        compiler_params=pltpu.CompilerParams(
+            collective_id=5, has_side_effects=True, vmem_limit_bytes=KERNEL_VMEM
+        ),
+        cost_estimate=pl.CostEstimate(
+            flops=8 << 30, bytes_accessed=300 << 20, transcendentals=0
+        ),
+        name="attention_backward",
+    )(
+        own,
+        out,
+        qkv,
+        lin,
+        query,
+        span,
+        probs,
+        cosine,
+        sine_part,
+        gain_query,
+        gain_key,
+        part_gateup,
+        part_down,
+    )
 
 def by_heads(
     tokens,
@@ -1288,7 +1867,6 @@
     chips = fsdp_count // 2
     rows = w_query.shape[0]
     ff_part = w_gate.shape[1] // fsdp_count
-    scale_factor = 1.0 / math.sqrt(HD)
     ctx_at = lax.axis_index("ctx")
     fsdp_at = lax.axis_index("fsdp")
 
@@ -1304,23 +1882,35 @@
     ]
     gain_sizes = [g.shape[0] for g in gain_list]
     gain_offsets = [sum(gain_sizes[:n]) for n in range(len(gain_sizes) + 1)]
-    all_gains = lax.all_gather(jnp.concatenate(gain_list), "fsdp", axis=0, tiled=False)
+    packed = jnp.concatenate(gain_list + [positions.astype(jnp.float32)])
+    packed = jnp.pad(packed, (0, -packed.shape[0] % 1024)).reshape(1, -1, 128)
+    packed = lax.all_gather(packed, "fsdp", axis=0, tiled=True).reshape(fsdp_count, -1)
     gain_in, gain_query, gain_key, gain_post, gain_laurel, gain_ffin, gain_ffout, gain_ple = (
-        all_gains[:, gain_offsets[n] : gain_offsets[n + 1]].reshape(-1) for n in range(8)
-    )
-    block_positions = lax.all_gather(positions, "fsdp", axis=0, tiled=True)
+        packed[:, gain_offsets[n] : gain_offsets[n + 1]].reshape(-1) for n in range(8)
+    )
+    block_positions = packed[:, gain_offsets[8] : gain_offsets[8] + tok_count].reshape(-1)
     cosine, sine_part = rope_tables(block_positions, HD)
     cosine, sine_part = cosine[:, 0], sine_part[:, 0]
 
-    query_parts = w_query.reshape(rows, fsdp_count, HD)
     group_size = HQ // KV
-    key_parts = jnp.repeat(w_key.reshape(rows, KV, HD), group_size, axis=1)
-    value_parts = jnp.repeat(w_value.reshape(rows, KV, HD), group_size, axis=1)
-    col_qkv = to_columns([query_parts, key_parts, value_parts], ctx_count)
-    col_gateup = to_columns(
-        [w_gate.reshape(rows, fsdp_count, ff_part), w_up.reshape(rows, fsdp_count, ff_part)],
-        ctx_count,
-    )
+    eighth = rows // 8
+    at_x, at_y = ctx_at % 2, ctx_at // 2
+
+    def own_rows(weight, width):
+        starts = (at_x * 2 + at_y, 4 + at_y * 2 + at_x)
+        halves = [lax.dynamic_slice_in_dim(weight, n * eighth, eighth, 0) for n in starts]
+        held = jnp.stack(halves).astype(bfloat)
+        return jnp.transpose(held.reshape(2, eighth, -1, width), (0, 2, 1, 3))
+
+    qkv_own = jnp.concatenate(
+        [
+            own_rows(w_query, HD),
+            jnp.repeat(own_rows(w_key, HD), group_size, axis=1),
+            jnp.repeat(own_rows(w_value, HD), group_size, axis=1),
+        ],
+        axis=3,
+    )
+    gate_own, up_own = own_rows(w_gate, ff_part), own_rows(w_up, ff_part)
     out_low = w_out.astype(bfloat)
     down_low = w_down.astype(bfloat)
     full_left, full_right, full_pgate, full_pproj = (
@@ -1332,35 +1922,27 @@
     ple_input = per_layer.astype(jnp.float32)
     normed, norm_back = jax.vjp(rms_norm, inputs, gain_in)
     normed_low = normed.astype(bfloat)
-    normed_all = gather_tokens(normed_low)
-    qkv_lin = matmul(normed_all, col_qkv)
-    query_lin, key_lin, value_lin = qkv_lin[:, :HD], qkv_lin[:, HD : 2 * HD], qkv_lin[:, 2 * HD :]
-    rope_here = functools.partial(head_rope, cosine, sine_part)
-    query_rot, query_back = jax.vjp(rope_here, query_lin, gain_query)
-    key_rot, key_back = jax.vjp(rope_here, key_lin, gain_key)
-    query_low = query_rot.astype(bfloat)
-    own_kv = jnp.stack([key_rot.astype(bfloat), value_lin.astype(bfloat)])
-    before_kv = passed_along(own_kv[:, block_len - WINDOW :], "ctx", 1)
-    span_kv = jnp.concatenate([before_kv, own_kv], axis=1)
-
-    chunk = 256
-    span_len = WINDOW + chunk
     block_start = ctx_at * block_len
-    prob_list, attended_list = [], []
-    for begin in range(0, block_len, chunk):
-        visible = visibility(
-            doc_lengths, block_start + begin, block_start + begin - WINDOW, chunk, span_len
+    places = block_start - WINDOW + jnp.arange(WINDOW + block_len, dtype=jnp.int32)
+    key_docs = jnp.where(places >= 0, document_ids(doc_lengths, places), -1)
+    projected, normed_all, qkv_full, gateup_full, qk_lin, query_low, span_kv, probs, attended_low = (
+        attention_forward(
+            normed_low,
+            qkv_own,
+            gate_own,
+            up_own,
+            out_low,
+            cosine,
+            sine_part,
+            gain_query[None, :],
+            gain_key[None, :],
+            key_docs[WINDOW:, None],
+            key_docs[None, :],
         )
-        keys = span_kv[0, begin : begin + span_len]
-        values = span_kv[1, begin : begin + span_len]
-        scores = matmul_nt(query_low[begin : begin + chunk], keys) * scale_factor
-        scores = jnp.where(visible, scores, NEGATIVE)
-        shifted = jnp.exp(scores - jnp.max(scores, axis=-1, keepdims=True))
-        probs = shifted / jnp.sum(shifted, axis=-1, keepdims=True)
-        prob_list.append(probs)
-        attended_list.append(matmul(probs.astype(bfloat), values))
-    attended_low = jnp.concatenate(attended_list, axis=0).astype(bfloat)
-    projected = scatter_tokens(matmul(attended_low, out_low))
+    )
+    normed_all = normed_all.reshape(block_len, -1)
+    col_qkv = qkv_full.reshape(normed_all.shape[1], -1)
+    col_gateup = gateup_full.reshape(normed_all.shape[1], -1)
     narrow_low = matmul(normed_low, full_left).astype(bfloat)
     widened = matmul(narrow_low, full_right)
     mixed, mix_back = jax.vjp(mix_piece, inputs, normed, projected, widened, gain_post, gain_laurel)
@@ -1395,41 +1977,31 @@
     grad_in_first, grad_normed, grad_proj, grad_lwide, grad_gpost, grad_glaurel = mix_back(
         grad_mixed
     )
-    grad_proj_all = gather_tokens(grad_proj.astype(bfloat))
-    part_wout = matmul_tn(attended_low, grad_proj_all).astype(bfloat)
-    grad_att_low = matmul_nt(grad_proj_all, out_low).astype(bfloat)
     grad_lwide_low = grad_lwide.astype(bfloat)
     part_right = matmul_tn(narrow_low, grad_lwide_low)
     grad_narrow_low = matmul_nt(grad_lwide_low, full_right).astype(bfloat)
     part_left = matmul_tn(normed_low, grad_narrow_low)
     grad_normed = grad_normed + matmul_nt(grad_narrow_low, full_left)
 
-    grad_query_list = []
-    grad_keys = jnp.zeros((WINDOW + block_len, HD), jnp.float32)
-    grad_values = jnp.zeros((WINDOW + block_len, HD), jnp.float32)
-    for at, begin in enumerate(range(0, block_len, chunk)):
-        keys = span_kv[0, begin : begin + span_len]
-        values = span_kv[1, begin : begin + span_len]
-        probs = prob_list[at]
-        grad_rows = grad_att_low[begin : begin + chunk]
-        grad_probs = matmul_nt(grad_rows, values)
-        inner_sum = jnp.sum(probs * grad_probs, axis=-1, keepdims=True)
-        grad_scores = (probs * (grad_probs - inner_sum)).astype(bfloat)
-        grad_query_list.append(matmul(grad_scores, keys) * scale_factor)
-        grad_keys = grad_keys.at[begin : begin + span_len].add(
-            matmul_tn(grad_scores, query_low[begin : begin + chunk]) * scale_factor
+    grad_normed_more, grad_proj_all, grad_qkv_low, grad_head_gains, held_gateup, held_wdown = (
+        attention_backward(
+            grad_proj.astype(bfloat),
+            out_low,
+            col_qkv,
+            qk_lin,
+            query_low,
+            span_kv,
+            probs,
+            cosine,
+            sine_part,
+            gain_query[None, :],
+            gain_key[None, :],
+            part_gateup,
+            part_wdown,
         )
-        grad_values = grad_values.at[begin : begin + span_len].add(
-            matmul_tn(probs.astype(bfloat), grad_rows)
-        )
-    returned = passed_along(
-        jnp.stack([grad_keys[:WINDOW], grad_values[:WINDOW]]).astype(bfloat), "ctx", -1
-    ).astype(jnp.float32)
-    returned = jnp.pad(returned, ((0, 0), (block_len - WINDOW, 0), (0, 0)))
-    grad_qlin, grad_gquery = query_back(jnp.concatenate(grad_query_list, axis=0))
-    grad_klin, grad_gkey = key_back(grad_keys[WINDOW:] + returned[0])
-    grad_vlin = grad_values[WINDOW:] + returned[1]
-    grad_qkv_low = jnp.concatenate([grad_qlin, grad_klin, grad_vlin], axis=1).astype(bfloat)
+    )
+    grad_gquery, grad_gkey = grad_head_gains[0], grad_head_gains[1]
+    part_wout = matmul_tn(attended_low, grad_proj_all.reshape(block_len, -1)).astype(bfloat)
     part_qkv = matmul_tn(normed_all, grad_qkv_low).astype(bfloat).reshape(fsdp_count, rows, -1)
     small_parts = [
         part.astype(bfloat).reshape(fsdp_count, -1, inputs.shape[1])
@@ -1444,7 +2016,7 @@
     small = lax.psum_scatter(
         jnp.concatenate(small_parts, axis=1), "fsdp", scatter_dimension=0, tiled=False
     )
-    grad_normed = grad_normed + scatter_tokens(matmul_nt(grad_qkv_low, col_qkv))
+    grad_normed = grad_normed + grad_normed_more
     grad_in_second, grad_gin = norm_back(grad_normed)
     grad_tokens = grad_in_first + grad_in_second
 
@@ -1463,7 +2035,7 @@
     gain_parts = gain_parts.astype(bfloat).reshape(fsdp_count, 128, 128)
 
     sum_wgate, sum_wup, sum_wdown, sum_wout, sum_qkv, sum_small, sum_gains = gradient_sum(
-        [part_gateup, part_wdown, part_wout, part_qkv, small, gain_parts]
+        [held_gateup, held_wdown], [part_wout, part_qkv, small, gain_parts]
     )
     gain_sums = jnp.sum(sum_gains.astype(jnp.float32), axis=0).reshape(-1)
     grad_wgate = sum_wgate.astype(jnp.float32)

time: 1130 us -> 898 us (0.79)
  waiting for transfers between devices: 231 us -> 0.09 us
  Pallas kernels: 481 us -> 679 us
  blocking collectives: 161 us -> 44.8 us
  local copies, waits for them, and re-layouts: 75.6 us -> 40.6 us
  matrix products: 73.3 us -> 44.2 us
    pallas_call x1 -> x3, Pallas kernels: 297 us -> 508 us  [the longest x1 189 us: gradient_sum(): pl.pallas_call(functools.partial(gradient_sum_kernel, held_columns, colum...]
    all_gather x4 -> x0, waiting for transfers between devices: 136 us -> none  [the longest x2 91.5 us: gather_tokens(): return lax.all_gather(part, 'fsdp', axis=0, tiled=True)]
    all_to_all x2 -> x0, blocking collectives: 97 us -> none  [to_columns(): lax.all_to_all(mine, 'fsdp', split_axis=1, concat_axis=0, tiled=False)]
    reduce_scatter x1, waiting for transfers between devices: 47 us -> 0.01 us  [by_heads(): lax.psum_scatter(jnp.concatenate(small_parts, axis=1), 'fsdp', scatter_di...]
    ppermute x2 -> x0, waiting for transfers between devices: 45.1 us -> none  [passed_along(): return lax.ppermute(block, axis, route)]
    unnamed x324 -> x153, local copies, waits for them, and re-layouts: 43 us -> 14.5 us
    unnamed x1 -> x0, blocking collectives: 27.2 us -> none
    dot_general x14 -> x4, matrix products: 19.7 us -> 4.9 us  [matmul_nt(): lax.dot_general(left_mat, right_mat, (((1,), (1,)), ((), ())), preferred_...]
  transfers between devices with their start and end apart: 11 -> 3, of which waited for: 8 -> 0; matrix products, arithmetic and copies ran while one was open for 9% -> 9% of each run, Pallas kernels for 9% -> 46%
where the time goes in v4:
time: 898 us; the launch traced here: 890 us
  Pallas kernels  679 us (76%)
  other arithmetic  65.7 us (7%)
  blocking collectives  44.8 us (5%)
  matrix products  44.2 us (5%)
  local copies, waits for them, and re-layouts  40.6 us (5%)
  between operations  15.3 us (2%)
    pallas_call x1, Pallas kernels, gradient_sum(): pl.pallas_call(functools.partial(gradient_sum_kernel, held_columns, colum...  189 us
    pallas_call x1, Pallas kernels, attention_forward(): pl.pallas_call(functools.partial(attention_forward_kernel, chips), out_sh...  174 us
    pallas_call x1, Pallas kernels, attention_backward(): pl.pallas_call(functools.partial(attention_backward_kernel, chips), out_s...  145 us
    pallas_call x1, Pallas kernels, ffn_forward(): pl.pallas_call(functools.partial(ffn_forward_kernel, chips), out_shape=[j...  87.2 us
    pallas_call x1, Pallas kernels, ffn_backward(): pl.pallas_call(functools.partial(ffn_backward_kernel, chips), out_shape=[...  84.3 us
    dot_general x8, matrix products, matmul_tn(): lax.dot_general(left_mat, right_mat, (((0,), (0,)), ((), ())), preferred_...  34.9 us
    all_gather x2, blocking collectives, by_heads(): lax.all_gather(w.astype(bfloat), 'fsdp', axis=0, tiled=True)  29.1 us
  transfers between devices with their start and end apart: 3, of which 0 were waited for; matrix products, arithmetic and copies ran while one was open for 9% of the time, Pallas kernels for 46%

profile of v4, /device:TPU:0, one launch (start us, length us, event | category | flops | bytes accessed | tf_op | source)
XLA Modules:
  0.0 889.8 jit_solution(13614251823921023954)
XLA Ops:
  12.9 15.7 %all_gather.15 = f32[8,16,128]{2,1,0:T(8,128)S(1)} all-gather(f32[1,16,128]{2,1,0:T(8,128)S(1)} %pad_bitcast_fusion.1), channel_id=1, replica_groups=mesh['ctx'=4,'fsdp'=8] {'fsdp'}, dimensions={0}, use_global_device_ids=true | all-gather | bytes 73728 | tf_op jit(solution)/shard_map/all_gather | solution.py:1887
  40.6 14.8 %all_gather.17 = bf16[64,2048]{1,0:T(8,128)(2,1)S(1)} all-gather(bf16[8,2048]{1,0:T(8,128)(2,1)S(1)} %convert_element_type.136), channel_id=1, replica_groups=mesh['ctx'=4,'fsdp'=8] {'fsdp'}, dimensions={0}, use_global_device_ids=true | all-gather | bytes 294912 | tf_op jit(solution)/shard_map/all_gather | solution.py:1917
  55.4 14.3 %all_gather.16 = bf16[2048,64]{0,1:T(8,128)(2,1)S(1)} all-gather(bf16[256,64]{0,1:T(8,128)(2,1)S(1)} %convert_element_type.134), channel_id=1, replica_groups=mesh['ctx'=4,'fsdp'=8] {'fsdp'}, dimensions={0}, use_global_device_ids=true | all-gather | bytes 294912 | tf_op jit(solution)/shard_map/all_gather | solution.py:1917
  76.1 2.4 dynamic-slice_convert_fusion.1
  81.1 2.7 convert_element_type.138.down_hbm
  83.8 3.0 multiply_sine_fusion
  90.0 174.0 %attention_forward.1 = (f32[128,2048]{1,0:T(8,128)}, bf16[4,2,128,2048]{3,2,1,0:T(8,128)(2,1)}, bf16[8,256,768]{2,1,0:T(8,128)(2,1)}, bf16[8,256,2048]{2,1,0:T(8...) custom-call(bf16[128,2048]{1,0:T(8,128)(2,1)} %copy-done.9, ...), custom_call_target="tpu_custom_call" | custom-call | flops 8589934592 | bytes 314572800 | tf_op jit(solution)/shard_map/attention_forward/pallas_call | solution.py:1542
  265.4 1.8 multiply_reduce_fusion.10
  268.7 87.2 %ffn_forward.1 = (f32[128,2048]{1,0:T(8,128)}, bf16[4,2,128,2048]{3,2,1,0:T(8,128)(2,1)}, bf16[1024,1024]{1,0:T(8,128)(2,1)}, bf16[1024,1024]{1,0:T(8,128)(2,1)}, bf16[1024,1024]{1,0:T(8,128)(2,1)}) custom-call(bf16[128,2048]{1,0:T(8,128)(2,1)} %multiply_convert_fusion.own_ref, bf16[2048,2048]{1,0:T(8,128)(2,1)} %bitcast.168, ...), custom_call_target="tpu_custom_call" | custom-call | flops 12884901888 | bytes 41943040 | tf_op jit(solution)/shard_map/ffn_forward/pallas_call | solution.py:788
  360.1 1.9 fusion.22
  362.1 1.8 multiply_reduce_fusion.8
  363.9 2.0 fusion.12
  366.0 2.6 fusion.13
  374.3 2.3 reshape.349
  376.6 2.3 fusion.14.own_ref
  379.0 84.3 %ffn_backward.1 = (f32[128,2048]{1,0:T(8,128)}, bf16[4,2,128,2048]{3,2,1,0:T(8,128)(2,1)}, bf16[1024,2048]{1,0:T(8,128)(2,1)}) custom-call(bf16[128,2048]{1,0:T(8,128)(2,1)} %fusion.14.own_ref, bf16[2048,2048]{1,0:T(8,128)(2,1)} %bitcast.169, bf16[1024,2048]{1,0:T(8,128)(2,1)} %convert_element_type.138.down_hbm, ...), custom_call_target="tpu_custom_call" | custom-call | flops 12884901888 | bytes 41943040 | tf_op jit(solution)/shard_map/ffn_backward/pallas_call | solution.py:911
  464.9 2.7 multiply_reduce_fusion.2
  470.1 2.3 constant_dynamic-update-slice_fusion.2
  476.6 9.6 %convolution_convert_fusion.1.down_hbm = bf16[1024,2048]{1,0:T(8,128)(2,1)} fusion(bf16[1024,1024]{1,0:T(8,128)(2,1)} %get-tuple-element.65, bf16[1024,2048]{1,0:T(8,128)(2,1)} %bitcast.173), kind=kOutput, calls=%fused_computation.2 | convolution fusion | flops 4297064448 | bytes 10485760 | tf_op jit(solution)/shard_map/dot_general | solution.py:38
  486.2 11.6 %convolution_convert_fusion = bf16[2048,2048]{1,0:T(8,128)(2,1)} fusion(bf16[1024,2048]{1,0:T(8,128)(2,1)S(1)} %bitcast.172, bf16[1024,2048]{1,0:T(8,128)(2,1)S(1)} %copy-done.62), kind=kOutput, calls=%fused_computation | convolution fusion | flops 8594128896 | bytes 16777216 | tf_op jit(solution)/shard_map/dot_general | solution.py:38
  497.8 145.0 %attention_backward.1 = (f32[128,2048]{1,0:T(8,128)}, bf16[4,2,128,2048]{3,2,1,0:T(8,128)(2,1)}, bf16[1024,768]{1,0:T(8,128)(2,1)}, f32[2,256]{1,0:T(2,128)}, bf...) custom-call(bf16[128,2048]{1,0:T(8,128)(2,1)} %get-tuple-element.222.own_ref, ...), custom_call_target="tpu_custom_call" | custom-call | flops 8589934592 | bytes 314572800 | tf_op jit(solution)/shard_map/attention_backward/pallas_call | solution.py:1792
  642.8 1.8 fusion.10
  646.4 4.7 convolution_convert_fusion.5.refs_2_
  652.5 4.9 convolution_convert_fusion.2
  657.4 188.6 %gradient_sum.1 = (bf16[256,8192]{1,0:T(8,128)(2,1)}, bf16[256,8192]{1,0:T(8,128)(2,1)}, bf16[1024,2048]{1,0:T(8,128)(2,1)}, bf16[256,2048]{1,0:T(8,128)(2,1)}, ...) custom-call(bf16[2,8,32,2048]{3,2,1,0:T(8,128)(2,1)} %get-tuple-element.68.refs_0_, ...), custom_call_target="tpu_custom_call" | custom-call | bytes 314572800 | tf_op jit(solution)/shard_map/gradient_sum/pallas_call | solution.py:1290
  851.9 2.4 convert_element_type.160
  857.3 2.8 convert_element_type.161
  860.1 1.8 copy.103
  861.9 2.9 copy.106
  867.3 6.7 convert_element_type.163
  874.0 4.4 convert_element_type.164
  878.4 4.4 convert_element_type.165
  (261 shorter events, 64.8 us)
Async XLA Ops:
  7.2 66.1 %copy-start.17 = (f32[256,2048]{1,0:T(8,128)S(1)}, f32[256,2048]{1,0:T(8,128)}, u32[]{:S(2)}) copy-start(f32[256,2048]{1,0:T(8,128)} %param.32) | copy-start | bytes 6291460
  7.2 352.9 %all-gather.3.cloned.1.call-start = ((), (), s32[]{:S(2)}) async-start(), calls=%async_computation.1 | async-start | bytes 1179648 | tf_op jit(solution)/shard_map/all_gather | solution.py:1917
  9.0 353.0 %all-gather.5.cloned.1.call-start = ((), (), s32[]{:S(2)}) async-start(), calls=%async_computation.2 | async-start | bytes 1179648 | tf_op jit(solution)/shard_map/all_gather | solution.py:1917
  10.7 63.7 %copy-start.6 = (bf16[128,2048]{1,0:T(8,128)(2,1)S(1)}, bf16[128,2048]{1,0:T(8,128)(2,1)}, u32[]{:S(2)}) copy-start(bf16[128,2048]{1,0:T(8,128)(2,1)} %param.24) | copy-start | bytes 1572868
  10.7 646.6 %reduce-scatter.2.cloned.1.call-start = ((), (), s32[]{:S(2)}) async-start(), calls=%async_computation.3 | async-start | bytes 4718592 | tf_op jit(solution)/shard_map/reduce_scatter | solution.py:2016
  31.2 6.8 copy-start.49
  55.4 20.7 %copy-start.15 = (bf16[64,2048]{1,0:T(8,128)(2,1)}, bf16[64,2048]{1,0:T(8,128)(2,1)S(1)}, u32[]{:S(2)}) copy-start(bf16[64,2048]{1,0:T(8,128)(2,1)S(1)} %all_gather.17) | copy-start | bytes 786436
  76.1 189.2 %copy-start.41 = (f32[128]{0:T(128)}, f32[128]{0:T(128)S(1)}, u32[]{:S(2)}) copy-start(f32[128]{0:T(128)S(1)} %fusion.35) | copy-start | bytes 1540
  90.0 175.4 %copy-start.30 = (f32[1,2,8,128]{3,1,2,0:T(2,128)S(1)}, f32[1,2,8,128]{3,1,2,0:T(2,128)}, u32[]{:S(2)}) copy-start(f32[1,2,8,128]{3,1,2,0:T(2,128)} %copy.119) | copy-start | bytes 24580
  90.0 175.4 %copy-start.31 = (f32[1,2,8,128]{3,1,2,0:T(2,128)S(1)}, f32[1,2,8,128]{3,1,2,0:T(2,128)}, u32[]{:S(2)}) copy-start(f32[1,2,8,128]{3,1,2,0:T(2,128)} %copy.118) | copy-start | bytes 24580
  90.0 175.4 %copy-start.36 = (f32[128]{0:T(128)S(1)}, f32[128]{0:T(128)}, u32[]{:S(2)}) copy-start(f32[128]{0:T(128)} %fusion.33) | copy-start | bytes 1540
  265.3 90.6 %copy-start.52 = (f32[128]{0:T(128)}, f32[128]{0:T(128)S(1)}, u32[]{:S(2)}) copy-start(f32[128]{0:T(128)S(1)} %multiply_reduce_fusion.12) | copy-start | bytes 1540
  267.2 88.7 %copy-start.55 = (f32[128]{0:T(128)}, f32[128]{0:T(128)S(1)}, u32[]{:S(2)}) copy-start(f32[128]{0:T(128)S(1)} %get-tuple-element.209) | copy-start | bytes 1540
  268.7 87.3 %copy-start.33 = (f32[1,2,8,128]{3,2,1,0:T(8,128)S(1)}, f32[1,2,8,128]{3,2,1,0:T(8,128)}, u32[]{:S(2)}) copy-start(f32[1,2,8,128]{3,2,1,0:T(8,128)} %get-tuple-element.240) | copy-start | bytes 24580
  268.7 87.9 %copy-start.32 = (f32[1,2,8,128]{3,2,1,0:T(8,128)S(1)}, f32[1,2,8,128]{3,2,1,0:T(8,128)}, u32[]{:S(2)}) copy-start(f32[1,2,8,128]{3,2,1,0:T(8,128)} %get-tuple-element.241) | copy-start | bytes 24580
  362.1 8.0 copy-start.18
  365.9 6.8 copy-start
  365.9 6.8 copy-start.13
  365.9 6.8 copy-start.26
  378.9 84.3 %copy-start.46 = (f32[128]{0:T(128)S(1)}, f32[128]{0:T(128)}, u32[]{:S(2)}) copy-start(f32[128]{0:T(128)} %copy-done.45) | copy-start | bytes 1540
  378.9 85.9 %copy-start.56 = (f32[128]{0:T(128)S(1)}, f32[128]{0:T(128)}, u32[]{:S(2)}) copy-start(f32[128]{0:T(128)} %copy-done.55) | copy-start | bytes 1540
  378.9 85.9 %copy-start.1 = (f32[128,2048]{1,0:T(8,128)S(1)}, f32[128,2048]{1,0:T(8,128)}, u32[]{:S(2)}) copy-start(f32[128,2048]{1,0:T(8,128)} %get-tuple-element.52) | copy-start | bytes 3145732
  378.9 85.9 %copy-start.28 = (f32[2048]{0:T(1024)S(1)}, f32[2048]{0:T(1024)}, u32[]{:S(2)}) copy-start(f32[2048]{0:T(1024)} %get-tuple-element.262) | copy-start | bytes 24580
  378.9 85.9 %copy-start.29 = (f32[2048]{0:T(1024)S(1)}, f32[2048]{0:T(1024)}, u32[]{:S(2)}) copy-start(f32[2048]{0:T(1024)} %get-tuple-element.263) | copy-start | bytes 24580
  378.9 85.9 %copy-start.42 = (f32[128]{0:T(128)S(1)}, f32[128]{0:T(128)}, u32[]{:S(2)}) copy-start(f32[128]{0:T(128)} %copy-done.41) | copy-start | bytes 1540
  378.9 85.9 %copy-start.44 = (f32[128]{0:T(128)S(1)}, f32[128]{0:T(128)}, u32[]{:S(2)}) copy-start(f32[128]{0:T(128)} %copy-done.43) | copy-start | bytes 1540
  379.0 85.9 %copy-start.54 = (f32[128]{0:T(128)S(1)}, f32[128]{0:T(128)}, u32[]{:S(2)}) copy-start(f32[128]{0:T(128)} %get-tuple-element.250) | copy-start | bytes 1540
  476.6 9.6 %copy-start.60 = (bf16[4,2,128,2048]{3,2,1,0:T(8,128)(2,1)S(1)}, bf16[4,2,128,2048]{3,2,1,0:T(8,128)(2,1)}, u32[]{:S(2)}) copy-start(bf16[4,2,128,2048]{3,2,1,0:T(8,128)(2,1)} %get-tuple-element.63) | copy-start | bytes 12582916
  476.6 9.6 %copy-start.62 = (bf16[1024,2048]{1,0:T(8,128)(2,1)S(1)}, bf16[1024,2048]{1,0:T(8,128)(2,1)}, u32[]{:S(2)}) copy-start(bf16[1024,2048]{1,0:T(8,128)(2,1)} %get-tuple-element.64) | copy-start | bytes 12582916
  497.8 145.0 %copy-start.3 = (f32[128,2048]{1,0:T(8,128)S(1)}, f32[128,2048]{1,0:T(8,128)}, u32[]{:S(2)}) copy-start(f32[128,2048]{1,0:T(8,128)} %copy-done.2) | copy-start | bytes 3145732
  497.8 145.0 %copy-start.7 = (bf16[128,2048]{1,0:T(8,128)(2,1)S(1)}, bf16[128,2048]{1,0:T(8,128)(2,1)}, u32[]{:S(2)}) copy-start(bf16[128,2048]{1,0:T(8,128)(2,1)} %param.24) | copy-start | bytes 1572868
  497.8 145.0 %copy-start.37 = (f32[128]{0:T(128)S(1)}, f32[128]{0:T(128)}, u32[]{:S(2)}) copy-start(f32[128]{0:T(128)} %fusion.33) | copy-start | bytes 1540
  (36 other events, 152.5 us)
Sparse Core Ops, SparseCore 0:
  10.2 24.9 all-gather.2
  37.4 23.0 all-gather.4
  476.6 59.8 reduce-scatter.1

commit v5 on v4

--- a/solution.py
+++ b/solution.py
@@ -1,3 +1,4 @@
+import dataclasses
 import functools
 import math
 
@@ -21,7 +22,7 @@
 GELU_ROOT = math.sqrt(2.0 / math.pi)
 GELU_CUBE = 0.044715
 SCORE_SCALE = 1.0 / math.sqrt(HD)
-KERNEL_VMEM = 60 << 20
+KERNEL_VMEM = 62 << 20
 
 
 def passed_along(block, axis, distance):
@@ -409,6 +410,427 @@
         wide_part(sum_gple),
     )
 
+class Plane:
+    def locate(self, columns, rows):
+        self.columns = columns
+        at = lax.axis_index("ctx")
+        self.at_x, self.at_y = at % 2, at // 2
+        self.beside = (at + 1 - 2 * (at % 2), (at + 2) % 4)
+        self.me = lax.axis_index("fsdp")
+        self.members = lax.axis_size("fsdp")
+        self.half = rows // 2
+        self.quarter = rows // 4
+        self.eighth = rows // 8
+
+    def rows(self, ref, start, size):
+        start = pl.multiple_of(start, size)
+        return ref.at[:, pl.ds(start, size)] if self.columns else ref.at[pl.ds(start, size)]
+
+    def sides(self, half):
+        return (self.at_x, self.at_y) if half == 0 else (self.at_y, self.at_x)
+
+    def kept_start(self, half):
+        return half * self.half + self.sides(half)[0] * self.quarter
+
+    def given_start(self, half):
+        return half * self.half + (1 - self.sides(half)[0]) * self.quarter
+
+    def own_start(self, half):
+        return self.kept_start(half) + self.sides(half)[1] * self.eighth
+
+    def copy(self, src, dst, send_sem, recv_sem, half, stage):
+        return pltpu.make_async_remote_copy(
+            src_ref=src,
+            dst_ref=dst,
+            send_sem=send_sem.at[half, stage],
+            recv_sem=recv_sem.at[half, stage],
+            device_id={"ctx": self.beside[(half + stage) % 2]},
+            device_id_type=pl.DeviceIdType.MESH,
+        )
+
+
+class Summed(Plane):
+    def __init__(self, source, refs, columns):
+        self.source = source
+        self.kept, self.taken, self.last, self.load_sem, self.sum_send, self.sum_recv = refs
+        self.locate(columns, source.shape[-2])
+
+    def load(self, half):
+        return pltpu.make_async_copy(
+            self.rows(self.source, self.kept_start(half), self.quarter),
+            self.kept.at[half],
+            self.load_sem.at[half],
+        )
+
+    def first(self, half):
+        return self.copy(
+            self.rows(self.source, self.given_start(half), self.quarter),
+            self.taken.at[half],
+            self.sum_send,
+            self.sum_recv,
+            half,
+            0,
+        )
+
+    def second(self, half):
+        other = (1 - self.sides(half)[1]) * self.eighth
+        return self.copy(
+            self.rows(self.kept.at[half], other, self.eighth),
+            self.last.at[half],
+            self.sum_send,
+            self.sum_recv,
+            half,
+            1,
+        )
+
+    def begin(self):
+        for half in (0, 1):
+            self.first(half).start()
+            self.load(half).start()
+
+    def add(self, half, start, more, more_start):
+        step = min(32, self.eighth)
+        blocks = self.eighth // step
+        layers = self.source.shape[0] if self.columns else 1
+
+        @pl.loop(0, layers * blocks)
+        def _(at):
+            layer, block = at // blocks, at % blocks
+            here = pl.ds(pl.multiple_of(start + block * step, step), step)
+            there = pl.ds(pl.multiple_of(more_start + block * step, step), step)
+            if self.columns:
+                self.kept[half, layer, here] += more[half, layer, there]
+            else:
+                self.kept[half, here] += more[half, there]
+
+    def middle(self):
+        for half in (0, 1):
+            self.load(half).wait()
+            self.first(half).wait_recv()
+            side = self.sides(half)[1]
+            other = (1 - side) * self.eighth
+            self.add(half, other, self.taken, other)
+            self.second(half).start()
+            mine = side * self.eighth
+            self.add(half, mine, self.taken, mine)
+
+    def finish(self):
+        for half in (0, 1):
+            self.second(half).wait_recv()
+            self.add(half, self.sides(half)[1] * self.eighth, self.last, 0)
+
+    def own_rows(self, half):
+        return self.rows(self.kept.at[half], self.sides(half)[1] * self.eighth, self.eighth)
+
+    def held(self, half, member):
+        side = self.sides(half)[1] * self.eighth
+        return self.kept.at[half, member, pl.ds(pl.multiple_of(side, self.eighth), self.eighth)]
+
+    def sum_sent(self):
+        for half in (0, 1):
+            self.first(half).wait_send()
+            self.second(half).wait_send()
+
+
+class Held:
+    def __init__(self, kept, side=0, sides=1):
+        self.kept = kept
+        width = kept.shape[-1] // sides
+        self.cols = pl.ds(side * width, width)
+
+    def own_rows(self, half):
+        return self.kept.at[half]
+
+    def held(self, half, member):
+        return self.kept.at[half, member, :, self.cols]
+
+
+class Spread(Plane):
+    def __init__(self, source, refs, columns):
+        self.own_rows, self.held = source.own_rows, source.held
+        self.final, self.spread_send, self.spread_recv, self.place_sem = refs[:4]
+        if columns:
+            self.swap_send, self.swap_recv = refs[4:]
+        self.locate(columns, self.final.shape[-2])
+
+    def place(self, half):
+        return pltpu.make_async_copy(
+            self.own_rows(half),
+            self.rows(self.final, self.own_start(half), self.eighth),
+            self.place_sem.at[half],
+        )
+
+    def place_all(self):
+        for half in (0, 1):
+            self.place(half).start()
+        for half in (0, 1):
+            self.place(half).wait()
+
+    def swap_place(self, half, member):
+        start = pl.multiple_of(self.own_start(half), self.eighth)
+        return self.final.at[member, pl.ds(start, self.eighth)]
+
+    def swap_copy(self, half, hop, src_member):
+        target = lax.rem(self.me + hop, self.members)
+        return remote(
+            self.held(half, target),
+            self.swap_place(half, src_member),
+            self.swap_send.at[hop, half],
+            self.swap_recv.at[hop, half],
+            target,
+        )
+
+    def swap_local(self, half):
+        return pltpu.make_async_copy(
+            self.held(half, self.me),
+            self.swap_place(half, self.me),
+            self.place_sem.at[half],
+        )
+
+    def swap_begin(self):
+        for half in (0, 1):
+            for hop in range(1, self.members):
+                self.swap_copy(half, hop, self.me).start()
+            self.swap_local(half).start()
+
+    def swap_end(self):
+        for half in (0, 1):
+            for hop in range(1, self.members):
+                source = lax.rem(self.me + self.members - hop, self.members)
+                self.swap_copy(half, hop, source).wait_recv()
+            self.swap_local(half).wait()
+
+    def spread_copy(self, half, stage):
+        if stage == 0:
+            rows = self.rows(self.final, self.own_start(half), self.eighth)
+        else:
+            rows = self.rows(self.final, self.kept_start(half), self.quarter)
+        return self.copy(rows, rows, self.spread_send, self.spread_recv, half, 1 - stage)
+
+    def spread_wait(self, half, stage):
+        side = self.sides(half)[1]
+        if stage == 0:
+            start = self.kept_start(half) + (1 - side) * self.eighth
+            rows = self.rows(self.final, start, self.eighth)
+        else:
+            rows = self.rows(self.final, self.given_start(half), self.quarter)
+        self.copy(rows, rows, self.spread_send, self.spread_recv, half, 1 - stage).wait_recv()
+
+    def spread_begin(self):
+        for half in (0, 1):
+            self.spread_copy(half, 0).start()
+
+    def spread_on(self):
+        for half in (0, 1):
+            self.spread_wait(half, 0)
+            self.spread_copy(half, 1).start()
+
+    def spread_end(self):
+        for half in (0, 1):
+            self.spread_wait(half, 1)
+
+    def spread_sent(self):
+        for half in (0, 1):
+            self.spread_copy(half, 0).wait_send()
+            self.spread_copy(half, 1).wait_send()
+            if self.columns:
+                for hop in range(1, self.members):
+                    self.swap_copy(half, hop, self.me).wait_send()
+
+
+class GroupSpread(Spread):
+    def __init__(self, source, refs):
+        self.landing = refs[0]
+        super().__init__(source, refs[1:], True)
+
+    def swap_place(self, half, member):
+        return self.landing.at[half, member]
+
+    def swap_end(self):
+        super().swap_end()
+        groups = self.final.shape[0]
+        size = self.landing.shape[1] // groups
+        for half in (0, 1):
+            rows = pl.ds(pl.multiple_of(self.own_start(half), self.eighth), self.eighth)
+            for group in range(groups):
+                total = self.landing[half, group * size].astype(jnp.float32)
+                for member in range(group * size + 1, (group + 1) * size):
+                    total = total + self.landing[half, member].astype(jnp.float32)
+                self.final[group, rows] = total.astype(jnp.bfloat16)
+
+
+def sum_scratch(shape):
+    dma = pltpu.SemaphoreType.DMA
+    rows, width = shape[-2:]
+
+    def buffer(count):
+        return pltpu.VMEM((2,) + shape[:-2] + (count, width), jnp.bfloat16)
+
+    buffers = [buffer(rows // 4), buffer(rows // 4), buffer(rows // 8)]
+    return buffers + [dma((2,)), dma((2, 2)), dma((2, 2))]
+
+
+SUM_REFS = 6
+
+
+def spread_scratch(shape, members=None):
+    dma = pltpu.SemaphoreType.DMA
+    scratch = [pltpu.VMEM(shape, jnp.bfloat16), dma((2, 2)), dma((2, 2)), dma((2,))]
+    if len(shape) == 3:
+        count = members or shape[0]
+        scratch += [dma((count, 2)), dma((count, 2))]
+    return scratch
+
+
+def spread_refs(columns):
+    return 6 if columns else 4
+
+
+def gradient_sum_kernel(plan, *refs):
+    refs = list(refs)
+    count = len(plan)
+    sources = refs[:count]
+    results_count = sum(max(1, one.sides) for one in plan)
+    results = refs[count : count + results_count]
+    scratch = refs[count + results_count :]
+    store_sem = scratch.pop()
+
+    def take(size):
+        taken = scratch[:size]
+        del scratch[:size]
+        return taken
+
+    sums, spreads, late = [], [], []
+    for source, one in zip(sources, plan):
+        if one.summed:
+            held = Held(source, *one.part)
+        else:
+            held = Summed(source, take(SUM_REFS), one.columns)
+            sums.append(held)
+        size = spread_refs(one.columns)
+        if one.groups:
+            spreads.append(GroupSpread(held, take(size + 1)))
+        else:
+            spreads.append(Spread(held, take(size), one.columns))
+        if not one.summed:
+            late.append(spreads[-1])
+    early = [spread for spread in spreads if spread not in late]
+    greet_all()
+
+    def stores(at):
+        final, sides = spreads[at].final, plan[at].sides
+        first = sum(max(1, one.sides) for one in plan[:at])
+        if sides == 0:
+            return [pltpu.make_async_copy(final, results[first], store_sem.at[at, 0, 0])]
+        part = final.shape[2] // sides
+        return [
+            pltpu.make_async_copy(
+                final.at[member, :, pl.ds(side * part, part)],
+                results[first + side].at[:, pl.ds(member * part, part)],
+                store_sem.at[at, side, member],
+            )
+            for member in range(final.shape[0])
+            for side in range(sides)
+        ]
+
+    def launch(spread):
+        if spread.columns:
+            spread.swap_begin()
+        else:
+            spread.place_all()
+            spread.spread_begin()
+
+    for share in sums:
+        share.begin()
+    for spread in early:
+        launch(spread)
+    for share in sums:
+        share.middle()
+    for spread in early[:1]:
+        spread.swap_end()
+        spread.spread_begin()
+    for share, spread in zip(sums, late):
+        share.finish()
+        launch(spread)
+    for spread in early[:1]:
+        spread.spread_on()
+    for spread in early[1:]:
+        spread.swap_end()
+        spread.spread_begin()
+    for spread in late:
+        if spread.columns:
+            spread.swap_end()
+            spread.spread_begin()
+        else:
+            spread.spread_on()
+    for spread in early[1:]:
+        spread.spread_on()
+    for spread in late:
+        if spread.columns:
+            spread.spread_on()
+    for at in sorted(range(count), key=lambda one: spreads[one] in early):
+        spreads[at].spread_end()
+        for store in stores(at):
+            store.start()
+    for share in sums:
+        share.sum_sent()
+    for spread in spreads:
+        spread.spread_sent()
+    for at in range(count):
+        for store in stores(at):
+            store.wait()
+
+
+@dataclasses.dataclass
+class Source:
+    array: jax.Array
+    summed: bool = False
+    part: tuple = (0, 1)
+    groups: int = 0
+    sides: int = 0
+
+    @property
+    def columns(self):
+        return self.array.ndim - self.summed == 3
+
+    @property
+    def shape(self):
+        shape = self.array.shape
+        if self.summed:
+            shape = shape[1:-2] + (8 * shape[-2], shape[-1] // self.part[1])
+        return shape
+
+
+def gradient_sum(sources):
+    members = lax.axis_size("fsdp")
+    anywhere = pl.BlockSpec(memory_space=pl.ANY)
+    scratch, results = [], []
+    for one in sources:
+        shape = one.shape
+        if not one.summed:
+            scratch += sum_scratch(shape)
+        if one.groups:
+            landing = (2, members, shape[1] // 8, shape[2])
+            scratch.append(pltpu.VMEM(landing, jnp.bfloat16))
+            shape = (one.groups,) + shape[1:]
+        scratch += spread_scratch(shape, members)
+        if one.sides == 0:
+            results.append(shape)
+        else:
+            results += [(shape[1], shape[0] * shape[2] // one.sides)] * one.sides
+    return pl.pallas_call(
+        functools.partial(gradient_sum_kernel, sources),
+        out_shape=[jax.ShapeDtypeStruct(shape, jnp.bfloat16) for shape in results],
+        in_specs=[anywhere] * len(sources),
+        out_specs=[anywhere] * len(results),
+        scratch_shapes=scratch + [pltpu.SemaphoreType.DMA((len(sources), 2, members))],
+        compiler_params=pltpu.CompilerParams(
+            collective_id=3, has_side_effects=True, vmem_limit_bytes=KERNEL_VMEM
+        ),
+        cost_estimate=pl.CostEstimate(flops=0, bytes_accessed=300 << 20, transcendentals=0),
+        name="gradient_sum",
+    )(*(one.array for one in sources))
+
 def remote(src, dst, send_sem, recv_sem, place):
     return pltpu.make_async_remote_copy(
         src_ref=src,
@@ -643,7 +1065,7 @@
         def _():
             self.flow(chip, False, False)
 
-    def scatter_rest(self, result_ref):
+    def scatter_rest(self, result_ref, between=None):
         for rank in range(3, 2 * self.chips - 2):
             right = rank - self.chip
 
@@ -656,6 +1078,9 @@
             @pl.when((self.chip < self.chips - 1) & (left < self.chip) & (left >= 0))
             def _(left=left):
                 self.flow(left, False, True)
+
+            if between is not None:
+                between(rank)
 
         own = self.chip
         self.core_copy(own).wait_recv()
@@ -824,45 +1249,61 @@
     own_ref,
     gateup_hbm,
     down_hbm,
+    hidden_hbm,
     act_hbm,
     slope_hbm,
+    inputs_hbm,
+    pgate_hbm,
+    pproj_hbm,
     result_ref,
-    all_hbm,
-    grad_hbm,
+    part_hbm,
+    down_kept,
+    pgate_kept,
+    pproj_kept,
     *scratch,
 ):
     line = Line(chips, scratch[:LINE_REFS])
-    gateup, down, act, slope, grad, load_sems, store_sems = scratch[LINE_REFS:]
+    scratch = scratch[LINE_REFS:]
+    gateup, down, hidden, act, slope, inputs, grad, part_down, staged = scratch[:9]
+    load_sems, store_sems, kept_sems = scratch[9:12]
+    share = Summed(part_down, scratch[12 : 12 + SUM_REFS], False)
+    small = [
+        Summed(pgate_hbm, scratch[12 + SUM_REFS : 12 + 2 * SUM_REFS], True),
+        Summed(pproj_hbm, scratch[12 + 2 * SUM_REFS :], True),
+    ]
     ff_part = down.shape[0]
     width = down.shape[1]
     pair = 2 * line.tok
     loads = [
-        pltpu.make_async_copy(down_hbm, down, load_sems.at[0]),
-        pltpu.make_async_copy(act_hbm, act, load_sems.at[1]),
-        pltpu.make_async_copy(slope_hbm, slope, load_sems.at[2]),
-        pltpu.make_async_copy(gateup_hbm, gateup, load_sems.at[3]),
+        pltpu.make_async_copy(src, dst, load_sems.at[at])
+        for at, (src, dst) in enumerate(
+            (
+                (down_hbm, down),
+                (act_hbm, act),
+                (slope_hbm, slope),
+                (gateup_hbm, gateup),
+                (hidden_hbm, hidden),
+                (inputs_hbm, inputs),
+            )
+        )
     ]
     for load in loads:
         load.start()
-    line.barrier()
+    greet_all()
     line.gather_begin(own_ref)
+    for one in small:
+        one.begin()
     line.own_copy(own_ref).wait()
 
-    def stores(chip):
-        rows = pl.ds(pl.multiple_of(chip * pair, pair), pair)
-        return [
-            pltpu.make_async_copy(line.slots.at[chip], all_hbm.at[chip], store_sems.at[chip, 0]),
-            pltpu.make_async_copy(grad.at[rows], grad_hbm.at[rows], store_sems.at[chip, 1]),
-        ]
-
     tile = 256
+    wide = 512
     for step in range(chips):
         if step > 0:
             line.gather_step(step)
         chip = line.order(step)
         line.gather_other(chip)
         if step == 0:
-            for load in loads:
+            for load in loads[:4]:
                 load.wait()
         rows = pl.ds(pl.multiple_of(chip * pair, pair), pair)
 
@@ -879,11 +1320,6 @@
                 jnp.bfloat16
             )
 
-        for copy in stores(chip):
-            copy.start()
-
-        wide = 512
-
         @pl.loop(0, width // wide)
         def _(at, chip=chip, rows=rows):
             cols = pl.ds(pl.multiple_of(at * wide, wide), wide)
@@ -894,413 +1330,124 @@
         if step > 0:
             line.scatter_first(line.order(step - 1))
     line.scatter_first(line.order(chips - 1))
-    line.scatter_rest(result_ref)
+    for one in small:
+        one.middle()
+    for load in loads[4:]:
+        load.wait()
+
+    block = chips * pair
+
+    def down_grads():
+        @pl.loop(0, ff_part // tile)
+        def _(at):
+            rows = pl.ds(pl.multiple_of(at * tile, tile), tile)
+            left = hidden[:, rows]
+            for start in range(0, width, wide):
+                right = line.slots[:, :, :, start : start + wide].reshape(block, wide)
+                part_down[rows, start : start + wide] = dot_tn(left, right).astype(jnp.bfloat16)
+
+    def part_store(at):
+        slot = at % 2
+        return pltpu.make_async_copy(
+            staged.at[slot], part_hbm.at[at], store_sems.at[slot]
+        )
+
+    def gateup_grads(first, last):
+        @pl.loop(first, last)
+        def _(at):
+            cols = pl.ds(pl.multiple_of(at * tile, tile), tile)
+
+            @pl.when(at >= 2)
+            def _():
+                part_store(at - 2).wait()
+
+            left = inputs[:, cols]
+            for start in range(0, 2 * ff_part, wide):
+                staged[at % 2, :, start : start + wide] = dot_tn(
+                    left, grad[:, start : start + wide]
+                ).astype(jnp.bfloat16)
+            part_store(at).start()
+
+    tiles = width // tile
+    done = [0]
+
+    def between(rank):
+        if rank == 3:
+            down_grads()
+            share.begin()
+            for one in small:
+                one.finish()
+        else:
+            upto = min(tiles, done[0] + 2)
+            gateup_grads(done[0], upto)
+            done[0] = upto
+
+    line.scatter_rest(result_ref, between)
+    share.middle()
+    gateup_grads(done[0], tiles)
+    share.finish()
+    stores = [
+        pltpu.make_async_copy(one.own_rows(half), kept.at[half], kept_sems.at[at, half])
+        for at, (one, kept) in enumerate(
+            ((share, down_kept), (small[0], pgate_kept), (small[1], pproj_kept))
+        )
+        for half in (0, 1)
+    ]
+    for store in stores:
+        store.start()
     line.gather_end()
-    for chip in range(chips):
-        for copy in stores(chip):
-            copy.wait()
-
-
-def ffn_backward(own, gateup, down, act, slope, chips):
+    for one in [share] + small:
+        one.sum_sent()
+    for at in (tiles - 2, tiles - 1):
+        part_store(at).wait()
+    for store in stores:
+        store.wait()
+
+
+def ffn_backward(own, gateup, down, hidden, act, slope, inputs, pgate, pproj, chips):
     tok_count, width = own.shape
     ff_part = down.shape[0]
     block = 2 * chips * tok_count
     bfloat = jnp.bfloat16
     anywhere = pl.BlockSpec(memory_space=pl.ANY)
     vmem = pl.BlockSpec(memory_space=pltpu.VMEM)
-    result, gathered, grad = pl.pallas_call(
+    dma = pltpu.SemaphoreType.DMA
+    tile = 256
+    held = (gateup, down, hidden, act, slope, inputs)
+    return pl.pallas_call(
         functools.partial(ffn_backward_kernel, chips),
         out_shape=[
             jax.ShapeDtypeStruct((tok_count, width), jnp.float32),
-            jax.ShapeDtypeStruct((chips, 2, tok_count, width), bfloat),
-            jax.ShapeDtypeStruct((block, 2 * ff_part), bfloat),
+            jax.ShapeDtypeStruct((width // tile, tile, 2 * ff_part), bfloat),
+            jax.ShapeDtypeStruct((2, ff_part // 8, width), bfloat),
+        ]
+        + [
+            jax.ShapeDtypeStruct((2, one.shape[0], one.shape[1] // 8, one.shape[2]), bfloat)
+            for one in (pgate, pproj)
         ],
-        in_specs=[vmem] + [anywhere] * 4,
-        out_specs=[vmem, anywhere, anywhere],
+        in_specs=[vmem] + [anywhere] * 8,
+        out_specs=[vmem] + [anywhere] * 4,
         scratch_shapes=line_scratch(chips, tok_count, width)
+        + [pltpu.VMEM(one.shape, bfloat) for one in held]
         + [
-            pltpu.VMEM(gateup.shape, bfloat),
+            pltpu.VMEM((block, 2 * ff_part), bfloat),
             pltpu.VMEM(down.shape, bfloat),
-            pltpu.VMEM((block, ff_part), bfloat),
-            pltpu.VMEM((block, ff_part), bfloat),
-            pltpu.VMEM((block, 2 * ff_part), bfloat),
-            pltpu.SemaphoreType.DMA((4,)),
-            pltpu.SemaphoreType.DMA((chips, 2)),
-        ],
+            pltpu.VMEM((2, tile, 2 * ff_part), bfloat),
+            dma((6,)),
+            dma((2,)),
+            dma((3, 2)),
+        ]
+        + sum_scratch(down.shape)
+        + sum_scratch(pgate.shape)
+        + sum_scratch(pproj.shape),
         compiler_params=pltpu.CompilerParams(
             collective_id=2, has_side_effects=True, vmem_limit_bytes=KERNEL_VMEM
         ),
         cost_estimate=pl.CostEstimate(
-            flops=6 * block * width * ff_part, bytes_accessed=40 << 20, transcendentals=0
+            flops=12 * block * width * ff_part, bytes_accessed=40 << 20, transcendentals=0
         ),
         name="ffn_backward",
-    )(own, gateup, down, act, slope)
-    return result, gathered.reshape(block, width), grad
-
-class Plane:
-    def locate(self, columns, rows):
-        self.columns = columns
-        at = lax.axis_index("ctx")
-        self.at_x, self.at_y = at % 2, at // 2
-        self.beside = (at + 1 - 2 * (at % 2), (at + 2) % 4)
-        self.me = lax.axis_index("fsdp")
-        self.members = lax.axis_size("fsdp")
-        self.half = rows // 2
-        self.quarter = rows // 4
-        self.eighth = rows // 8
-
-    def rows(self, ref, start, size):
-        start = pl.multiple_of(start, size)
-        return ref.at[:, pl.ds(start, size)] if self.columns else ref.at[pl.ds(start, size)]
-
-    def sides(self, half):
-        return (self.at_x, self.at_y) if half == 0 else (self.at_y, self.at_x)
-
-    def kept_start(self, half):
-        return half * self.half + self.sides(half)[0] * self.quarter
-
-    def given_start(self, half):
-        return half * self.half + (1 - self.sides(half)[0]) * self.quarter
-
-    def own_start(self, half):
-        return self.kept_start(half) + self.sides(half)[1] * self.eighth
-
-    def copy(self, src, dst, send_sem, recv_sem, half, stage):
-        return pltpu.make_async_remote_copy(
-            src_ref=src,
-            dst_ref=dst,
-            send_sem=send_sem.at[half, stage],
-            recv_sem=recv_sem.at[half, stage],
-            device_id={"ctx": self.beside[(half + stage) % 2]},
-            device_id_type=pl.DeviceIdType.MESH,
-        )
-
-
-class Summed(Plane):
-    def __init__(self, source, refs, columns):
-        self.source = source
-        self.kept, self.taken, self.last, self.load_sem, self.sum_send, self.sum_recv = refs
-        self.locate(columns, source.shape[-2])
-
-    def load(self, half):
-        return pltpu.make_async_copy(
-            self.rows(self.source, self.kept_start(half), self.quarter),
-            self.kept.at[half],
-            self.load_sem.at[half],
-        )
-
-    def first(self, half):
-        return self.copy(
-            self.rows(self.source, self.given_start(half), self.quarter),
-            self.taken.at[half],
-            self.sum_send,
-            self.sum_recv,
-            half,
-            0,
-        )
-
-    def second(self, half):
-        other = (1 - self.sides(half)[1]) * self.eighth
-        return self.copy(
-            self.rows(self.kept.at[half], other, self.eighth),
-            self.last.at[half],
-            self.sum_send,
-            self.sum_recv,
-            half,
-            1,
-        )
-
-    def begin(self):
-        for half in (0, 1):
-            self.first(half).start()
-            self.load(half).start()
-
-    def add(self, half, start, more, more_start):
-        step = min(32, self.eighth)
-        blocks = self.eighth // step
-        layers = self.source.shape[0] if self.columns else 1
-
-        @pl.loop(0, layers * blocks)
-        def _(at):
-            layer, block = at // blocks, at % blocks
-            here = pl.ds(pl.multiple_of(start + block * step, step), step)
-            there = pl.ds(pl.multiple_of(more_start + block * step, step), step)
-            if self.columns:
-                total = self.kept[half, layer, here].astype(jnp.float32)
-                total = total + more[half, layer, there].astype(jnp.float32)
-                self.kept[half, layer, here] = total.astype(jnp.bfloat16)
-            else:
-                total = self.kept[half, here].astype(jnp.float32)
-                total = total + more[half, there].astype(jnp.float32)
-                self.kept[half, here] = total.astype(jnp.bfloat16)
-
-    def middle(self):
-        for half in (0, 1):
-            self.load(half).wait()
-            self.first(half).wait_recv()
-            side = self.sides(half)[1]
-            other = (1 - side) * self.eighth
-            self.add(half, other, self.taken, other)
-            self.second(half).start()
-            mine = side * self.eighth
-            self.add(half, mine, self.taken, mine)
-
-    def finish(self):
-        for half in (0, 1):
-            self.second(half).wait_recv()
-            self.add(half, self.sides(half)[1] * self.eighth, self.last, 0)
-
-    def own_rows(self, half):
-        return self.rows(self.kept.at[half], self.sides(half)[1] * self.eighth, self.eighth)
-
-    def held(self, half, member):
-        side = self.sides(half)[1] * self.eighth
-        return self.kept.at[half, member, pl.ds(pl.multiple_of(side, self.eighth), self.eighth)]
-
-    def sum_sent(self):
-        for half in (0, 1):
-            self.first(half).wait_send()
-            self.second(half).wait_send()
-
-
-class Held:
-    def __init__(self, kept):
-        self.kept = kept
-
-    def own_rows(self, half):
-        return self.kept.at[half]
-
-    def held(self, half, member):
-        return self.kept.at[half, member]
-
-
-class Spread(Plane):
-    def __init__(self, source, refs, columns):
-        self.own_rows, self.held = source.own_rows, source.held
-        self.final, self.spread_send, self.spread_recv, self.place_sem = refs[:4]
-        if columns:
-            self.swap_send, self.swap_recv = refs[4:]
-        self.locate(columns, self.final.shape[-2])
-
-    def place(self, half):
-        return pltpu.make_async_copy(
-            self.own_rows(half),
-            self.rows(self.final, self.own_start(half), self.eighth),
-            self.place_sem.at[half],
-        )
-
-    def place_all(self):
-        for half in (0, 1):
-            self.place(half).start()
-        for half in (0, 1):
-            self.place(half).wait()
-
-    def swap_copy(self, half, hop, src_member):
-        target = lax.rem(self.me + hop, self.members)
-        final_rows = pl.ds(pl.multiple_of(self.own_start(half), self.eighth), self.eighth)
-        return remote(
-            self.held(half, target),
-            self.final.at[src_member, final_rows],
-            self.swap_send.at[hop, half],
-            self.swap_recv.at[hop, half],
-            target,
-        )
-
-    def swap_local(self, half):
-        final_rows = pl.ds(pl.multiple_of(self.own_start(half), self.eighth), self.eighth)
-        return pltpu.make_async_copy(
-            self.held(half, self.me),
-            self.final.at[self.me, final_rows],
-            self.place_sem.at[half],
-        )
-
-    def swap_begin(self):
-        for half in (0, 1):
-            for hop in range(1, self.members):
-                self.swap_copy(half, hop, self.me).start()
-            self.swap_local(half).start()
-
-    def swap_end(self):
-        for half in (0, 1):
-            for hop in range(1, self.members):
-                source = lax.rem(self.me + self.members - hop, self.members)
-                self.swap_copy(half, hop, source).wait_recv()
-            self.swap_local(half).wait()
-
-    def spread_copy(self, half, stage):
-        if stage == 0:
-            rows = self.rows(self.final, self.own_start(half), self.eighth)
-        else:
-            rows = self.rows(self.final, self.kept_start(half), self.quarter)
-        return self.copy(rows, rows, self.spread_send, self.spread_recv, half, 1 - stage)
-
-    def spread_wait(self, half, stage):
-        side = self.sides(half)[1]
-        if stage == 0:
-            start = self.kept_start(half) + (1 - side) * self.eighth
-            rows = self.rows(self.final, start, self.eighth)
-        else:
-            rows = self.rows(self.final, self.given_start(half), self.quarter)
-        self.copy(rows, rows, self.spread_send, self.spread_recv, half, 1 - stage).wait_recv()
-
-    def spread_begin(self):
-        for half in (0, 1):
-            self.spread_copy(half, 0).start()
-
-    def spread_on(self):
-        for half in (0, 1):
-            self.spread_wait(half, 0)
-            self.spread_copy(half, 1).start()
-
-    def spread_end(self):
-        for half in (0, 1):
-            self.spread_wait(half, 1)
-
-    def spread_sent(self):
-        for half in (0, 1):
-            self.spread_copy(half, 0).wait_send()
-            self.spread_copy(half, 1).wait_send()
-            if self.columns:
-                for hop in range(1, self.members):
-                    self.swap_copy(half, hop, self.me).wait_send()
-
-
-def sum_scratch(shape):
-    dma = pltpu.SemaphoreType.DMA
-    rows, width = shape[-2:]
-
-    def buffer(count):
-        return pltpu.VMEM((2,) + shape[:-2] + (count, width), jnp.bfloat16)
-
-    buffers = [buffer(rows // 4), buffer(rows // 4), buffer(rows // 8)]
-    return buffers + [dma((2,)), dma((2, 2)), dma((2, 2))]
-
-
-SUM_REFS = 6
-
-
-def spread_scratch(shape):
-    dma = pltpu.SemaphoreType.DMA
-    scratch = [pltpu.VMEM(shape, jnp.bfloat16), dma((2, 2)), dma((2, 2)), dma((2,))]
-    if len(shape) == 3:
-        scratch += [dma((shape[0], 2)), dma((shape[0], 2))]
-    return scratch
-
-
-def spread_refs(columns):
-    return 6 if columns else 4
-
-
-def gradient_sum_kernel(held_columns, columns, *refs):
-    refs = list(refs)
-    helds, sources = refs[: len(held_columns)], refs[len(held_columns) :][: len(columns)]
-    count = len(helds) + len(sources)
-    results = refs[count : 2 * count + 1]
-    scratch = refs[2 * count + 1 :]
-    store_sem = scratch.pop()
-    sums, spreads = [], []
-    for kept, by_column in zip(helds, held_columns):
-        size = spread_refs(by_column)
-        spreads.append(Spread(Held(kept), scratch[:size], by_column))
-        del scratch[:size]
-    for source, by_column in zip(sources, columns):
-        sums.append(Summed(source, scratch[:SUM_REFS], by_column))
-        del scratch[:SUM_REFS]
-        size = spread_refs(by_column)
-        spreads.append(Spread(sums[-1], scratch[:size], by_column))
-        del scratch[:size]
-    early, late = spreads[: len(helds)], spreads[len(helds) :]
-    greet_all()
-
-    def stores(at):
-        final = spreads[at].final
-        if at > 0:
-            return [pltpu.make_async_copy(final, results[at + 1], store_sem.at[0, at])]
-        part = final.shape[2] // 2
-        return [
-            pltpu.make_async_copy(
-                final.at[member, :, pl.ds(side * part, part)],
-                results[side].at[:, pl.ds(member * part, part)],
-                store_sem.at[1 + side, member],
-            )
-            for member in range(final.shape[0])
-            for side in (0, 1)
-        ]
-
-    def launch(spread):
-        if spread.columns:
-            spread.swap_begin()
-        else:
-            spread.place_all()
-            spread.spread_begin()
-
-    for share in sums:
-        share.begin()
-    for spread in early:
-        launch(spread)
-    for share in sums:
-        share.middle()
-    for spread in early:
-        if spread.columns:
-            spread.swap_end()
-            spread.spread_begin()
-        else:
-            spread.spread_on()
-    for share, spread in zip(sums, late):
-        share.finish()
-        launch(spread)
-    for spread in early:
-        if spread.columns:
-            spread.spread_on()
-    for spread in late:
-        if spread.columns:
-            spread.swap_end()
-            spread.spread_begin()
-        else:
-            spread.spread_on()
-    for spread in late:
-        if spread.columns:
-            spread.spread_on()
-    for at, spread in enumerate(spreads):
-        spread.spread_end()
-        for store in stores(at):
-            store.start()
-    for share in sums:
-        share.sum_sent()
-    for spread in spreads:
-        spread.spread_sent()
-    for at in range(count):
-        for store in stores(at):
-            store.wait()
-
-
-def gradient_sum(helds, grads):
-    held_shapes = [held.shape[1:-2] + (8 * held.shape[-2], held.shape[-1]) for held in helds]
-    members, rows, width = held_shapes[0]
-    wide = (rows, members * width // 2)
-    shapes = held_shapes + [grad.shape for grad in grads]
-    held_columns = [len(shape) == 3 for shape in held_shapes]
-    columns = [grad.ndim == 3 for grad in grads]
-    anywhere = pl.BlockSpec(memory_space=pl.ANY)
-    scratch = []
-    for shape in held_shapes:
-        scratch += spread_scratch(shape)
-    for grad in grads:
-        scratch += sum_scratch(grad.shape) + spread_scratch(grad.shape)
-    return pl.pallas_call(
-        functools.partial(gradient_sum_kernel, held_columns, columns),
-        out_shape=[
-            jax.ShapeDtypeStruct(shape, jnp.bfloat16) for shape in [wide, wide] + shapes[1:]
-        ],
-        in_specs=[anywhere] * len(shapes),
-        out_specs=[anywhere] * (len(shapes) + 1),
-        scratch_shapes=scratch + [pltpu.SemaphoreType.DMA((3, members))],
-        compiler_params=pltpu.CompilerParams(
-            collective_id=3, has_side_effects=True, vmem_limit_bytes=KERNEL_VMEM
-        ),
-        cost_estimate=pl.CostEstimate(flops=0, bytes_accessed=300 << 20, transcendentals=0),
-        name="gradient_sum",
-    )(*helds, *grads)
+    )(own, *held, pgate, pproj)
 
 def rope_norm(lin, gain, cosine, sine_part):
     scale = lax.rsqrt(jnp.mean(lin * lin, axis=-1, keepdims=True) + EPSILON)
@@ -1598,25 +1745,28 @@
     gain_query_ref,
     gain_key_ref,
     gateup_hbm,
-    down_hbm,
+    down_kept,
+    inputs_hbm,
+    attended_hbm,
     result_ref,
-    all_hbm,
-    grad_hbm,
+    query_part_hbm,
+    kv_part_hbm,
+    out_part_hbm,
     gains_ref,
     gateup_kept,
-    down_kept,
+    down_sum,
     *scratch,
 ):
     scratch = list(scratch)
     line = Line(chips, scratch[:LINE_REFS])
     del scratch[:LINE_REFS]
-    shares = []
-    for source, columns in ((gateup_hbm, True), (down_hbm, False)):
-        shares.append(Summed(source, scratch[:SUM_REFS], columns))
-        del scratch[:SUM_REFS]
-    gateup, down = shares
+    gateup = Summed(gateup_hbm, scratch[:SUM_REFS], True)
+    del scratch[:SUM_REFS]
+    down = Spread(Held(down_kept), scratch[: spread_refs(False)], False)
+    del scratch[: spread_refs(False)]
     out, qkv, lin, query, span, probs, grad, grad_span, back, across, returned = scratch[:11]
-    load_sem, store_sem, back_send, back_recv, grad_out = scratch[11:]
+    load_sem, store_sem, back_send, back_recv, grad_out = scratch[11:16]
+    inputs, attended, query_part, kv_part, out_part = scratch[16:]
     width = line.slots.shape[3]
     pair = 2 * line.tok
     block = chips * pair
@@ -1633,6 +1783,8 @@
                 (lin_hbm, lin),
                 (query_hbm, query),
                 (qkv_hbm, qkv),
+                (inputs_hbm, inputs),
+                (attended_hbm, attended),
             )
         )
     ]
@@ -1644,7 +1796,7 @@
     grad_span[...] = jnp.zeros_like(grad_span)
     gains_ref[...] = jnp.zeros_like(gains_ref)
     line.own_copy(own_ref).wait()
-    for load in loads:
+    for load in loads[:6]:
         load.wait()
 
     span_len = WINDOW + pair
@@ -1669,9 +1821,6 @@
         grad_span[0, span_rows] += dot_tn(grad_score, query[rows])
         grad_span[1, span_rows] += dot_tn(probs[rows], grad_out[rows])
 
-    store_all = pltpu.make_async_copy(line.slots, all_hbm, store_sem.at[0])
-    store_all.start()
-
     part = WINDOW // 2
     mine, others = line.core * part, (1 - line.core) * part
     back[...] = grad_span[:, pl.ds(pl.multiple_of(others, part), part)].astype(bfloat)
@@ -1695,7 +1844,8 @@
     def _():
         to_before.start()
 
-    down.begin()
+    down.place_all()
+    down.spread_begin()
 
     @pl.when(ctx_at < planes - 1)
     def _():
@@ -1713,46 +1863,65 @@
         grad[rows, HD : 2 * HD] = grad_lin.astype(bfloat)
         gains_ref[1:2] += grad_gain
         grad[rows, 2 * HD :] = grad_span[1, span_rows].astype(bfloat)
-        wide = 512
-
-        @pl.loop(0, width // wide)
-        def _(at, chip=chip, rows=rows):
-            cols = pl.ds(pl.multiple_of(at * wide, wide), wide)
-            sums = dot_nt(grad[rows], qkv[cols]).astype(bfloat)
-            line.parts[chip, :, :, cols] = sums.reshape(2, line.tok, wide)
-
-        line.core_copy(chip).start()
-        if step > 0:
-            line.scatter_first(line.order(chips - step))
-    line.scatter_first(line.order(0))
-    store_grad = pltpu.make_async_copy(grad, grad_hbm, store_sem.at[1])
-    store_grad.start()
+
+    wide = 512
+
+    @pl.loop(0, width // wide)
+    def _(at):
+        cols = pl.ds(pl.multiple_of(at * wide, wide), wide)
+        sums = dot_nt(grad[...], qkv[cols]).astype(bfloat)
+        line.parts[:, :, :, cols] = sums.reshape(chips, 2, line.tok, wide)
+
+    for step in range(chips):
+        line.core_copy(line.order(chips - 1 - step)).start()
+    for step in range(chips - 1):
+        line.scatter_first(line.order(chips - 1 - step))
+    for load in loads[6:]:
+        load.wait()
+    part_stores = [
+        pltpu.make_async_copy(out_part, out_part_hbm, store_sem.at[0]),
+        pltpu.make_async_copy(query_part, query_part_hbm, store_sem.at[1]),
+        pltpu.make_async_copy(kv_part, kv_part_hbm, store_sem.at[5]),
+    ]
+
+    def between(rank):
+        if rank == 3:
+            for start in range(0, width, wide):
+                right = line.slots[:, :, :, start : start + wide].reshape(block, wide)
+                out_part[:, start : start + wide] = dot_tn(attended[...], right).astype(bfloat)
+            part_stores[0].start()
+        if rank == 4:
+
+            @pl.loop(0, width // HD)
+            def _(at):
+                left = inputs[:, pl.ds(pl.multiple_of(at * HD, HD), HD)]
+                query_part[at] = dot_tn(left, grad[:, :HD]).astype(bfloat)
+                kv_part[at] = dot_tn(left, grad[:, HD:]).astype(bfloat)
+
+            part_stores[1].start()
+            part_stores[2].start()
+
     gateup.middle()
-    line.scatter_rest(result_ref)
-    down.middle()
+    down.spread_on()
+    line.scatter_rest(result_ref, between)
     gateup.finish()
-    down.finish()
-    stores = []
-    for at, (share, kept) in enumerate(((gateup, gateup_kept), (down, down_kept))):
-        for half in (0, 1):
-            stores.append(
-                pltpu.make_async_copy(
-                    share.own_rows(half), kept.at[half], store_sem.at[2 + 2 * at + half]
-                )
-            )
+    stores = [
+        pltpu.make_async_copy(gateup.own_rows(half), gateup_kept.at[half], store_sem.at[2 + half])
+        for half in (0, 1)
+    ]
+    down.spread_end()
+    stores.append(pltpu.make_async_copy(down.final, down_sum, store_sem.at[4]))
     for store in stores:
         store.start()
     line.gather_end()
-    for share in shares:
-        share.sum_sent()
+    gateup.sum_sent()
+    down.spread_sent()
 
     @pl.when(ctx_at > 0)
     def _():
         to_before.wait_send()
 
-    store_all.wait()
-    store_grad.wait()
-    for store in stores:
+    for store in stores + part_stores:
         store.wait()
 
 
@@ -1769,7 +1938,9 @@
     gain_query,
     gain_key,
     part_gateup,
-    part_down,
+    held_down,
+    inputs,
+    attended,
 ):
     tok_count, width = own.shape
     members = part_gateup.shape[0]
@@ -1780,23 +1951,25 @@
     vmem = pl.BlockSpec(memory_space=pltpu.VMEM)
     dma = pltpu.SemaphoreType.DMA
     eighth = part_gateup.shape[1] // 8
+    down_shape = (8 * held_down.shape[1], held_down.shape[2])
     outputs = [
         ((tok_count, width), jnp.float32),
-        ((chips, 2, tok_count, width), bfloat),
-        ((block, 3 * HD), bfloat),
+        ((members, HD, HD), bfloat),
+        ((members, HD, 2 * HD), bfloat),
+        ((HD, width), bfloat),
         ((2, HD), jnp.float32),
         ((2, members, eighth, part_gateup.shape[2]), bfloat),
-        ((2, part_down.shape[0] // 8, part_down.shape[1]), bfloat),
+        (down_shape, bfloat),
     ]
     half_span = (2, WINDOW // 2, HD)
     return pl.pallas_call(
         functools.partial(attention_backward_kernel, chips),
         out_shape=[jax.ShapeDtypeStruct(*output) for output in outputs],
-        in_specs=[vmem] + [anywhere] * 6 + [vmem] * 4 + [anywhere] * 2,
-        out_specs=[vmem, anywhere, anywhere, vmem, anywhere, anywhere],
+        in_specs=[vmem] + [anywhere] * 6 + [vmem] * 4 + [anywhere] * 4,
+        out_specs=[vmem, anywhere, anywhere, anywhere, vmem, anywhere, anywhere],
         scratch_shapes=line_scratch(chips, tok_count, width)
         + sum_scratch(part_gateup.shape)
-        + sum_scratch(part_down.shape)
+        + spread_scratch(down_shape)
         + [pltpu.VMEM(one.shape, one.dtype) for one in (out, qkv, lin, query, span, probs)]
         + [
             pltpu.VMEM((block, 3 * HD), bfloat),
@@ -1804,11 +1977,16 @@
             pltpu.VMEM(half_span, bfloat),
             pltpu.VMEM(half_span, bfloat),
             pltpu.VMEM(half_span, bfloat),
-            dma((6,)),
+            dma((8,)),
             dma((6,)),
             dma((2,)),
             dma((2,)),
             pltpu.VMEM((block, HD), bfloat),
+            pltpu.VMEM((block, width), bfloat),
+            pltpu.VMEM((block, HD), bfloat),
+            pltpu.VMEM((members, HD, HD), bfloat),
+            pltpu.VMEM((members, HD, 2 * HD), bfloat),
+            pltpu.VMEM((HD, width), bfloat),
         ],
         compiler_params=pltpu.CompilerParams(
             collective_id=5, has_side_effects=True, vmem_limit_bytes=KERNEL_VMEM
@@ -1830,7 +2008,9 @@
         gain_query,
         gain_key,
         part_gateup,
-        part_down,
+        held_down,
+        inputs,
+        attended,
     )
 
 def by_heads(
@@ -1913,9 +2093,23 @@
     gate_own, up_own = own_rows(w_gate, ff_part), own_rows(w_up, ff_part)
     out_low = w_out.astype(bfloat)
     down_low = w_down.astype(bfloat)
-    full_left, full_right, full_pgate, full_pproj = (
-        lax.all_gather(w.astype(bfloat), "fsdp", axis=0, tiled=True)
-        for w in (laurel_left, laurel_right, ple_gate, ple_proj)
+    width = tokens.shape[1]
+    small_weights = (ple_gate, ple_proj, laurel_left, laurel_right)
+    small_sizes = [weight.size // width for weight in small_weights]
+    small_total = sum(small_sizes)
+    share_rows = -(-small_total // (8 * ctx_count)) * 8
+    small_packed = jnp.concatenate(
+        [weight.astype(bfloat).reshape(-1, width) for weight in small_weights]
+        + [jnp.zeros((share_rows * ctx_count - small_total, width), bfloat)]
+    )
+    small_share = lax.dynamic_slice_in_dim(small_packed, ctx_at * share_rows, share_rows, 0)
+    small_full = lax.all_gather(small_share, ("ctx", "fsdp"), axis=0, tiled=False)
+    small_full = small_full.reshape(ctx_count, fsdp_count, share_rows, width)
+    small_full = jnp.transpose(small_full, (1, 0, 2, 3)).reshape(fsdp_count, -1, width)
+    small_ends = [sum(small_sizes[:n]) for n in range(5)]
+    full_pgate, full_pproj, full_left, full_right = (
+        small_full[:, small_ends[n] : small_ends[n + 1]].reshape(-1, weight.shape[1])
+        for n, weight in enumerate(small_weights)
     )
 
     inputs = tokens.astype(jnp.float32)
@@ -1967,11 +2161,19 @@
     part_pgate = matmul_tn(layer_low, grad_plelin_low)
     grad_layer = grad_layer + matmul_nt(grad_plelin_low, full_pgate)
     grad_mixed, grad_down, grad_gffout = ffn_out_back(grad_layer)
-    grad_ffn, grad_down_all, grad_gateup_low = ffn_backward(
-        grad_down.astype(bfloat), col_gateup, down_low, act_low, slope_low, chips
-    )
-    part_wdown = matmul_tn(hidden_low, grad_down_all).astype(bfloat)
-    part_gateup = matmul_tn(ffn_all, grad_gateup_low).astype(bfloat).reshape(fsdp_count, rows, -1)
+    grad_ffn, part_gateup, held_wdown, held_pgate, held_pproj = ffn_backward(
+        grad_down.astype(bfloat),
+        col_gateup,
+        down_low,
+        hidden_low,
+        act_low,
+        slope_low,
+        ffn_all,
+        part_pgate.astype(bfloat).reshape(fsdp_count, rows, -1),
+        part_pproj.astype(bfloat).reshape(fsdp_count, 128, -1),
+        chips,
+    )
+    part_gateup = part_gateup.reshape(fsdp_count, rows, -1)
     grad_mixed_more, grad_gffin = ffn_norm_back(grad_ffn)
     grad_mixed = grad_mixed + grad_mixed_more
     grad_in_first, grad_normed, grad_proj, grad_lwide, grad_gpost, grad_glaurel = mix_back(
@@ -1983,7 +2185,15 @@
     part_left = matmul_tn(normed_low, grad_narrow_low)
     grad_normed = grad_normed + matmul_nt(grad_narrow_low, full_left)
 
-    grad_normed_more, grad_proj_all, grad_qkv_low, grad_head_gains, held_gateup, held_wdown = (
+    (
+        grad_normed_more,
+        part_query,
+        part_kv,
+        part_wout,
+        grad_head_gains,
+        held_gateup,
+        sum_wdown,
+    ) = (
         attention_backward(
             grad_proj.astype(bfloat),
             out_low,
@@ -1997,24 +2207,15 @@
             gain_query[None, :],
             gain_key[None, :],
             part_gateup,
-            part_wdown,
+            held_wdown,
+            normed_all,
+            attended_low,
         )
     )
     grad_gquery, grad_gkey = grad_head_gains[0], grad_head_gains[1]
-    part_wout = matmul_tn(attended_low, grad_proj_all.reshape(block_len, -1)).astype(bfloat)
-    part_qkv = matmul_tn(normed_all, grad_qkv_low).astype(bfloat).reshape(fsdp_count, rows, -1)
-    small_parts = [
-        part.astype(bfloat).reshape(fsdp_count, -1, inputs.shape[1])
-        for part in (part_pgate, part_pproj, part_left, part_right)
-    ]
-    small_sizes = [part.shape[1] for part in small_parts]
-    small_total = sum(small_sizes)
-    small_rows = -(-small_total // 128) * 128
-    small_parts.append(
-        jnp.zeros((fsdp_count, small_rows - small_total, inputs.shape[1]), bfloat)
-    )
-    small = lax.psum_scatter(
-        jnp.concatenate(small_parts, axis=1), "fsdp", scatter_dimension=0, tiled=False
+    part_laurel = jnp.concatenate(
+        [part.astype(bfloat).reshape(fsdp_count, 128, -1) for part in (part_left, part_right)],
+        axis=2,
     )
     grad_normed = grad_normed + grad_normed_more
     grad_in_second, grad_gin = norm_back(grad_normed)
@@ -2034,26 +2235,43 @@
     gain_parts = jnp.pad(gain_parts, ((0, 0), (0, 128 * 128 - gain_parts.shape[1])))
     gain_parts = gain_parts.astype(bfloat).reshape(fsdp_count, 128, 128)
 
-    sum_wgate, sum_wup, sum_wdown, sum_wout, sum_qkv, sum_small, sum_gains = gradient_sum(
-        [held_gateup, held_wdown], [part_wout, part_qkv, small, gain_parts]
+    (
+        sum_wgate,
+        sum_wup,
+        sum_wquery,
+        sum_wkey,
+        sum_wvalue,
+        sum_wout,
+        sum_pgate,
+        sum_pproj,
+        sum_laurel,
+        sum_gains,
+    ) = gradient_sum(
+        [
+            Source(held_gateup, summed=True, part=(0, 2), sides=1),
+            Source(held_gateup, summed=True, part=(1, 2), sides=1),
+            Source(part_query, sides=1),
+            Source(part_kv, groups=KV, sides=2),
+            Source(part_wout),
+            Source(held_pgate, summed=True, groups=1, sides=1),
+            Source(held_pproj, summed=True, groups=1, sides=1),
+            Source(part_laurel, groups=1, sides=1),
+            Source(gain_parts),
+        ]
     )
     gain_sums = jnp.sum(sum_gains.astype(jnp.float32), axis=0).reshape(-1)
     grad_wgate = sum_wgate.astype(jnp.float32)
     grad_wup = sum_wup.astype(jnp.float32)
     grad_wdown = sum_wdown.astype(jnp.float32)
     grad_wout = sum_wout.astype(jnp.float32)
-    sum_qkv = sum_qkv.astype(jnp.float32)
-    grad_wquery = jnp.transpose(sum_qkv[:, :, :HD], (1, 0, 2)).reshape(rows, -1)
-    sum_kv = jnp.sum(sum_qkv[:, :, HD:].reshape(KV, group_size, rows, 2 * HD), axis=1)
-    sum_kv = jnp.transpose(sum_kv, (1, 0, 2))
-    grad_wkey = sum_kv[:, :, :HD].reshape(rows, -1)
-    grad_wvalue = sum_kv[:, :, HD:].reshape(rows, -1)
-    sum_small = sum_small.astype(jnp.float32)
-    small_ends = [sum(small_sizes[:n]) for n in range(5)]
-    grad_pgate, grad_pproj, grad_wleft, grad_wright = (
-        sum_small[small_ends[n] : small_ends[n + 1]].reshape(weight.shape)
-        for n, weight in enumerate((ple_gate, ple_proj, laurel_left, laurel_right))
-    )
+    grad_wquery = sum_wquery.astype(jnp.float32)
+    grad_wkey = sum_wkey.astype(jnp.float32)
+    grad_wvalue = sum_wvalue.astype(jnp.float32)
+    grad_pgate = sum_pgate.astype(jnp.float32)
+    grad_pproj = sum_pproj.astype(jnp.float32).reshape(ple_proj.shape)
+    left_part = sum_laurel.shape[1] // 2
+    grad_wleft = sum_laurel[:, :left_part].astype(jnp.float32).reshape(laurel_left.shape)
+    grad_wright = sum_laurel[:, left_part:].astype(jnp.float32).reshape(laurel_right.shape)
     return (
         out_full.astype(bfloat),
         grad_tokens,

time: 898 us -> 791 us (0.88)
  Pallas kernels: 679 us -> 645 us
  matrix products: 44.2 us -> 14.3 us
  blocking collectives: 44.8 us -> 15.6 us
  local copies, waits for them, and re-layouts: 40.6 us -> 29.5 us
    pallas_call x1, Pallas kernels: 189 us -> 147 us  [gradient_sum(): pl.pallas_call(functools.partial(gradient_sum_kernel, sources), out_shape...]
    dot_general x8 -> x4, matrix products: 34.9 us -> 4.03 us  [matmul_tn(): lax.dot_general(left_mat, right_mat, (((0,), (0,)), ((), ())), preferred_...]
    all_gather x2 -> x0, blocking collectives: 29.1 us -> none  [by_heads(): lax.all_gather(w.astype(bfloat), 'fsdp', axis=0, tiled=True)]
    pallas_call x1, Pallas kernels: 145 us -> 122 us  [attention_backward(): pl.pallas_call(functools.partial(attention_backward_kernel, chips), out_s...]
    pallas_call x1, Pallas kernels: 84.3 us -> 104 us  [ffn_backward(): pl.pallas_call(functools.partial(ffn_backward_kernel, chips), out_shape=[...]
    pallas_call x1, Pallas kernels: 174 us -> 184 us  [attention_forward(): pl.pallas_call(functools.partial(attention_forward_kernel, chips), out_sh...]
    unnamed x153 -> x69, local copies, waits for them, and re-layouts: 14.5 us -> 4.61 us
  transfers between devices with their start and end apart: 3 -> 1, of which waited for: 0 -> 0; matrix products, arithmetic and copies ran while one was open for 9% -> 3% of each run, Pallas kernels for 46% -> 24%
where the time goes in v5:
time: 791 us; the launch traced here: 782 us
  Pallas kernels  645 us (82%)
  other arithmetic  61.5 us (8%)
  local copies, waits for them, and re-layouts  29.5 us (4%)
  blocking collectives  15.6 us (2%)
  between operations  15.3 us (2%)
  matrix products  14.3 us (2%)
    pallas_call x1, Pallas kernels, attention_forward(): pl.pallas_call(functools.partial(attention_forward_kernel, chips), out_sh...  184 us
    pallas_call x1, Pallas kernels, gradient_sum(): pl.pallas_call(functools.partial(gradient_sum_kernel, sources), out_shape...  147 us
    pallas_call x1, Pallas kernels, attention_backward(): pl.pallas_call(functools.partial(attention_backward_kernel, chips), out_s...  122 us
    pallas_call x1, Pallas kernels, ffn_backward(): pl.pallas_call(functools.partial(ffn_backward_kernel, chips), out_shape=[...  104 us
    pallas_call x1, Pallas kernels, ffn_forward(): pl.pallas_call(functools.partial(ffn_forward_kernel, chips), out_shape=[j...  88.7 us
  transfers between devices with their start and end apart: 1, of which 0 were waited for; matrix products, arithmetic and copies ran while one was open for 3% of the time, Pallas kernels for 24%

profile of v5, /device:TPU:0, one launch (start us, length us, event | category | flops | bytes accessed | tf_op | source)
XLA Modules:
  0.0 781.6 jit_solution(5581365041034332077)
XLA Ops:
  13.6 15.6 %all_gather.9 = f32[8,16,128]{2,1,0:T(8,128)S(1)} all-gather(f32[1,16,128]{2,1,0:T(8,128)S(1)} %pad_bitcast_fusion.1), channel_id=1, replica_groups=mesh['ctx'=4,'fsdp'=8] {'fsdp'}, dimensions={0}, use_global_device_ids=true | all-gather | bytes 73728 | tf_op jit(solution)/shard_map/all_gather | solution.py:2067
  36.5 2.8 dynamic-slice_convert_fusion.1
  41.8 2.7 convert_element_type.137.down_hbm
  47.9 3.0 multiply_sine_fusion
  52.5 184.4 %attention_forward.1 = (f32[128,2048]{1,0:T(8,128)}, bf16[4,2,128,2048]{3,2,1,0:T(8,128)(2,1)}, bf16[8,256,768]{2,1,0:T(8,128)(2,1)}, bf16[8,256,2048]{2,1,0:T(8...) custom-call(bf16[128,2048]{1,0:T(8,128)(2,1)} %fusion.6.own_ref, ...), custom_call_target="tpu_custom_call" | custom-call | flops 8589934592 | bytes 314572800 | tf_op jit(solution)/shard_map/attention_forward/pallas_call | solution.py:1689
  238.3 2.3 copy.99
  240.7 1.6 copy-done.7
  242.3 1.6 fusion.43
  244.7 2.3 multiply_reduce_fusion.11
  247.0 2.3 reshape.360
  249.3 1.8 multiply_reduce_fusion.10
  252.1 88.7 %ffn_forward.1 = (f32[128,2048]{1,0:T(8,128)}, bf16[4,2,128,2048]{3,2,1,0:T(8,128)(2,1)}, bf16[1024,1024]{1,0:T(8,128)(2,1)}, bf16[1024,1024]{1,0:T(8,128)(2,1)}, bf16[1024,1024]{1,0:T(8,128)(2,1)}) custom-call(bf16[128,2048]{1,0:T(8,128)(2,1)} %multiply_convert_fusion.own_ref, bf16[2048,2048]{1,0:T(8,128)(2,1)} %bitcast.153, ...), custom_call_target="tpu_custom_call" | custom-call | flops 12884901888 | bytes 41943040 | tf_op jit(solution)/shard_map/ffn_forward/pallas_call | solution.py:1213
  340.9 1.5 multiply_reduce_fusion.9
  342.4 1.5 multiply_add_fusion
  348.9 1.6 multiply_reduce_fusion
  351.9 2.5 reshape.364.pproj_hbm
  354.4 2.3 fusion.12.own_ref
  356.7 103.8 %ffn_backward.1 = (f32[128,2048]{1,0:T(8,128)}, bf16[8,256,2048]{2,1,0:T(8,128)(2,1)}, bf16[2,128,2048]{2,1,0:T(8,128)(2,1)}, bf16[2,8,32,256]{3,2,1,0:T(8,128)(2,1)}, bf16[2,8,16,512]{3,2,1,0:T(8,128)(2,1)}) custom-call(bf16[128,2048]{1,0:T(8,128)(2,1)} %fusion.12.own_ref, bf16[2048,2048]{1,0:T(8,128)(2,1)} %bitcast.154, ...), custom_call_target="tpu_custom_call" | custom-call | flops 25769803776 | bytes 41943040 | tf_op jit(solution)/shard_map/ffn_backward/pallas_call | solution.py:1417
  460.5 1.5 multiply_reduce_fusion.1
  462.0 3.4 multiply_reduce_fusion.2
  469.2 121.7 %attention_backward.1 = (f32[128,2048]{1,0:T(8,128)}, bf16[8,256,256]{2,1,0:T(8,128)(2,1)}, bf16[8,256,512]{2,1,0:T(8,128)(2,1)}, bf16[256,2048]{1,0:T(8,128)(2,...) custom-call(bf16[128,2048]{1,0:T(8,128)(2,1)} %get-tuple-element.234.own_ref, ...), custom_call_target="tpu_custom_call" | custom-call | flops 8589934592 | bytes 314572800 | tf_op jit(solution)/shard_map/attention_backward/pallas_call | solution.py:1965
  591.0 2.9 fusion.8
  596.6 146.7 %gradient_sum.1 = (bf16[256,8192]{1,0:T(8,128)(2,1)}, bf16[256,8192]{1,0:T(8,128)(2,1)}, bf16[256,2048]{1,0:T(8,128)(2,1)}, bf16[256,512]{1,0:T(8,128)(2,1)}, bf...) custom-call(bf16[2,8,32,2048]{3,2,1,0:T(8,128)(2,1)} %get-tuple-elem, ...), custom_call_target="tpu_custom_call" | custom-call | bytes 314572800 | tf_op jit(solution)/shard_map/gradient_sum/pallas_call | solution.py:821
  748.3 1.6 convert_element_type.160
  749.9 1.7 reshape.388
  751.6 1.8 convert_element_type.154
  753.4 1.8 convert_element_type.155
  755.2 2.9 convert_element_type.153
  758.1 1.6 convert_element_type.156
  759.7 4.4 convert_element_type.157
  764.1 4.4 convert_element_type.158
  768.5 4.4 convert_element_type.159
  (173 shorter events, 43.2 us)
Async XLA Ops:
  7.2 28.1 %copy-start.18 = (f32[256,2048]{1,0:T(8,128)S(1)}, f32[256,2048]{1,0:T(8,128)}, u32[]{:S(2)}) copy-start(f32[256,2048]{1,0:T(8,128)} %param.32) | copy-start | bytes 6291460
  7.2 231.1 %all-gather.3.cloned.1.call-start = ((), (), s32[]{:S(2)}) async-start(), calls=%async_computation | async-start | bytes 3244032 | tf_op jit(solution)/shard_map/all_gather | solution.py:2106
  35.3 6.5 slice-start
  39.3 2.4 slice-start.1
  44.5 3.1 copy-start.6
  240.6 1.7 copy-start.7
  240.6 3.7 copy-start.10
  243.8 5.5 copy-start.1
  244.4 4.9 copy-start.12
  340.8 3.1 copy-start.8
  340.9 3.4 copy-start.16
  340.9 3.4 copy-start.21
  342.4 2.3 copy-start.9
  345.1 3.8 copy-start
  462.0 3.5 copy-start.2
  462.0 3.5 copy-start.3
  465.4 1.3 copy-start.4
  465.4 3.6 copy-start.11
  469.2 121.8 %copy-start.5 = (f32[128,2048]{1,0:T(8,128)S(1)}, f32[128,2048]{1,0:T(8,128)}, u32[]{:S(2)}) copy-start(f32[128,2048]{1,0:T(8,128)} %copy-done.4) | copy-start | bytes 3145732
  591.0 3.0 copy-start.22
  591.0 4.1 copy-start.20
  744.2 13.9 %copy-start.19 = (bf16[256,2048]{1,0:T(8,128)(2,1)S(1)}, bf16[256,2048]{1,0:T(8,128)(2,1)}, u32[]{:S(2)}) copy-start(bf16[256,2048]{1,0:T(8,128)(2,1)} %get-tuple-element.86) | copy-start | bytes 3145732
  755.2 4.5 copy-start.15
  759.7 4.4 copy-start.14
  764.1 4.4 copy-start.13
  768.5 4.5 copy-start.17
Sparse Core Ops, SparseCore 0:
  12.2 71.0 all-gather.2

commit v6 on v5

--- a/solution.py
+++ b/solution.py
@@ -659,6 +659,77 @@
                 self.final[group, rows] = total.astype(jnp.bfloat16)
 
 
+class Everywhere(Spread):
+    def swap_begin(self):
+        chips = self.members // 2
+        for half in (0, 1):
+            own = self.own_rows(half)
+            for hop in range(1, chips):
+                self.hand_to(half, hop, own, lax.rem(self.me + 2 * hop, self.members)).start()
+            self.pass_on(half, self.me // 2, own).start()
+            self.swap_local(half).start()
+
+    def hand_to(self, half, hop, own, place):
+        return remote(
+            own,
+            self.swap_place(half, self.me),
+            self.swap_send.at[0, hop, half],
+            self.swap_recv.at[0, hop, half],
+            place,
+        )
+
+    def pass_on(self, half, chip, source):
+        core = self.me % 2
+        return remote(
+            source,
+            self.swap_place(half, 2 * chip + core),
+            self.swap_send.at[1, chip, half],
+            self.swap_recv.at[1, chip, half],
+            self.me + 1 - 2 * core,
+        )
+
+    def swap_on(self):
+        chips = self.members // 2
+        for hop in range(1, chips):
+            sender = lax.rem(self.me + self.members - 2 * hop, self.members)
+            for half in (0, 1):
+                place = self.swap_place(half, sender)
+                remote(
+                    place,
+                    place,
+                    self.swap_send.at[0, hop, half],
+                    self.swap_recv.at[0, hop, half],
+                    sender,
+                ).wait_recv()
+                self.pass_on(half, sender // 2, place).start()
+
+    def swap_end(self):
+        core = self.me % 2
+        for chip in range(self.members // 2):
+            for half in (0, 1):
+                place = self.swap_place(half, 2 * chip + 1 - core)
+                remote(
+                    place,
+                    place,
+                    self.swap_send.at[1, chip, half],
+                    self.swap_recv.at[1, chip, half],
+                    self.me + 1 - 2 * core,
+                ).wait_recv()
+        for half in (0, 1):
+            self.swap_local(half).wait()
+
+    def spread_sent(self):
+        chips = self.members // 2
+        for half in (0, 1):
+            self.spread_copy(half, 0).wait_send()
+            self.spread_copy(half, 1).wait_send()
+            own = self.own_rows(half)
+            for hop in range(1, chips):
+                self.hand_to(half, hop, own, lax.rem(self.me + 2 * hop, self.members)).wait_send()
+            for chip in range(chips):
+                self.pass_on(half, chip, own).wait_send()
+
+
 def sum_scratch(shape):
     dma = pltpu.SemaphoreType.DMA
     rows, width = shape[-2:]
@@ -680,6 +751,13 @@
         count = members or shape[0]
         scratch += [dma((count, 2)), dma((count, 2))]
     return scratch
+
+
+def everywhere_scratch(shape):
+    dma = pltpu.SemaphoreType.DMA
+    chips = shape[0] // 2
+    scratch = [pltpu.VMEM(shape, jnp.bfloat16), dma((2, 2)), dma((2, 2)), dma((2,))]
+    return scratch + [dma((2, chips, 2)), dma((2, chips, 2))]
 
 
 def spread_refs(columns):
@@ -1192,9 +1270,7 @@
             line.parts[chip, :, :, cols] = sums.reshape(2, line.tok, wide)
 
         line.core_copy(chip).start()
-        if step > 0:
-            line.scatter_first(line.order(step - 1))
-    line.scatter_first(line.order(chips - 1))
+        line.scatter_first(chip)
     line.scatter_rest(result_ref)
     line.gather_end()
     for chip in range(chips):
@@ -1327,9 +1403,7 @@
             line.parts[chip, :, :, cols] = sums.reshape(2, line.tok, wide)
 
         line.core_copy(chip).start()
-        if step > 0:
-            line.scatter_first(line.order(step - 1))
-    line.scatter_first(line.order(chips - 1))
+        line.scatter_first(chip)
     for one in small:
         one.middle()
     for load in loads[4:]:
@@ -1372,16 +1446,14 @@
     done = [0]
 
     def between(rank):
-        if rank == 3:
-            down_grads()
-            share.begin()
-            for one in small:
-                one.finish()
-        else:
-            upto = min(tiles, done[0] + 2)
-            gateup_grads(done[0], upto)
-            done[0] = upto
-
+        upto = min(tiles, done[0] + 2)
+        gateup_grads(done[0], upto)
+        done[0] = upto
+
+    down_grads()
+    share.begin()
+    for one in small:
+        one.finish()
     line.scatter_rest(result_ref, between)
     share.middle()
     gateup_grads(done[0], tiles)
@@ -1458,20 +1530,54 @@
     )
 
 
+class RowHeld:
+    def __init__(self, kept, part):
+        self.kept, self.part = kept, part
+
+    def own_rows(self, half):
+        return self.kept.at[half]
+
+    def held(self, half, member):
+        cols = pl.ds(pl.multiple_of(member * self.part, self.part), self.part)
+        return self.kept.at[half, :, cols]
+
+
+class SameHeld:
+    def __init__(self, shard, spread_rows):
+        self.shard, self.spread_rows = shard, spread_rows
+
+    def own_rows(self, half):
+        start, size = self.spread_rows(half)
+        return self.shard.at[pl.ds(pl.multiple_of(start, size), size)]
+
+    def held(self, half, member):
+        return self.own_rows(half)
+
+
+GAIN_ROWS = 24
+POSITION_ROW = 12
+QUERY_ROW = 13
+KEY_ROW = 15
+
+
 def attention_forward_kernel(
     chips,
-    own_ref,
-    qkv_own,
-    gate_own,
-    up_own,
+    tokens_ref,
+    packed_ref,
+    frequency_ref,
+    lengths_ref,
+    query_weight,
+    key_weight,
+    value_weight,
+    gate_weight,
+    up_weight,
     out_hbm,
+    small_hbm,
+    result_ref,
+    packed_all,
     cos_ref,
     sin_ref,
-    gain_query_ref,
-    gain_key_ref,
-    query_docs_ref,
-    key_docs_ref,
-    result_ref,
+    head_gains_ref,
     all_hbm,
     qkv_hbm,
     gateup_hbm,
@@ -1480,39 +1586,138 @@
     span_hbm,
     probs_hbm,
     attended_hbm,
+    small_all,
     *scratch,
 ):
     scratch = list(scratch)
     line = Line(chips, scratch[:LINE_REFS])
     del scratch[:LINE_REFS]
+    qkv_kept, gate_kept, up_kept = scratch[:3]
+    wide_rows, narrow_rows, row_sem = scratch[3:6]
+    own_ref, gains_send, gains_recv, query_docs, key_docs = scratch[6:11]
+    del scratch[:11]
+    ff_part = gate_kept.shape[2] // (2 * chips)
     spreads = []
-    for kept in (qkv_own, gate_own, up_own):
-        spreads.append(Spread(Held(kept), scratch[: spread_refs(True)], True))
+    for held in (Held(qkv_kept), RowHeld(gate_kept, ff_part), RowHeld(up_kept, ff_part)):
+        spreads.append(Spread(held, scratch[: spread_refs(True)], True))
         del scratch[: spread_refs(True)]
     qkv, gate, up = spreads
+    small_held = SameHeld(small_hbm, lambda half: (small.own_start(half), small.eighth))
+    small = Everywhere(small_held, scratch[: spread_refs(True)], True)
+    del scratch[: spread_refs(True)]
     out, lin, query, span, probs, attended = scratch[:6]
     load_sem, store_sem, span_send, span_recv = scratch[6:]
     width = line.slots.shape[3]
     pair = 2 * line.tok
     block = chips * pair
+    members = 2 * chips
     ctx_at = lax.axis_index("ctx")
     planes = lax.axis_size("ctx")
-    ff_part = gate.final.shape[2]
+    me = lax.axis_index("fsdp")
     bfloat = jnp.bfloat16
 
+    def row_load(weight, buffer, at):
+        return [
+            pltpu.make_async_copy(
+                weight.at[pl.ds(pl.multiple_of(qkv.own_start(half), qkv.eighth), qkv.eighth)],
+                buffer.at[half],
+                row_sem.at[at, half],
+            )
+            for half in (0, 1)
+        ]
+
+    query_rows = row_load(query_weight, wide_rows.at[0, :, :, pl.ds(0, HQ * HD)], 0)
+    key_rows = row_load(key_weight, narrow_rows.at[0], 1)
+    value_rows = row_load(value_weight, narrow_rows.at[1], 2)
+    gate_rows = row_load(gate_weight, wide_rows.at[1], 3)
+    up_rows = row_load(up_weight, wide_rows.at[0], 4)
+    for load in query_rows + key_rows + value_rows + gate_rows:
+        load.start()
     load_out = pltpu.make_async_copy(out_hbm, out, load_sem)
     load_out.start()
     greet_all()
+
+    def gains_copy(hop, source):
+        return remote(
+            packed_ref,
+            packed_all.at[source],
+            gains_send.at[hop],
+            gains_recv.at[hop],
+            lax.rem(me + hop, members),
+        )
+
+    for hop in range(1, members):
+        gains_copy(hop, me).start()
+    packed_all[me] = packed_ref[...]
+
+    for load in query_rows + key_rows + value_rows:
+        load.wait()
+    for half in (0, 1):
+        for member in range(members):
+            head = member * KV // members
+            qkv_kept[half, member, :, :HD] = wide_rows[
+                0, half, :, member * HD : (member + 1) * HD
+            ].astype(bfloat)
+            for side in (0, 1):
+                qkv_kept[half, member, :, (1 + side) * HD : (2 + side) * HD] = narrow_rows[
+                    side, half, :, head * HD : (head + 1) * HD
+                ].astype(bfloat)
     qkv.swap_begin()
+    for load in up_rows:
+        load.start()
+    for hop in range(1, members):
+        gains_copy(hop, lax.rem(me + members - hop, members)).wait_recv()
+
+    inputs = tokens_ref[...].astype(jnp.float32)
+    scale = lax.rsqrt(jnp.mean(inputs * inputs, axis=-1, keepdims=True) + EPSILON)
+    gain = jnp.concatenate(
+        [packed_all[member, row : row + 1] for member in range(members) for row in (0, 1)], axis=1
+    )
+    own_ref[...] = (inputs * scale * gain).astype(bfloat)
     line.gather_begin(own_ref)
+
+    for load in gate_rows + up_rows:
+        load.wait()
+    gate_kept[...] = wide_rows[1].astype(bfloat)
+    up_kept[...] = wide_rows[0].astype(bfloat)
+    for at, row in ((0, QUERY_ROW), (1, KEY_ROW)):
+        total = packed_all[0, row : row + 2]
+        for member in range(1, members):
+            total = total + packed_all[member, row : row + 2]
+        head_gains_ref[at : at + 1] = jnp.concatenate([total[0:1], total[1:2]], axis=1)
+    gain_query, gain_key = head_gains_ref[0:1], head_gains_ref[1:2]
+
     line.gather_step(1)
     qkv.swap_end()
     qkv.spread_begin()
+
+    places = ctx_at * block + lax.broadcasted_iota(jnp.int32, (block, 1), 0)
+    spots = ctx_at * block - WINDOW + lax.broadcasted_iota(jnp.int32, (1, WINDOW + block), 1)
+    doc_end = 0
+    query_doc = jnp.zeros(places.shape, jnp.int32)
+    key_doc = jnp.where(spots >= 0, 0, -1)
+    for doc in range(lengths_ref.shape[0] - 1):
+        doc_end = doc_end + lengths_ref[doc]
+        query_doc = query_doc + jnp.where(places >= doc_end, 1, 0)
+        key_doc = key_doc + jnp.where(spots >= doc_end, 1, 0)
+    query_docs[...] = query_doc
+    key_docs[...] = key_doc
+    positions = jnp.concatenate(
+        [packed_all[member, POSITION_ROW : POSITION_ROW + 1] for member in range(members)], axis=0
+    )
+    columns = jnp.transpose(positions)
+    for member in range(members):
+        angle = columns[:, member : member + 1] * frequency_ref[...]
+        token_rows = pl.ds(member * line.tok, line.tok)
+        cos_ref[token_rows] = jnp.cos(angle)
+        sin_ref[token_rows] = jnp.sin(angle)
+
     line.gather_step(2)
+    small.swap_begin()
+    gate.swap_begin()
     qkv.spread_on()
     for distance in range(3, chips):
         line.gather_step(distance)
-    gate.swap_begin()
     up.swap_begin()
     line.own_copy(own_ref).wait()
     for chip in range(chips):
@@ -1532,6 +1737,7 @@
         pltpu.make_async_copy(
             up.final, gateup_hbm.at[:, :, pl.ds(ff_part, ff_part)], store_sem.at[8]
         ),
+        pltpu.make_async_copy(small.final, small_all, store_sem.at[9]),
     ]
     stores[0].start()
     stores[1].start()
@@ -1545,7 +1751,7 @@
         key_lin = dot_nn(inputs, weights[:, HD : 2 * HD])
         lin[rows, HD : 2 * HD] = key_lin
         span[0, span_rows] = rope_norm(
-            key_lin, gain_key_ref[...], cos_ref[rows], sin_ref[rows]
+            key_lin, gain_key, cos_ref[rows], sin_ref[rows]
         ).astype(bfloat)
         span[1, span_rows] = dot_nn(inputs, weights[:, 2 * HD :]).astype(bfloat)
 
@@ -1582,7 +1788,7 @@
         weights = qkv.final[...].reshape(width, 3 * HD)
         query_lin = dot_nn(inputs, weights[:, :HD])
         lin[rows, :HD] = query_lin
-        rotated = rope_norm(query_lin, gain_query_ref[...], cos_ref[rows], sin_ref[rows])
+        rotated = rope_norm(query_lin, gain_query, cos_ref[rows], sin_ref[rows])
         query[rows] = (rotated.astype(bfloat).astype(jnp.float32) * SCORE_SCALE).astype(bfloat)
 
     @pl.when(ctx_at > 0)
@@ -1594,6 +1800,7 @@
     for store in stores[2:5]:
         store.start()
     load_out.wait()
+    small.swap_on()
 
     span_len = WINDOW + pair
     for step in range(chips):
@@ -1609,7 +1816,7 @@
         visible = (
             (distance >= 0)
             & (distance < WINDOW)
-            & (query_docs_ref[rows] == key_docs_ref[:, span_rows])
+            & (query_docs[rows] == key_docs[:, span_rows])
         )
         scores = jnp.where(visible, scores, NEGATIVE)
         shifted = jnp.exp(scores - jnp.max(scores, axis=-1, keepdims=True))
@@ -1626,25 +1833,35 @@
             line.parts[chip, :, :, cols] = sums.reshape(2, line.tok, wide)
 
         line.core_copy(chip).start()
-        if step > 0:
-            line.scatter_first(line.order(chips - step))
-        if step == 1:
+        line.scatter_first(chip)
+        if step == 0:
             gate.swap_end()
             gate.spread_begin()
-    line.scatter_first(line.order(0))
+            small.swap_end()
+            small.spread_begin()
     for store in stores[5:7]:
         store.start()
     gate.spread_on()
-    up.swap_end()
-    up.spread_begin()
-    line.scatter_rest(result_ref)
-    up.spread_on()
+
+    def between(rank):
+        if rank == 3:
+            up.swap_end()
+            up.spread_begin()
+            small.spread_on()
+        if rank == 2 * chips - 3:
+            up.spread_on()
+
+    line.scatter_rest(result_ref, between)
     gate.spread_end()
     stores[7].start()
     up.spread_end()
     stores[8].start()
+    small.spread_end()
+    stores[9].start()
     line.gather_end()
-    for spread in spreads:
+    for hop in range(1, members):
+        gains_copy(hop, me).wait_send()
+    for spread in spreads + [small]:
         spread.spread_sent()
 
     @pl.when(ctx_at < planes - 1)
@@ -1660,15 +1877,15 @@
 
 
 def attention_forward(
-    own, qkv_own, gate_own, up_own, out, cosine, sine_part, gain_query, gain_key, query_docs, key_docs
+    tokens, packed, frequency, lengths, query_weight, key_weight, value_weight, gate, up, out, small
 ):
-    tok_count, width = own.shape
-    members = qkv_own.shape[1]
+    tok_count, width = tokens.shape
+    rows = query_weight.shape[0]
+    members = width // rows
     chips = members // 2
     block = members * tok_count
     span_len = WINDOW + block
-    rows = 8 * qkv_own.shape[2]
-    ff_part = gate_own.shape[3]
+    ff_part = gate.shape[1] // members
     bfloat = jnp.bfloat16
     anywhere = pl.BlockSpec(memory_space=pl.ANY)
     vmem = pl.BlockSpec(memory_space=pltpu.VMEM)
@@ -1682,22 +1899,40 @@
     ]
     outputs = [
         ((tok_count, width), jnp.float32),
+        ((members,) + packed.shape, jnp.float32),
+        ((block, HD // 2), jnp.float32),
+        ((block, HD // 2), jnp.float32),
+        ((2, HD), jnp.float32),
         ((chips, 2, tok_count, width), bfloat),
         ((members, rows, 3 * HD), bfloat),
         ((members, rows, 2 * ff_part), bfloat),
-    ] + kept
+    ] + kept + [((members,) + small.shape, bfloat)]
     return pl.pallas_call(
         functools.partial(attention_forward_kernel, chips),
         out_shape=[jax.ShapeDtypeStruct(*output) for output in outputs],
-        in_specs=[vmem] + [anywhere] * 4 + [vmem] * 6,
-        out_specs=[vmem] + [anywhere] * 8,
+        in_specs=[vmem] * 3 + [pl.BlockSpec(memory_space=pltpu.SMEM)] + [anywhere] * 7,
+        out_specs=[vmem] * 5 + [anywhere] * 9,
         scratch_shapes=line_scratch(chips, tok_count, width)
+        + [
+            pltpu.VMEM((2, members, rows // 8, 3 * HD), bfloat),
+            pltpu.VMEM((2, rows // 8, gate.shape[1]), bfloat),
+            pltpu.VMEM((2, rows // 8, gate.shape[1]), bfloat),
+            pltpu.VMEM((2, 2, rows // 8, gate.shape[1]), jnp.float32),
+            pltpu.VMEM((2, 2, rows // 8, KV * HD), jnp.float32),
+            dma((5, 2)),
+            pltpu.VMEM((tok_count, width), bfloat),
+            dma((members,)),
+            dma((members,)),
+            pltpu.VMEM((block, 1), jnp.int32),
+            pltpu.VMEM((1, span_len), jnp.int32),
+        ]
         + spread_scratch((members, rows, 3 * HD))
         + spread_scratch((members, rows, ff_part))
         + spread_scratch((members, rows, ff_part))
+        + everywhere_scratch((members,) + small.shape)
         + [pltpu.VMEM(out.shape, bfloat)]
         + [pltpu.VMEM(*one) for one in kept]
-        + [dma, dma((9,)), dma((2,)), dma((2,))],
+        + [dma, dma((10,)), dma((2,)), dma((2,))],
         compiler_params=pltpu.CompilerParams(
             collective_id=4, has_side_effects=True, vmem_limit_bytes=KERNEL_VMEM
         ),
@@ -1706,17 +1941,17 @@
         ),
         name="attention_forward",
     )(
-        own,
-        qkv_own,
-        gate_own,
-        up_own,
+        tokens,
+        packed,
+        frequency,
+        lengths,
+        query_weight,
+        key_weight,
+        value_weight,
+        gate,
+        up,
         out,
-        cosine,
-        sine_part,
-        gain_query,
-        gain_key,
-        query_docs,
-        key_docs,
+        small,
     )
 
 def rope_norm_back(grad, lin, gain, cosine, sine_part):
@@ -2050,90 +2285,85 @@
     ctx_at = lax.axis_index("ctx")
     fsdp_at = lax.axis_index("fsdp")
 
-    gain_list = [
-        attn_in_gain,
-        query_gain,
-        key_gain,
-        attn_out_gain,
-        laurel_gain,
-        ffn_in_gain,
-        ffn_out_gain,
-        ple_gain,
+    wide_gains = (attn_in_gain, attn_out_gain, laurel_gain, ffn_in_gain, ffn_out_gain, ple_gain)
+    head_starts = fsdp_at * query_gain.shape[0]
+    head_parts = [
+        lax.dynamic_update_slice_in_dim(jnp.zeros((HD,), jnp.float32), gain, head_starts, 0)
+        for gain in (query_gain, key_gain)
     ]
-    gain_sizes = [g.shape[0] for g in gain_list]
-    gain_offsets = [sum(gain_sizes[:n]) for n in range(len(gain_sizes) + 1)]
-    packed = jnp.concatenate(gain_list + [positions.astype(jnp.float32)])
-    packed = jnp.pad(packed, (0, -packed.shape[0] % 1024)).reshape(1, -1, 128)
-    packed = lax.all_gather(packed, "fsdp", axis=0, tiled=True).reshape(fsdp_count, -1)
-    gain_in, gain_query, gain_key, gain_post, gain_laurel, gain_ffin, gain_ffout, gain_ple = (
-        packed[:, gain_offsets[n] : gain_offsets[n + 1]].reshape(-1) for n in range(8)
-    )
-    block_positions = packed[:, gain_offsets[8] : gain_offsets[8] + tok_count].reshape(-1)
-    cosine, sine_part = rope_tables(block_positions, HD)
-    cosine, sine_part = cosine[:, 0], sine_part[:, 0]
-
-    group_size = HQ // KV
-    eighth = rows // 8
-    at_x, at_y = ctx_at % 2, ctx_at // 2
-
-    def own_rows(weight, width):
-        starts = (at_x * 2 + at_y, 4 + at_y * 2 + at_x)
-        halves = [lax.dynamic_slice_in_dim(weight, n * eighth, eighth, 0) for n in starts]
-        held = jnp.stack(halves).astype(bfloat)
-        return jnp.transpose(held.reshape(2, eighth, -1, width), (0, 2, 1, 3))
-
-    qkv_own = jnp.concatenate(
-        [
-            own_rows(w_query, HD),
-            jnp.repeat(own_rows(w_key, HD), group_size, axis=1),
-            jnp.repeat(own_rows(w_value, HD), group_size, axis=1),
-        ],
-        axis=3,
-    )
-    gate_own, up_own = own_rows(w_gate, ff_part), own_rows(w_up, ff_part)
+    packed = jnp.concatenate(list(wide_gains) + [positions.astype(jnp.float32)] + head_parts)
+    packed = jnp.pad(packed, (0, GAIN_ROWS * 128 - packed.shape[0])).reshape(GAIN_ROWS, 128)
+    frequency = jnp.exp(
+        jnp.arange(HD // 2, dtype=jnp.float32) * (-2.0 * math.log(ROPE_BASE) / HD)
+    )
+
     out_low = w_out.astype(bfloat)
     down_low = w_down.astype(bfloat)
-    width = tokens.shape[1]
-    small_weights = (ple_gate, ple_proj, laurel_left, laurel_right)
-    small_sizes = [weight.size // width for weight in small_weights]
-    small_total = sum(small_sizes)
-    share_rows = -(-small_total // (8 * ctx_count)) * 8
-    small_packed = jnp.concatenate(
-        [weight.astype(bfloat).reshape(-1, width) for weight in small_weights]
-        + [jnp.zeros((share_rows * ctx_count - small_total, width), bfloat)]
-    )
-    small_share = lax.dynamic_slice_in_dim(small_packed, ctx_at * share_rows, share_rows, 0)
-    small_full = lax.all_gather(small_share, ("ctx", "fsdp"), axis=0, tiled=False)
-    small_full = small_full.reshape(ctx_count, fsdp_count, share_rows, width)
-    small_full = jnp.transpose(small_full, (1, 0, 2, 3)).reshape(fsdp_count, -1, width)
-    small_ends = [sum(small_sizes[:n]) for n in range(5)]
-    full_pgate, full_pproj, full_left, full_right = (
-        small_full[:, small_ends[n] : small_ends[n + 1]].reshape(-1, weight.shape[1])
-        for n, weight in enumerate(small_weights)
+    def in_halves(weight):
+        return jnp.concatenate(jnp.split(weight.astype(bfloat), rows // 128, axis=0), axis=1)
+
+    def in_stacks(weight):
+        pieces = weight.astype(bfloat).reshape(weight.shape[0], 128 // weight.shape[0], -1)
+        return jnp.transpose(pieces, (1, 0, 2)).reshape(128, -1)
+
+    small = jnp.concatenate(
+        [in_halves(ple_gate), in_stacks(ple_proj), in_halves(laurel_left), in_stacks(laurel_right)],
+        axis=1,
     )
 
     inputs = tokens.astype(jnp.float32)
     ple_input = per_layer.astype(jnp.float32)
+    (
+        projected,
+        packed_all,
+        cosine,
+        sine_part,
+        head_gains,
+        normed_all,
+        qkv_full,
+        gateup_full,
+        qk_lin,
+        query_low,
+        span_kv,
+        probs,
+        attended_low,
+        small_all,
+    ) = attention_forward(
+        tokens,
+        packed,
+        frequency[None, :],
+        doc_lengths,
+        w_query,
+        w_key,
+        w_value,
+        w_gate,
+        w_up,
+        out_low,
+        small,
+    )
+    small_ends = [0]
+    for weight in (ple_gate, ple_proj, laurel_left, laurel_right):
+        small_ends.append(small_ends[-1] + weight.size // 128)
+    small_cols = [small_all[:, :, small_ends[n] : small_ends[n + 1]] for n in range(4)]
+
+    def side_by_side(cols, shape):
+        pieces = jnp.split(cols, cols.shape[2] // shape[1], axis=2)
+        return jnp.concatenate(pieces, axis=1).reshape(-1, shape[1])
+
+    def stacked(cols, shape):
+        pieces = cols.reshape(fsdp_count, -1, shape[0], cols.shape[2])
+        return jnp.transpose(pieces, (0, 2, 1, 3)).reshape(-1, shape[1])
+
+    full_pgate = side_by_side(small_cols[0], ple_gate.shape)
+    full_pproj = stacked(small_cols[1], ple_proj.shape)
+    full_left = side_by_side(small_cols[2], laurel_left.shape)
+    full_right = stacked(small_cols[3], laurel_right.shape)
+    wide_rows = attn_in_gain.shape[0] // 128
+    gain_in, gain_post, gain_laurel, gain_ffin, gain_ffout, gain_ple = (
+        packed_all[:, n * wide_rows : (n + 1) * wide_rows].reshape(-1) for n in range(6)
+    )
     normed, norm_back = jax.vjp(rms_norm, inputs, gain_in)
     normed_low = normed.astype(bfloat)
-    block_start = ctx_at * block_len
-    places = block_start - WINDOW + jnp.arange(WINDOW + block_len, dtype=jnp.int32)
-    key_docs = jnp.where(places >= 0, document_ids(doc_lengths, places), -1)
-    projected, normed_all, qkv_full, gateup_full, qk_lin, query_low, span_kv, probs, attended_low = (
-        attention_forward(
-            normed_low,
-            qkv_own,
-            gate_own,
-            up_own,
-            out_low,
-            cosine,
-            sine_part,
-            gain_query[None, :],
-            gain_key[None, :],
-            key_docs[WINDOW:, None],
-            key_docs[None, :],
-        )
-    )
     normed_all = normed_all.reshape(block_len, -1)
     col_qkv = qkv_full.reshape(normed_all.shape[1], -1)
     col_gateup = gateup_full.reshape(normed_all.shape[1], -1)
@@ -2204,8 +2434,8 @@
             probs,
             cosine,
             sine_part,
-            gain_query[None, :],
-            gain_key[None, :],
+            head_gains[0:1],
+            head_gains[1:2],
             part_gateup,
             held_wdown,
             normed_all,
@@ -2223,13 +2453,13 @@
 
     grad_gains = [
         grad_gin,
-        grad_gquery,
-        grad_gkey,
         grad_gpost,
         grad_glaurel,
         grad_gffin,
         grad_gffout,
         grad_gple,
+        grad_gquery,
+        grad_gkey,
     ]
     gain_parts = jnp.concatenate([g.reshape(fsdp_count, -1) for g in grad_gains], axis=1)
     gain_parts = jnp.pad(gain_parts, ((0, 0), (0, 128 * 128 - gain_parts.shape[1])))
@@ -2256,10 +2486,13 @@
             Source(held_pgate, summed=True, groups=1, sides=1),
             Source(held_pproj, summed=True, groups=1, sides=1),
             Source(part_laurel, groups=1, sides=1),
-            Source(gain_parts),
+            Source(gain_parts, groups=1),
         ]
     )
-    gain_sums = jnp.sum(sum_gains.astype(jnp.float32), axis=0).reshape(-1)
+    gain_sums = sum_gains.astype(jnp.float32).reshape(-1)
+    wide_size, head_size = attn_in_gain.shape[0], query_gain.shape[0]
+    wide_sums = gain_sums[: 6 * wide_size].reshape(6, wide_size)
+    head_sums = gain_sums[6 * wide_size : 6 * wide_size + 2 * head_size].reshape(2, head_size)
     grad_wgate = sum_wgate.astype(jnp.float32)
     grad_wup = sum_wup.astype(jnp.float32)
     grad_wdown = sum_wdown.astype(jnp.float32)
@@ -2287,7 +2520,10 @@
         grad_wdown,
         grad_pgate,
         grad_pproj,
-        *(gain_sums[gain_offsets[n] : gain_offsets[n + 1]] for n in range(8)),
+        wide_sums[0],
+        head_sums[0],
+        head_sums[1],
+        *(wide_sums[n] for n in range(1, 6)),
     )
 
 

time: 791 us -> 736 us (0.930)
  blocking collectives: 15.6 us -> 0 us
  Pallas kernels: 645 us -> 631 us
  between operations: 15.3 us -> 1.66 us
    all_gather x1 -> x0, blocking collectives: 15.6 us -> none  [by_heads(): lax.all_gather(packed, 'fsdp', axis=0, tiled=True).reshape(fsdp_count, -1)]
    pallas_call x1, Pallas kernels: 88.7 us -> 73.5 us  [ffn_forward(): pl.pallas_call(functools.partial(ffn_forward_kernel, chips), out_shape=[j...]
    pallas_call x1, Pallas kernels: 184 us -> 198 us  [attention_forward(): pl.pallas_call(functools.partial(attention_forward_kernel, chips), out_sh...]
    pallas_call x1, Pallas kernels: 104 us -> 93 us  [ffn_backward(): pl.pallas_call(functools.partial(ffn_backward_kernel, chips), out_shape=[...]
  transfers between devices with their start and end apart: 1 -> 0, of which waited for: 0 -> 0; matrix products, arithmetic and copies ran while one was open for 3% -> 0% of each run, Pallas kernels for 24% -> 0%
where the time goes in v6:
time: 736 us; the launch traced here: 727 us
  Pallas kernels  631 us (86%)
  other arithmetic  58.8 us (8%)
  local copies, waits for them, and re-layouts  24.3 us (3%)
  matrix products  11.1 us (2%)
    pallas_call x1, Pallas kernels, attention_forward(): pl.pallas_call(functools.partial(attention_forward_kernel, chips), out_sh...  198 us
    pallas_call x1, Pallas kernels, gradient_sum(): pl.pallas_call(functools.partial(gradient_sum_kernel, sources), out_shape...  145 us
    pallas_call x1, Pallas kernels, attention_backward(): pl.pallas_call(functools.partial(attention_backward_kernel, chips), out_s...  122 us
    pallas_call x1, Pallas kernels, ffn_backward(): pl.pallas_call(functools.partial(ffn_backward_kernel, chips), out_shape=[...  93 us
    pallas_call x1, Pallas kernels, ffn_forward(): pl.pallas_call(functools.partial(ffn_forward_kernel, chips), out_shape=[j...  73.5 us

profile of v6, /device:TPU:0, one launch (start us, length us, event | category | flops | bytes accessed | tf_op | source)
XLA Modules:
  0.0 726.6 jit_solution(1955424361987683587)
XLA Ops:
  0.7 1.4 fusion.17
  15.4 6.0 convert_element_type.123.down_hbm
  21.4 197.6 %attention_forward.1 = (f32[128,2048]{1,0:T(8,128)}, f32[8,24,128]{2,1,0:T(8,128)}, f32[1024,128]{1,0:T(8,128)}, f32[1024,128]{1,0:T(8,128)}, f32[2,256]{1,0:T(2...) custom-call(bf16[128,2048]{1,0:T(8,128)(2,1)} %tokens_ref.1, ...), custom_call_target="tpu_custom_call" | custom-call | flops 8589934592 | bytes 314572800 | tf_op jit(solution)/shard_map/attention_forward/pallas_call | solution.py:1910
  220.1 1.4 multiply_reduce_fusion.12
  221.5 1.3 fusion.55
  222.8 1.2 fusion.50
  226.3 1.2 copy.56
  231.0 73.5 %ffn_forward.1 = (f32[128,2048]{1,0:T(8,128)}, bf16[4,2,128,2048]{3,2,1,0:T(8,128)(2,1)}, bf16[1024,1024]{1,0:T(8,128)(2,1)}, bf16[1024,1024]{1,0:T(8,128)(2,1)}, bf16[1024,1024]{1,0:T(8,128)(2,1)}) custom-call(bf16[128,2048]{1,0:T(8,128)(2,1)} %multiply_convert_fusion.own_ref, bf16[2048,2048]{1,0:T(8,128)(2,1)} %bitcast.108, ...), custom_call_target="tpu_custom_call" | custom-call | flops 12884901888 | bytes 41943040 | tf_op jit(solution)/shard_map/ffn_forward/pallas_call | solution.py:1289
  304.5 1.5 multiply_reduce_fusion.9
  306.0 1.5 multiply_add_fusion
  309.7 2.7 fusion.11
  313.8 1.4 convolution_convert_fusion.1
  315.3 1.6 multiply_reduce_fusion
  316.9 2.3 fusion.12.own_ref
  319.6 1.5 reshape.319.pproj_hbm
  321.1 93.0 %ffn_backward.1 = (f32[128,2048]{1,0:T(8,128)}, bf16[8,256,2048]{2,1,0:T(8,128)(2,1)}, bf16[2,128,2048]{2,1,0:T(8,128)(2,1)}, bf16[2,8,32,256]{3,2,1,0:T(8,128)(2,1)}, bf16[2,8,16,512]{3,2,1,0:T(8,128)(2,1)}) custom-call(bf16[128,2048]{1,0:T(8,128)(2,1)} %fusion.12.own_ref, bf16[2048,2048]{1,0:T(8,128)(2,1)} %bitcast.109, ...), custom_call_target="tpu_custom_call" | custom-call | flops 25769803776 | bytes 41943040 | tf_op jit(solution)/shard_map/ffn_backward/pallas_call | solution.py:1489
  414.1 1.6 multiply_reduce_fusion.1
  415.7 3.7 multiply_reduce_fusion.2
  419.4 2.8 fusion.14
  422.2 1.4 convolution_convert_fusion.4
  423.7 121.9 %attention_backward.1 = (f32[128,2048]{1,0:T(8,128)}, bf16[8,256,256]{2,1,0:T(8,128)(2,1)}, bf16[8,256,512]{2,1,0:T(8,128)(2,1)}, bf16[256,2048]{1,0:T(8,128)(2,...) custom-call(bf16[128,2048]{1,0:T(8,128)(2,1)} %get-tuple-element.174.own_ref, ...), custom_call_target="tpu_custom_call" | custom-call | flops 8589934592 | bytes 314572800 | tf_op jit(solution)/shard_map/attention_backward/pallas_call | solution.py:2200
  545.6 2.9 fusion.8
  548.6 2.6 fusion.16
  554.4 144.7 %gradient_sum.1 = (bf16[256,8192]{1,0:T(8,128)(2,1)}, bf16[256,8192]{1,0:T(8,128)(2,1)}, bf16[256,2048]{1,0:T(8,128)(2,1)}, bf16[256,512]{1,0:T(8,128)(2,1)}, bf...) custom-call(bf16[2,8,32,2048]{3,2,1,0:T(8,128)(2,1)} %get-tuple-elem, ...), custom_call_target="tpu_custom_call" | custom-call | bytes 314572800 | tf_op jit(solution)/shard_map/gradient_sum/pallas_call | solution.py:899
  703.4 1.6 convert_element_type.146
  705.0 1.8 reshape.343
  706.8 1.8 convert_element_type.140
  709.5 1.6 convert_element_type.139
  711.0 1.6 convert_element_type.142
  712.9 4.4 convert_element_type.143
  717.3 4.4 convert_element_type.144
  721.7 4.4 convert_element_type.145
  (139 shorter events, 32.7 us)
Async XLA Ops:
  0.7 13.6 %copy-start.21 = (f32[256,2048]{1,0:T(8,128)S(1)}, f32[256,2048]{1,0:T(8,128)}, u32[]{:S(2)}) copy-start(f32[256,2048]{1,0:T(8,128)} %param.32) | copy-start | bytes 6291460
  219.1 5.9 copy-start.10
  219.1 6.3 copy-start.20
  224.2 0.8 copy-start.24
  227.5 1.6 copy-start.1
  229.1 1.0 copy-start.3
  304.5 3.0 copy-start.7
  306.0 1.9 copy-start.18
  306.0 1.9 copy-start.27
  307.6 2.2 copy-start.4
  307.6 1.8 copy-start.11
  308.4 1.0 copy-start.9
  309.7 2.7 copy-start.19
  312.4 4.4 copy-start.22
  312.4 1.4 copy-start.5
  312.4 2.8 copy-start
  312.4 2.9 copy-start.8
  312.4 2.8 copy-start.12
  316.8 2.3 copy-start.23
  414.1 1.6 copy-start.2
  422.2 1.4 copy-start.13
  423.7 122.0 %copy-start.6 = (f32[128,2048]{1,0:T(8,128)S(1)}, f32[128,2048]{1,0:T(8,128)}, u32[]{:S(2)}) copy-start(f32[128,2048]{1,0:T(8,128)} %get-tuple-element.164) | copy-start | bytes 3145732
  548.6 2.7 copy-start.29
  548.6 4.1 copy-start.14
  699.1 9.5 %copy-start.28 = (bf16[256,512]{1,0:T(8,128)(2,1)S(1)}, bf16[256,512]{1,0:T(8,128)(2,1)}, u32[]{:S(2)}) copy-start(bf16[256,512]{1,0:T(8,128)(2,1)} %get-tuple-element.95) | copy-start | bytes 786436
  699.1 10.4 %copy-start.26 = (bf16[256,2048]{1,0:T(8,128)(2,1)S(1)}, bf16[256,2048]{1,0:T(8,128)(2,1)}, u32[]{:S(2)}) copy-start(bf16[256,2048]{1,0:T(8,128)(2,1)} %get-tuple-element.93) | copy-start | bytes 3145732
  705.0 6.0 copy-start.25
  709.5 3.4 copy-start.17
  712.9 4.4 copy-start.16
  717.3 4.4 copy-start.15

commit v7 on v6

--- a/solution.py
+++ b/solution.py
@@ -629,11 +629,11 @@
         for half in (0, 1):
             self.spread_wait(half, 1)
 
-    def spread_sent(self):
+    def spread_sent(self, swapped=True):
         for half in (0, 1):
             self.spread_copy(half, 0).wait_send()
             self.spread_copy(half, 1).wait_send()
-            if self.columns:
+            if self.columns and swapped:
                 for hop in range(1, self.members):
                     self.swap_copy(half, hop, self.me).wait_send()
 
@@ -719,10 +719,14 @@
             self.swap_local(half).wait()
 
     def spread_sent(self):
-        chips = self.members // 2
         for half in (0, 1):
             self.spread_copy(half, 0).wait_send()
             self.spread_copy(half, 1).wait_send()
+        self.swap_sent()
+
+    def swap_sent(self):
+        chips = self.members // 2
+        for half in (0, 1):
             own = self.own_rows(half)
             for hop in range(1, chips):
                 self.hand_to(half, hop, own, lax.rem(self.me + 2 * hop, self.members)).wait_send()
@@ -1009,27 +1013,6 @@
             picked = picked + jnp.where(self.chip == chip, near[step], 0)
         return picked
 
-    def barrier(self):
-        sem = pltpu.get_barrier_semaphore()
-
-        def greet(place):
-            pl.semaphore_signal(
-                sem, inc=1, device_id={"fsdp": place}, device_id_type=pl.DeviceIdType.MESH
-            )
-
-        greet(self.place(self.chip, 1 - self.core))
-
-        @pl.when(self.chip > 0)
-        def _():
-            greet(self.place(self.chip - 1, self.core))
-
-        @pl.when(self.chip < self.chips - 1)
-        def _():
-            greet(self.place(self.chip + 1, self.core))
-
-        ends = jnp.where(self.chip == 0, 1, 0) + jnp.where(self.chip == self.chips - 1, 1, 0)
-        pl.semaphore_wait(sem, 3 - ends)
-
     def slot_copy(self, src, chip, way):
         place = (
             self.place(self.chip + 1, self.core),
@@ -1200,25 +1183,34 @@
     own_ref,
     gateup_hbm,
     down_hbm,
+    ple_held,
     result_ref,
     all_hbm,
     hidden_hbm,
     act_hbm,
     slope_hbm,
+    ple_hbm,
+    down_low,
     *scratch,
 ):
     line = Line(chips, scratch[:LINE_REFS])
-    gateup, down, hidden, act, slope, load_sems, store_sems = scratch[LINE_REFS:]
+    gateup, down, hidden, act, slope, load_sems, store_sems = scratch[LINE_REFS : LINE_REFS + 7]
+    down_wide = scratch[LINE_REFS + 7]
+    ple = Spread(Held(ple_held), scratch[LINE_REFS + 8 :], True)
     ff_part = down.shape[0]
     width = down.shape[1]
     pair = 2 * line.tok
     load_gateup = pltpu.make_async_copy(gateup_hbm, gateup, load_sems.at[0])
-    load_down = pltpu.make_async_copy(down_hbm, down, load_sems.at[1])
+    load_down = pltpu.make_async_copy(down_hbm, down_wide, load_sems.at[1])
+    store_down = pltpu.make_async_copy(down, down_low, load_sems.at[3])
     load_gateup.start()
     load_down.start()
-    line.barrier()
+    greet_all()
     line.gather_begin(own_ref)
+    ple.place_all()
+    ple.spread_begin()
     line.own_copy(own_ref).wait()
+    store_ple = pltpu.make_async_copy(ple.final, ple_hbm, load_sems.at[2])
 
     def stores(chip):
         rows = pl.ds(pl.multiple_of(chip * pair, pair), pair)
@@ -1238,6 +1230,8 @@
         if step == 0:
             load_gateup.wait()
             load_down.wait()
+            down[...] = down_wide[...].astype(jnp.bfloat16)
+            store_down.start()
         rows = pl.ds(pl.multiple_of(chip * pair, pair), pair)
 
         @pl.loop(0, ff_part // tile)
@@ -1271,14 +1265,20 @@
 
         line.core_copy(chip).start()
         line.scatter_first(chip)
+    ple.spread_on()
     line.scatter_rest(result_ref)
+    ple.spread_end()
+    store_ple.start()
     line.gather_end()
+    ple.spread_sent(False)
+    store_ple.wait()
+    store_down.wait()
     for chip in range(chips):
         for copy in stores(chip):
             copy.wait()
 
 
-def ffn_forward(own, gateup, down, chips):
+def ffn_forward(own, gateup, down, ple, chips):
     tok_count, width = own.shape
     ff_part = down.shape[0]
     block = 2 * chips * tok_count
@@ -1286,7 +1286,8 @@
     anywhere = pl.BlockSpec(memory_space=pl.ANY)
     vmem = pl.BlockSpec(memory_space=pltpu.VMEM)
     part = jax.ShapeDtypeStruct((block, ff_part), bfloat)
-    result, gathered, hidden, act, slope = pl.pallas_call(
+    ple_shape = (ple.shape[1], 8 * ple.shape[2], ple.shape[3])
+    result, gathered, hidden, act, slope, ple_all, down_low = pl.pallas_call(
         functools.partial(ffn_forward_kernel, chips),
         out_shape=[
             jax.ShapeDtypeStruct((tok_count, width), jnp.float32),
@@ -1294,9 +1295,11 @@
             part,
             part,
             part,
+            jax.ShapeDtypeStruct(ple_shape, bfloat),
+            jax.ShapeDtypeStruct(down.shape, bfloat),
         ],
-        in_specs=[vmem, anywhere, anywhere],
-        out_specs=[vmem, anywhere, anywhere, anywhere, anywhere],
+        in_specs=[vmem, anywhere, anywhere, anywhere],
+        out_specs=[vmem] + [anywhere] * 6,
         scratch_shapes=line_scratch(chips, tok_count, width)
         + [
             pltpu.VMEM(gateup.shape, bfloat),
@@ -1304,9 +1307,11 @@
             pltpu.VMEM((block, ff_part), bfloat),
             pltpu.VMEM((block, ff_part), bfloat),
             pltpu.VMEM((block, ff_part), bfloat),
-            pltpu.SemaphoreType.DMA((2,)),
+            pltpu.SemaphoreType.DMA((4,)),
             pltpu.SemaphoreType.DMA((chips, 4)),
-        ],
+            pltpu.VMEM(down.shape, down.dtype),
+        ]
+        + spread_scratch(ple_shape),
         compiler_params=pltpu.CompilerParams(
             collective_id=1, has_side_effects=True, vmem_limit_bytes=KERNEL_VMEM
         ),
@@ -1316,8 +1321,8 @@
             transcendentals=block * ff_part,
         ),
         name="ffn_forward",
-    )(own, gateup, down)
-    return result, gathered.reshape(block, width), hidden, act, slope
+    )(own, gateup, down, ple)
+    return result, gathered.reshape(block, width), hidden, act, slope, ple_all, down_low
 
 
 def ffn_backward_kernel(
@@ -1573,6 +1578,7 @@
     up_weight,
     out_hbm,
     small_hbm,
+    ple_hbm,
     result_ref,
     packed_all,
     cos_ref,
@@ -1587,6 +1593,7 @@
     probs_hbm,
     attended_hbm,
     small_all,
+    ple_held,
     *scratch,
 ):
     scratch = list(scratch)
@@ -1605,6 +1612,9 @@
     small_held = SameHeld(small_hbm, lambda half: (small.own_start(half), small.eighth))
     small = Everywhere(small_held, scratch[: spread_refs(True)], True)
     del scratch[: spread_refs(True)]
+    ple_source = SameHeld(ple_hbm, lambda half: (ple.own_start(half), ple.eighth))
+    ple = Everywhere(ple_source, scratch[: spread_refs(True)], True)
+    del scratch[: spread_refs(True)]
     out, lin, query, span, probs, attended = scratch[:6]
     load_sem, store_sem, span_send, span_recv = scratch[6:]
     width = line.slots.shape[3]
@@ -1719,6 +1729,7 @@
     for distance in range(3, chips):
         line.gather_step(distance)
     up.swap_begin()
+    ple.swap_begin()
     line.own_copy(own_ref).wait()
     for chip in range(chips):
         line.gather_other(chip)
@@ -1738,6 +1749,13 @@
             up.final, gateup_hbm.at[:, :, pl.ds(ff_part, ff_part)], store_sem.at[8]
         ),
         pltpu.make_async_copy(small.final, small_all, store_sem.at[9]),
+    ] + [
+        pltpu.make_async_copy(
+            ple.rows(ple.final, ple.own_start(half), ple.eighth),
+            ple_held.at[half],
+            store_sem.at[10 + half],
+        )
+        for half in (0, 1)
     ]
     stores[0].start()
     stores[1].start()
@@ -1848,10 +1866,14 @@
             up.swap_end()
             up.spread_begin()
             small.spread_on()
+            ple.swap_on()
         if rank == 2 * chips - 3:
             up.spread_on()
 
     line.scatter_rest(result_ref, between)
+    ple.swap_end()
+    for store in stores[10:]:
+        store.start()
     gate.spread_end()
     stores[7].start()
     up.spread_end()
@@ -1863,6 +1885,7 @@
         gains_copy(hop, me).wait_send()
     for spread in spreads + [small]:
         spread.spread_sent()
+    ple.swap_sent()
 
     @pl.when(ctx_at < planes - 1)
     def _():
@@ -1877,7 +1900,18 @@
 
 
 def attention_forward(
-    tokens, packed, frequency, lengths, query_weight, key_weight, value_weight, gate, up, out, small
+    tokens,
+    packed,
+    frequency,
+    lengths,
+    query_weight,
+    key_weight,
+    value_weight,
+    gate,
+    up,
+    out,
+    small,
+    ple,
 ):
     tok_count, width = tokens.shape
     rows = query_weight.shape[0]
@@ -1906,12 +1940,14 @@
         ((chips, 2, tok_count, width), bfloat),
         ((members, rows, 3 * HD), bfloat),
         ((members, rows, 2 * ff_part), bfloat),
-    ] + kept + [((members,) + small.shape, bfloat)]
+    ] + kept
+    outputs.append(((members,) + small.shape, bfloat))
+    outputs.append(((2, members, ple.shape[0] // 8, ple.shape[1]), bfloat))
     return pl.pallas_call(
         functools.partial(attention_forward_kernel, chips),
         out_shape=[jax.ShapeDtypeStruct(*output) for output in outputs],
-        in_specs=[vmem] * 3 + [pl.BlockSpec(memory_space=pltpu.SMEM)] + [anywhere] * 7,
-        out_specs=[vmem] * 5 + [anywhere] * 9,
+        in_specs=[vmem] * 3 + [pl.BlockSpec(memory_space=pltpu.SMEM)] + [anywhere] * 8,
+        out_specs=[vmem] * 5 + [anywhere] * 10,
         scratch_shapes=line_scratch(chips, tok_count, width)
         + [
             pltpu.VMEM((2, members, rows // 8, 3 * HD), bfloat),
@@ -1930,9 +1966,10 @@
         + spread_scratch((members, rows, ff_part))
         + spread_scratch((members, rows, ff_part))
         + everywhere_scratch((members,) + small.shape)
+        + everywhere_scratch((members,) + ple.shape)
         + [pltpu.VMEM(out.shape, bfloat)]
         + [pltpu.VMEM(*one) for one in kept]
-        + [dma, dma((10,)), dma((2,)), dma((2,))],
+        + [dma, dma((12,)), dma((2,)), dma((2,))],
         compiler_params=pltpu.CompilerParams(
             collective_id=4, has_side_effects=True, vmem_limit_bytes=KERNEL_VMEM
         ),
@@ -1952,6 +1989,7 @@
         up,
         out,
         small,
+        ple,
     )
 
 def rope_norm_back(grad, lin, gain, cosine, sine_part):
@@ -2286,19 +2324,22 @@
     fsdp_at = lax.axis_index("fsdp")
 
     wide_gains = (attn_in_gain, attn_out_gain, laurel_gain, ffn_in_gain, ffn_out_gain, ple_gain)
-    head_starts = fsdp_at * query_gain.shape[0]
+    turn = jnp.arange(HD, dtype=jnp.int32) // query_gain.shape[0]
     head_parts = [
-        lax.dynamic_update_slice_in_dim(jnp.zeros((HD,), jnp.float32), gain, head_starts, 0)
+        jnp.where(turn == fsdp_at, jnp.tile(gain, fsdp_count), 0.0)
         for gain in (query_gain, key_gain)
     ]
-    packed = jnp.concatenate(list(wide_gains) + [positions.astype(jnp.float32)] + head_parts)
-    packed = jnp.pad(packed, (0, GAIN_ROWS * 128 - packed.shape[0])).reshape(GAIN_ROWS, 128)
+    packed = jnp.zeros((GAIN_ROWS * 128,), jnp.float32)
+    at = 0
+    for part in list(wide_gains) + [positions.astype(jnp.float32)] + head_parts:
+        packed = packed + jnp.pad(part, (at, packed.shape[0] - at - part.shape[0]))
+        at += part.shape[0]
+    packed = packed.reshape(GAIN_ROWS, 128)
     frequency = jnp.exp(
         jnp.arange(HD // 2, dtype=jnp.float32) * (-2.0 * math.log(ROPE_BASE) / HD)
     )
 
     out_low = w_out.astype(bfloat)
-    down_low = w_down.astype(bfloat)
     def in_halves(weight):
         return jnp.concatenate(jnp.split(weight.astype(bfloat), rows // 128, axis=0), axis=1)
 
@@ -2306,10 +2347,8 @@
         pieces = weight.astype(bfloat).reshape(weight.shape[0], 128 // weight.shape[0], -1)
         return jnp.transpose(pieces, (1, 0, 2)).reshape(128, -1)
 
-    small = jnp.concatenate(
-        [in_halves(ple_gate), in_stacks(ple_proj), in_halves(laurel_left), in_stacks(laurel_right)],
-        axis=1,
-    )
+    small = jnp.concatenate([in_halves(laurel_left), in_stacks(laurel_right)], axis=1)
+    ple_small = jnp.concatenate([in_halves(ple_gate), in_stacks(ple_proj)], axis=1)
 
     inputs = tokens.astype(jnp.float32)
     ple_input = per_layer.astype(jnp.float32)
@@ -2328,6 +2367,7 @@
         probs,
         attended_low,
         small_all,
+        ple_held,
     ) = attention_forward(
         tokens,
         packed,
@@ -2340,12 +2380,8 @@
         w_up,
         out_low,
         small,
-    )
-    small_ends = [0]
-    for weight in (ple_gate, ple_proj, laurel_left, laurel_right):
-        small_ends.append(small_ends[-1] + weight.size // 128)
-    small_cols = [small_all[:, :, small_ends[n] : small_ends[n + 1]] for n in range(4)]
-
+        ple_small,
+    )
     def side_by_side(cols, shape):
         pieces = jnp.split(cols, cols.shape[2] // shape[1], axis=2)
         return jnp.concatenate(pieces, axis=1).reshape(-1, shape[1])
@@ -2354,10 +2390,9 @@
         pieces = cols.reshape(fsdp_count, -1, shape[0], cols.shape[2])
         return jnp.transpose(pieces, (0, 2, 1, 3)).reshape(-1, shape[1])
 
-    full_pgate = side_by_side(small_cols[0], ple_gate.shape)
-    full_pproj = stacked(small_cols[1], ple_proj.shape)
-    full_left = side_by_side(small_cols[2], laurel_left.shape)
-    full_right = stacked(small_cols[3], laurel_right.shape)
+    left_size = laurel_left.size // 128
+    full_left = side_by_side(small_all[:, :, :left_size], laurel_left.shape)
+    full_right = stacked(small_all[:, :, left_size:], laurel_right.shape)
     wide_rows = attn_in_gain.shape[0] // 128
     gain_in, gain_post, gain_laurel, gain_ffin, gain_ffout, gain_ple = (
         packed_all[:, n * wide_rows : (n + 1) * wide_rows].reshape(-1) for n in range(6)
@@ -2371,9 +2406,12 @@
     widened = matmul(narrow_low, full_right)
     mixed, mix_back = jax.vjp(mix_piece, inputs, normed, projected, widened, gain_post, gain_laurel)
     ffn_normed, ffn_norm_back = jax.vjp(rms_norm, mixed, gain_ffin)
-    down_lin, ffn_all, hidden_low, act_low, slope_low = ffn_forward(
-        ffn_normed.astype(bfloat), col_gateup, down_low, chips
-    )
+    down_lin, ffn_all, hidden_low, act_low, slope_low, ple_all, down_low = ffn_forward(
+        ffn_normed.astype(bfloat), col_gateup, w_down, ple_held, chips
+    )
+    pgate_size = ple_gate.size // 128
+    full_pgate = side_by_side(ple_all[:, :, :pgate_size], ple_gate.shape)
+    full_pproj = stacked(ple_all[:, :, pgate_size:], ple_proj.shape)
     layer_mid, ffn_out_back = jax.vjp(ffn_out_piece, mixed, down_lin, gain_ffout)
     layer_low = layer_mid.astype(bfloat)
     ple_lin = matmul(layer_low, full_pgate)

time: 736 us -> 710 us (0.965)
  Pallas kernels: 631 us -> 618 us
    pallas_call x1, Pallas kernels: 198 us -> 181 us  [attention_forward(): pl.pallas_call(functools.partial(attention_forward_kernel, chips), out_sh...]
where the time goes in v7:
time: 710 us; the launch traced here: 701 us
  Pallas kernels  618 us (87%)
  other arithmetic  54.7 us (8%)
  local copies, waits for them, and re-layouts  17.4 us (2%)
  matrix products  9.94 us (1%)
    pallas_call x1, Pallas kernels, attention_forward(): pl.pallas_call(functools.partial(attention_forward_kernel, chips), out_sh...  181 us
    pallas_call x1, Pallas kernels, gradient_sum(): pl.pallas_call(functools.partial(gradient_sum_kernel, sources), out_shape...  146 us
    pallas_call x1, Pallas kernels, attention_backward(): pl.pallas_call(functools.partial(attention_backward_kernel, chips), out_s...  121 us
    pallas_call x1, Pallas kernels, ffn_backward(): pl.pallas_call(functools.partial(ffn_backward_kernel, chips), out_shape=[...  93.3 us
    pallas_call x1, Pallas kernels, ffn_forward(): pl.pallas_call(functools.partial(ffn_forward_kernel, chips), out_shape=[j...  76.6 us

profile of v7, /device:TPU:0, one launch (start us, length us, event | category | flops | bytes accessed | tf_op | source)
XLA Modules:
  0.0 701.2 jit_solution(8162963897720988882)
XLA Ops:
  0.7 1.4 fusion.17
  4.7 1.4 add_bitcast_fusion.packed_ref
  11.3 1.1 convert_element_type.128.out_hbm
  12.5 180.9 %attention_forward.1 = (f32[128,2048]{1,0:T(8,128)}, f32[8,24,128]{2,1,0:T(8,128)}, f32[1024,128]{1,0:T(8,128)}, f32[1024,128]{1,0:T(8,128)}, f32[2,256]{1,0:T(2...) custom-call(bf16[128,2048]{1,0:T(8,128)(2,1)} %tokens_ref.1, ...), custom_call_target="tpu_custom_call" | custom-call | flops 8589934592 | bytes 314572800 | tf_op jit(solution)/shard_map/attention_forward/pallas_call | solution.py:1946
  194.4 1.4 multiply_reduce_fusion.12
  195.8 1.3 fusion.56
  197.2 1.3 fusion.51
  201.3 76.6 %ffn_forward.1 = (f32[128,2048]{1,0:T(8,128)}, bf16[4,2,128,2048]{3,2,1,0:T(8,128)(2,1)}, bf16[1024,1024]{1,0:T(8,128)(2,1)}, bf16[1024,1024]{1,0:T(8,128)(2,1)}...) custom-call(bf16[128,2048]{1,0:T(8,128)(2,1)} %multiply_convert_fusion.own_ref, ...), custom_call_target="tpu_custom_call" | custom-call | flops 12884901888 | bytes 41943040 | tf_op jit(solution)/shard_map/ffn_forward/pallas_call | solution.py:1290
  277.9 1.5 multiply_reduce_fusion.9
  279.5 1.4 multiply_add_fusion
  284.7 2.7 fusion.11
  287.4 1.2 fusion.37
  288.8 1.4 convolution_convert_fusion.1
  290.2 1.6 multiply_reduce_fusion
  291.8 2.3 fusion.12.own_ref
  294.6 1.5 reshape.321.pproj_hbm
  296.1 93.3 %ffn_backward.1 = (f32[128,2048]{1,0:T(8,128)}, bf16[8,256,2048]{2,1,0:T(8,128)(2,1)}, bf16[2,128,2048]{2,1,0:T(8,128)(2,1)}, bf16[2,8,32,256]{3,2,1,0:T(8,128)(2,1)}, bf16[2,8,16,512]{3,2,1,0:T(8,128)(2,1)}) custom-call(bf16[128,2048]{1,0:T(8,128)(2,1)} %fusion.12.own_ref, bf16[2048,2048]{1,0:T(8,128)(2,1)} %bitcast.109, ...), custom_call_target="tpu_custom_call" | custom-call | flops 25769803776 | bytes 41943040 | tf_op jit(solution)/shard_map/ffn_backward/pallas_call | solution.py:1494
  389.4 1.6 multiply_reduce_fusion.1
  391.1 3.7 multiply_reduce_fusion.2
  394.8 2.8 fusion.14
  398.4 120.6 %attention_backward.1 = (f32[128,2048]{1,0:T(8,128)}, bf16[8,256,256]{2,1,0:T(8,128)(2,1)}, bf16[8,256,512]{2,1,0:T(8,128)(2,1)}, bf16[256,2048]{1,0:T(8,128)(2,...) custom-call(bf16[128,2048]{1,0:T(8,128)(2,1)} %get-tuple-element.178.own_ref, ...), custom_call_target="tpu_custom_call" | custom-call | flops 8589934592 | bytes 314572800 | tf_op jit(solution)/shard_map/attention_backward/pallas_call | solution.py:2238
  519.0 2.9 fusion.8
  521.9 2.6 fusion.16
  527.8 146.1 %gradient_sum.1 = (bf16[256,8192]{1,0:T(8,128)(2,1)}, bf16[256,8192]{1,0:T(8,128)(2,1)}, bf16[256,2048]{1,0:T(8,128)(2,1)}, bf16[256,512]{1,0:T(8,128)(2,1)}, bf...) custom-call(bf16[2,8,32,2048]{3,2,1,0:T(8,128)(2,1)} %get-tuple-elem, ...), custom_call_target="tpu_custom_call" | custom-call | bytes 314572800 | tf_op jit(solution)/shard_map/gradient_sum/pallas_call | solution.py:903
  678.1 1.6 convert_element_type.158
  679.8 1.7 reshape.345
  681.4 1.8 convert_element_type.152
  684.1 1.6 convert_element_type.151
  685.7 1.6 convert_element_type.154
  687.6 4.4 convert_element_type.155
  692.0 4.4 convert_element_type.156
  696.4 4.4 convert_element_type.157
  (137 shorter events, 25.6 us)
Async XLA Ops:
  0.7 10.7 %copy-start.22 = (f32[256,2048]{1,0:T(8,128)S(1)}, f32[256,2048]{1,0:T(8,128)}, u32[]{:S(2)}) copy-start(f32[256,2048]{1,0:T(8,128)} %param.32) | copy-start | bytes 6291460
  193.4 5.1 copy-start.10
  194.4 4.6 copy-start.20
  197.2 2.2 copy-start.1
  198.5 0.8 copy-start.26
  199.4 1.0 copy-start.3
  277.9 3.0 copy-start.23
  280.9 3.8 copy-start.4
  281.2 1.1 copy-start.7
  282.1 0.8 copy-start.29
  282.4 1.0 copy-start.18
  282.4 1.9 copy-start.11
  283.3 1.0 copy-start.9
  284.7 2.7 copy-start.19
  287.4 2.9 copy-start.24
  287.4 1.4 copy-start.5
  287.4 2.9 copy-start
  287.4 2.8 copy-start.8
  287.4 2.8 copy-start.12
  291.8 2.3 copy-start.25
  389.4 1.6 copy-start.2
  394.8 2.9 copy-start.21
  397.6 0.8 copy-start.13
  398.4 120.6 %copy-start.6 = (f32[128,2048]{1,0:T(8,128)S(1)}, f32[128,2048]{1,0:T(8,128)}, u32[]{:S(2)}) copy-start(f32[128,2048]{1,0:T(8,128)} %get-tuple-element.170) | copy-start | bytes 3145732
  521.9 2.7 copy-start.31
  521.9 4.1 copy-start.14
  673.8 9.4 %copy-start.30 = (bf16[256,512]{1,0:T(8,128)(2,1)S(1)}, bf16[256,512]{1,0:T(8,128)(2,1)}, u32[]{:S(2)}) copy-start(bf16[256,512]{1,0:T(8,128)(2,1)} %get-tuple-element.101) | copy-start | bytes 786436
  673.9 10.3 %copy-start.28 = (bf16[256,2048]{1,0:T(8,128)(2,1)S(1)}, bf16[256,2048]{1,0:T(8,128)(2,1)}, u32[]{:S(2)}) copy-start(bf16[256,2048]{1,0:T(8,128)(2,1)} %get-tuple-element.99) | copy-start | bytes 3145732
  683.3 2.4 copy-start.27
  684.1 3.5 copy-start.17
  687.6 4.4 copy-start.16
  692.0 4.4 copy-start.15

commit v8 on v7

--- a/solution.py
+++ b/solution.py
@@ -659,6 +659,70 @@
                 self.final[group, rows] = total.astype(jnp.bfloat16)
 
 
+class PairSpread(Spread):
+    def __init__(self, source, refs):
+        self.landing = refs[0]
+        super().__init__(source, refs[1:], True)
+        self.chips = self.members // 2
+        self.chip, self.core = self.me // 2, self.me % 2
+
+    def to_member(self, half, at):
+        return remote(
+            self.held(half, at),
+            self.landing.at[half, self.chip],
+            self.swap_send.at[at, half],
+            self.swap_recv.at[self.chip, half],
+            self.core * self.chips + at,
+        )
+
+    def from_chip(self, half, chip):
+        place = self.landing.at[half, chip]
+        return remote(
+            place,
+            place,
+            self.swap_send.at[chip, half],
+            self.swap_recv.at[chip, half],
+            lax.rem(self.me + 1, self.members),
+        )
+
+    def swap_local(self, half):
+        return pltpu.make_async_copy(
+            self.held(half, self.me - self.core * self.chips),
+            self.landing.at[half, self.chip],
+            self.place_sem.at[half],
+        )
+
+    def swap_begin(self):
+        for half in (0, 1):
+            for at in range(self.chips):
+                mine = self.core * self.chips + at == self.me
+                pl.when(mine)(self.swap_local(half).start)
+                pl.when(jnp.logical_not(mine))(self.to_member(half, at).start)
+
+    def swap_end(self):
+        groups = self.final.shape[0]
+        size = self.chips // groups
+        for half in (0, 1):
+            for chip in range(self.chips):
+                mine = 2 * chip + self.me // self.chips == self.me
+                pl.when(mine)(self.swap_local(half).wait)
+                pl.when(jnp.logical_not(mine))(self.from_chip(half, chip).wait_recv)
+            rows = pl.ds(pl.multiple_of(self.own_start(half), self.eighth), self.eighth)
+            for group in range(groups):
+                total = self.landing[half, group * size].astype(jnp.float32)
+                for chip in range(group * size + 1, (group + 1) * size):
+                    total = total + self.landing[half, chip].astype(jnp.float32)
+                self.final[group, rows] = total.astype(jnp.bfloat16)
+
+    def spread_sent(self):
+        for half in (0, 1):
+            self.spread_copy(half, 0).wait_send()
+            self.spread_copy(half, 1).wait_send()
+            for at in range(self.chips):
+                mine = self.core * self.chips + at == self.me
+                pl.when(jnp.logical_not(mine))(self.to_member(half, at).wait_send)
+
+
 class Everywhere(Spread):
     def swap_begin(self):
         chips = self.members // 2
@@ -791,7 +855,8 @@
             sums.append(held)
         size = spread_refs(one.columns)
         if one.groups:
-            spreads.append(GroupSpread(held, take(size + 1)))
+            kind = PairSpread if one.paired else GroupSpread
+            spreads.append(kind(held, take(size + 1)))
         else:
             spreads.append(Spread(held, take(size), one.columns))
         if not one.summed:
@@ -869,6 +934,7 @@
     summed: bool = False
     part: tuple = (0, 1)
     groups: int = 0
+    paired: bool = False
     sides: int = 0
 
     @property
@@ -892,7 +958,7 @@
         if not one.summed:
             scratch += sum_scratch(shape)
         if one.groups:
-            landing = (2, members, shape[1] // 8, shape[2])
+            landing = (2, shape[0] if one.paired else members, shape[1] // 8, shape[2])
             scratch.append(pltpu.VMEM(landing, jnp.bfloat16))
             shape = (one.groups,) + shape[1:]
         scratch += spread_scratch(shape, members)
@@ -2039,7 +2105,7 @@
     del scratch[: spread_refs(False)]
     out, qkv, lin, query, span, probs, grad, grad_span, back, across, returned = scratch[:11]
     load_sem, store_sem, back_send, back_recv, grad_out = scratch[11:16]
-    inputs, attended, query_part, kv_part, out_part = scratch[16:]
+    inputs, attended, query_part, kv_part, out_part, pair_send, pair_recv = scratch[16:]
     width = line.slots.shape[3]
     pair = 2 * line.tok
     block = chips * pair
@@ -2154,8 +2220,19 @@
     part_stores = [
         pltpu.make_async_copy(out_part, out_part_hbm, store_sem.at[0]),
         pltpu.make_async_copy(query_part, query_part_hbm, store_sem.at[1]),
-        pltpu.make_async_copy(kv_part, kv_part_hbm, store_sem.at[5]),
+        pltpu.make_async_copy(
+            kv_part.at[pl.ds(line.core * chips, chips)], kv_part_hbm, store_sem.at[5]
+        ),
     ]
+
+    def pair_copy(at):
+        return remote(
+            kv_part.at[(1 - line.core) * chips + at],
+            probs.at[pl.ds(at * HD, HD), pl.ds(0, 2 * HD)],
+            pair_send.at[at],
+            pair_recv.at[at],
+            line.place(line.chip, 1 - line.core),
+        )
 
     def between(rank):
         if rank == 3:
@@ -2172,6 +2249,12 @@
                 kv_part[at] = dot_tn(left, grad[:, HD:]).astype(bfloat)
 
             part_stores[1].start()
+            for at in range(chips):
+                pair_copy(at).start()
+        if rank == 5:
+            for at in range(chips):
+                pair_copy(at).wait_recv()
+                kv_part[line.core * chips + at] += probs[at * HD : (at + 1) * HD, : 2 * HD]
             part_stores[2].start()
 
     gateup.middle()
@@ -2189,6 +2272,8 @@
     line.gather_end()
     gateup.sum_sent()
     down.spread_sent()
+    for at in range(chips):
+        pair_copy(at).wait_send()
 
     @pl.when(ctx_at > 0)
     def _():
@@ -2228,7 +2313,7 @@
     outputs = [
         ((tok_count, width), jnp.float32),
         ((members, HD, HD), bfloat),
-        ((members, HD, 2 * HD), bfloat),
+        ((chips, HD, 2 * HD), bfloat),
         ((HD, width), bfloat),
         ((2, HD), jnp.float32),
         ((2, members, eighth, part_gateup.shape[2]), bfloat),
@@ -2260,6 +2345,8 @@
             pltpu.VMEM((members, HD, HD), bfloat),
             pltpu.VMEM((members, HD, 2 * HD), bfloat),
             pltpu.VMEM((HD, width), bfloat),
+            dma((chips,)),
+            dma((chips,)),
         ],
         compiler_params=pltpu.CompilerParams(
             collective_id=5, has_side_effects=True, vmem_limit_bytes=KERNEL_VMEM
@@ -2519,7 +2606,7 @@
             Source(held_gateup, summed=True, part=(0, 2), sides=1),
             Source(held_gateup, summed=True, part=(1, 2), sides=1),
             Source(part_query, sides=1),
-            Source(part_kv, groups=KV, sides=2),
+            Source(part_kv, groups=KV, paired=True, sides=2),
             Source(part_wout),
             Source(held_pgate, summed=True, groups=1, sides=1),
             Source(held_pproj, summed=True, groups=1, sides=1),

time: 710 us -> 703 us (level)
  Pallas kernels: 618 us -> 609 us
    pallas_call x1, Pallas kernels: 146 us -> 138 us  [gradient_sum(): pl.pallas_call(functools.partial(gradient_sum_kernel, sources), out_shape...]
where the time goes in v8:
time: 703 us; the launch traced here: 693 us
  Pallas kernels  609 us (87%)
  other arithmetic  54.7 us (8%)
  local copies, waits for them, and re-layouts  17.4 us (2%)
  matrix products  9.94 us (1%)
    pallas_call x1, Pallas kernels, attention_forward(): pl.pallas_call(functools.partial(attention_forward_kernel, chips), out_sh...  181 us
    pallas_call x1, Pallas kernels, gradient_sum(): pl.pallas_call(functools.partial(gradient_sum_kernel, sources), out_shape...  138 us
    pallas_call x1, Pallas kernels, attention_backward(): pl.pallas_call(functools.partial(attention_backward_kernel, chips), out_s...  121 us
    pallas_call x1, Pallas kernels, ffn_backward(): pl.pallas_call(functools.partial(ffn_backward_kernel, chips), out_shape=[...  93.3 us
    pallas_call x1, Pallas kernels, ffn_forward(): pl.pallas_call(functools.partial(ffn_forward_kernel, chips), out_shape=[j...  76.6 us

profile of v8, /device:TPU:0, one launch (start us, length us, event | category | flops | bytes accessed | tf_op | source)
XLA Modules:
  0.0 692.9 jit_solution(13832803575577524279)
XLA Ops:
  0.7 1.4 fusion.17
  4.7 1.4 add_bitcast_fusion.packed_ref
  11.3 1.1 convert_element_type.128.out_hbm
  12.5 180.9 %attention_forward.1 = (f32[128,2048]{1,0:T(8,128)}, f32[8,24,128]{2,1,0:T(8,128)}, f32[1024,128]{1,0:T(8,128)}, f32[1024,128]{1,0:T(8,128)}, f32[2,256]{1,0:T(2...) custom-call(bf16[128,2048]{1,0:T(8,128)(2,1)} %tokens_ref.1, ...), custom_call_target="tpu_custom_call" | custom-call | flops 8589934592 | bytes 314572800 | tf_op jit(solution)/shard_map/attention_forward/pallas_call | solution.py:2012
  194.4 1.4 multiply_reduce_fusion.12
  195.8 1.3 fusion.56
  197.2 1.3 fusion.51
  201.3 76.6 %ffn_forward.1 = (f32[128,2048]{1,0:T(8,128)}, bf16[4,2,128,2048]{3,2,1,0:T(8,128)(2,1)}, bf16[1024,1024]{1,0:T(8,128)(2,1)}, bf16[1024,1024]{1,0:T(8,128)(2,1)}...) custom-call(bf16[128,2048]{1,0:T(8,128)(2,1)} %multiply_convert_fusion.own_ref, ...), custom_call_target="tpu_custom_call" | custom-call | flops 12884901888 | bytes 41943040 | tf_op jit(solution)/shard_map/ffn_forward/pallas_call | solution.py:1356
  277.9 1.5 multiply_reduce_fusion.9
  279.5 1.4 multiply_add_fusion
  284.7 2.7 fusion.11
  287.4 1.2 fusion.37
  288.8 1.4 convolution_convert_fusion.1
  290.2 1.6 multiply_reduce_fusion
  291.8 2.3 fusion.12.own_ref
  294.6 1.5 reshape.321.pproj_hbm
  296.1 93.3 %ffn_backward.1 = (f32[128,2048]{1,0:T(8,128)}, bf16[8,256,2048]{2,1,0:T(8,128)(2,1)}, bf16[2,128,2048]{2,1,0:T(8,128)(2,1)}, bf16[2,8,32,256]{3,2,1,0:T(8,128)(2,1)}, bf16[2,8,16,512]{3,2,1,0:T(8,128)(2,1)}) custom-call(bf16[128,2048]{1,0:T(8,128)(2,1)} %fusion.12.own_ref, bf16[2048,2048]{1,0:T(8,128)(2,1)} %bitcast.109, ...), custom_call_target="tpu_custom_call" | custom-call | flops 25769803776 | bytes 41943040 | tf_op jit(solution)/shard_map/ffn_backward/pallas_call | solution.py:1560
  389.4 1.6 multiply_reduce_fusion.1
  391.1 3.7 multiply_reduce_fusion.2
  394.8 2.8 fusion.14
  398.4 120.6 %attention_backward.1 = (f32[128,2048]{1,0:T(8,128)}, bf16[8,256,256]{2,1,0:T(8,128)(2,1)}, bf16[4,256,512]{2,1,0:T(8,128)(2,1)}, bf16[256,2048]{1,0:T(8,128)(2,...) custom-call(bf16[128,2048]{1,0:T(8,128)(2,1)} %get-tuple-element.178.own_ref, ...), custom_call_target="tpu_custom_call" | custom-call | flops 8589934592 | bytes 314572800 | tf_op jit(solution)/shard_map/attention_backward/pallas_call | solution.py:2323
  519.1 2.9 fusion.8
  522.0 2.6 fusion.16
  527.8 137.6 %gradient_sum.1 = (bf16[256,8192]{1,0:T(8,128)(2,1)}, bf16[256,8192]{1,0:T(8,128)(2,1)}, bf16[256,2048]{1,0:T(8,128)(2,1)}, bf16[256,512]{1,0:T(8,128)(2,1)}, bf...) custom-call(bf16[2,8,32,2048]{3,2,1,0:T(8,128)(2,1)} %get-tuple-elem, ...), custom_call_target="tpu_custom_call" | custom-call | bytes 314572800 | tf_op jit(solution)/shard_map/gradient_sum/pallas_call | solution.py:969
  669.8 1.6 convert_element_type.158
  671.4 1.7 reshape.345
  673.1 1.8 convert_element_type.152
  675.8 1.6 convert_element_type.151
  677.3 1.6 convert_element_type.154
  679.2 4.4 convert_element_type.155
  683.6 4.4 convert_element_type.156
  688.0 4.4 convert_element_type.157
  (137 shorter events, 25.6 us)
Async XLA Ops:
  0.7 10.7 %copy-start.22 = (f32[256,2048]{1,0:T(8,128)S(1)}, f32[256,2048]{1,0:T(8,128)}, u32[]{:S(2)}) copy-start(f32[256,2048]{1,0:T(8,128)} %param.32) | copy-start | bytes 6291460
  193.4 5.1 copy-start.10
  194.4 4.6 copy-start.20
  197.2 2.2 copy-start.1
  198.5 0.8 copy-start.26
  199.4 1.0 copy-start.3
  277.9 3.0 copy-start.23
  280.9 3.8 copy-start.4
  281.2 1.1 copy-start.7
  282.1 0.8 copy-start.29
  282.4 1.0 copy-start.18
  282.4 1.9 copy-start.11
  283.3 1.0 copy-start.9
  284.7 2.7 copy-start.19
  287.4 2.9 copy-start.24
  287.4 1.4 copy-start.5
  287.4 2.9 copy-start
  287.4 2.8 copy-start.8
  287.4 2.8 copy-start.12
  291.8 2.3 copy-start.25
  389.4 1.6 copy-start.2
  394.8 2.9 copy-start.21
  397.6 0.8 copy-start.13
  398.4 120.7 %copy-start.6 = (f32[128,2048]{1,0:T(8,128)S(1)}, f32[128,2048]{1,0:T(8,128)}, u32[]{:S(2)}) copy-start(f32[128,2048]{1,0:T(8,128)} %get-tuple-element.170) | copy-start | bytes 3145732
  522.0 2.7 copy-start.31
  522.0 4.1 copy-start.14
  665.5 9.4 %copy-start.30 = (bf16[256,512]{1,0:T(8,128)(2,1)S(1)}, bf16[256,512]{1,0:T(8,128)(2,1)}, u32[]{:S(2)}) copy-start(bf16[256,512]{1,0:T(8,128)(2,1)} %get-tuple-element.101) | copy-start | bytes 786436
  665.5 10.3 %copy-start.28 = (bf16[256,2048]{1,0:T(8,128)(2,1)S(1)}, bf16[256,2048]{1,0:T(8,128)(2,1)}, u32[]{:S(2)}) copy-start(bf16[256,2048]{1,0:T(8,128)(2,1)} %get-tuple-element.99) | copy-start | bytes 3145732
  674.9 2.4 copy-start.27
  675.8 3.5 copy-start.17
  679.2 4.4 copy-start.16
  683.6 4.4 copy-start.15

commit v9 on v8

--- a/solution.py
+++ b/solution.py
@@ -1933,7 +1933,7 @@
             up.spread_begin()
             small.spread_on()
             ple.swap_on()
-        if rank == 2 * chips - 3:
+        if rank == 2 * chips - 4:
             up.spread_on()
 
     line.scatter_rest(result_ref, between)

time: 703 us -> 703 us (level)
  no operation moved by 1% of the time
where the time goes in v9:
time: 703 us; the launch traced here: 693 us
  Pallas kernels  609 us (87%)
  other arithmetic  54.7 us (8%)
  local copies, waits for them, and re-layouts  17.4 us (2%)
  matrix products  9.94 us (1%)
    pallas_call x1, Pallas kernels, attention_forward(): pl.pallas_call(functools.partial(attention_forward_kernel, chips), out_sh...  181 us
    pallas_call x1, Pallas kernels, gradient_sum(): pl.pallas_call(functools.partial(gradient_sum_kernel, sources), out_shape...  138 us
    pallas_call x1, Pallas kernels, attention_backward(): pl.pallas_call(functools.partial(attention_backward_kernel, chips), out_s...  121 us
    pallas_call x1, Pallas kernels, ffn_backward(): pl.pallas_call(functools.partial(ffn_backward_kernel, chips), out_shape=[...  93.3 us
    pallas_call x1, Pallas kernels, ffn_forward(): pl.pallas_call(functools.partial(ffn_forward_kernel, chips), out_shape=[j...  76.6 us

profile of v9, /device:TPU:0, one launch (start us, length us, event | category | flops | bytes accessed | tf_op | source)
XLA Modules:
  0.0 692.9 jit_solution(1402035205629303609)
XLA Ops:
  0.7 1.4 fusion.17
  4.7 1.4 add_bitcast_fusion.packed_ref
  11.3 1.1 convert_element_type.128.out_hbm
  12.5 180.9 %attention_forward.1 = (f32[128,2048]{1,0:T(8,128)}, f32[8,24,128]{2,1,0:T(8,128)}, f32[1024,128]{1,0:T(8,128)}, f32[1024,128]{1,0:T(8,128)}, f32[2,256]{1,0:T(2...) custom-call(bf16[128,2048]{1,0:T(8,128)(2,1)} %tokens_ref.1, ...), custom_call_target="tpu_custom_call" | custom-call | flops 8589934592 | bytes 314572800 | tf_op jit(solution)/shard_map/attention_forward/pallas_call | solution.py:2012
  194.4 1.4 multiply_reduce_fusion.12
  195.8 1.3 fusion.56
  197.2 1.3 fusion.51
  201.3 76.6 %ffn_forward.1 = (f32[128,2048]{1,0:T(8,128)}, bf16[4,2,128,2048]{3,2,1,0:T(8,128)(2,1)}, bf16[1024,1024]{1,0:T(8,128)(2,1)}, bf16[1024,1024]{1,0:T(8,128)(2,1)}...) custom-call(bf16[128,2048]{1,0:T(8,128)(2,1)} %multiply_convert_fusion.own_ref, ...), custom_call_target="tpu_custom_call" | custom-call | flops 12884901888 | bytes 41943040 | tf_op jit(solution)/shard_map/ffn_forward/pallas_call | solution.py:1356
  277.9 1.5 multiply_reduce_fusion.9
  279.5 1.4 multiply_add_fusion
  284.7 2.7 fusion.11
  287.4 1.2 fusion.37
  288.8 1.4 convolution_convert_fusion.1
  290.2 1.6 multiply_reduce_fusion
  291.8 2.3 fusion.12.own_ref
  294.6 1.5 reshape.321.pproj_hbm
  296.1 93.3 %ffn_backward.1 = (f32[128,2048]{1,0:T(8,128)}, bf16[8,256,2048]{2,1,0:T(8,128)(2,1)}, bf16[2,128,2048]{2,1,0:T(8,128)(2,1)}, bf16[2,8,32,256]{3,2,1,0:T(8,128)(2,1)}, bf16[2,8,16,512]{3,2,1,0:T(8,128)(2,1)}) custom-call(bf16[128,2048]{1,0:T(8,128)(2,1)} %fusion.12.own_ref, bf16[2048,2048]{1,0:T(8,128)(2,1)} %bitcast.109, ...), custom_call_target="tpu_custom_call" | custom-call | flops 25769803776 | bytes 41943040 | tf_op jit(solution)/shard_map/ffn_backward/pallas_call | solution.py:1560
  389.4 1.6 multiply_reduce_fusion.1
  391.1 3.7 multiply_reduce_fusion.2
  394.8 2.8 fusion.14
  398.4 120.6 %attention_backward.1 = (f32[128,2048]{1,0:T(8,128)}, bf16[8,256,256]{2,1,0:T(8,128)(2,1)}, bf16[4,256,512]{2,1,0:T(8,128)(2,1)}, bf16[256,2048]{1,0:T(8,128)(2,...) custom-call(bf16[128,2048]{1,0:T(8,128)(2,1)} %get-tuple-element.178.own_ref, ...), custom_call_target="tpu_custom_call" | custom-call | flops 8589934592 | bytes 314572800 | tf_op jit(solution)/shard_map/attention_backward/pallas_call | solution.py:2323
  519.1 2.9 fusion.8
  522.0 2.6 fusion.16
  527.8 137.6 %gradient_sum.1 = (bf16[256,8192]{1,0:T(8,128)(2,1)}, bf16[256,8192]{1,0:T(8,128)(2,1)}, bf16[256,2048]{1,0:T(8,128)(2,1)}, bf16[256,512]{1,0:T(8,128)(2,1)}, bf...) custom-call(bf16[2,8,32,2048]{3,2,1,0:T(8,128)(2,1)} %get-tuple-elem, ...), custom_call_target="tpu_custom_call" | custom-call | bytes 314572800 | tf_op jit(solution)/shard_map/gradient_sum/pallas_call | solution.py:969
  669.8 1.6 convert_element_type.158
  671.4 1.7 reshape.345
  673.1 1.8 convert_element_type.152
  675.8 1.6 convert_element_type.151
  677.3 1.6 convert_element_type.154
  679.2 4.4 convert_element_type.155
  683.6 4.4 convert_element_type.156
  688.0 4.4 convert_element_type.157
  (137 shorter events, 25.6 us)
Async XLA Ops:
  0.7 10.7 %copy-start.22 = (f32[256,2048]{1,0:T(8,128)S(1)}, f32[256,2048]{1,0:T(8,128)}, u32[]{:S(2)}) copy-start(f32[256,2048]{1,0:T(8,128)} %param.32) | copy-start | bytes 6291460
  193.4 5.1 copy-start.10
  194.4 4.6 copy-start.20
  197.2 2.2 copy-start.1
  198.5 0.8 copy-start.26
  199.4 1.0 copy-start.3
  277.9 3.0 copy-start.23
  280.9 3.8 copy-start.4
  281.2 1.1 copy-start.7
  282.1 0.8 copy-start.29
  282.4 1.0 copy-start.18
  282.4 1.9 copy-start.11
  283.3 1.0 copy-start.9
  284.7 2.7 copy-start.19
  287.4 2.9 copy-start.24
  287.4 1.4 copy-start.5
  287.4 2.9 copy-start
  287.4 2.8 copy-start.8
  287.4 2.8 copy-start.12
  291.8 2.3 copy-start.25
  389.4 1.6 copy-start.2
  394.8 2.9 copy-start.21
  397.6 0.8 copy-start.13
  398.4 120.7 %copy-start.6 = (f32[128,2048]{1,0:T(8,128)S(1)}, f32[128,2048]{1,0:T(8,128)}, u32[]{:S(2)}) copy-start(f32[128,2048]{1,0:T(8,128)} %get-tuple-element.170) | copy-start | bytes 3145732
  522.0 2.7 copy-start.31
  522.0 4.1 copy-start.14
  665.5 9.4 %copy-start.30 = (bf16[256,512]{1,0:T(8,128)(2,1)S(1)}, bf16[256,512]{1,0:T(8,128)(2,1)}, u32[]{:S(2)}) copy-start(bf16[256,512]{1,0:T(8,128)(2,1)} %get-tuple-element.101) | copy-start | bytes 786436
  665.5 10.3 %copy-start.28 = (bf16[256,2048]{1,0:T(8,128)(2,1)S(1)}, bf16[256,2048]{1,0:T(8,128)(2,1)}, u32[]{:S(2)}) copy-start(bf16[256,2048]{1,0:T(8,128)(2,1)} %get-tuple-element.99) | copy-start | bytes 3145732
  674.9 2.4 copy-start.27
  675.8 3.5 copy-start.17
  679.2 4.4 copy-start.16
  683.6 4.4 copy-start.15
